TPU v7x, 128 devices: a whole 4x4x4 slice. The times are simulated.
128 devices in a mesh: dp: 4 (over y_hi, core), cent: 32 (over z, x, y_lo).
Axes of the slice: x: 4, y: 4 (y_hi: 2, y_lo: 2; y = y_hi * 2 + y_lo), z: 4, core: 2. Of those that a mesh axis runs over, the one named last changes fastest.
Arguments:
- points: bfloat16 [8192, 1024], P(('dp', 'cent')), may hold values from -100 to 100
- centroids: bfloat16 [50176, 1024], P('cent'), may hold values from -8 to 8
Outputs:
- new_centroids: bfloat16 [50176, 1024], P('cent', 'dp')
- log_partition: float32 [8192], P(('dp', 'cent'))
All inputs are finite; a program needn't handle non-finite values.
Results may differ from a plain program's by a relative error of at most 0.0024.
Values may be sent and summed in bfloat16 or wider, within the bound.
No kernel may reach another device: no remote copies, remote signals or barrier semaphores. Data moves between devices by JAX's collectives and lax.ppermute only.
A program may use at most 128 MiB of HBM per device.

v0:
```python
import jax
import jax.numpy as jnp
from jax import lax
from jax.sharding import PartitionSpec as P

D = 1024
PTS_DEV = 64


def on_device(points, centroids):
    scale = 1.0 / D**0.5
    group = lax.all_gather(points, "cent", axis=0, tiled=True)
    cnorm = jnp.sum(jnp.square(centroids.astype(jnp.float32)), axis=1)
    cross = lax.dot_general(
        group, centroids, (((1,), (1,)), ((), ())), preferred_element_type=jnp.float32
    )
    logits = (2.0 * cross - cnorm[None, :]) * scale
    local_max = jnp.max(logits, axis=1)
    row_max = lax.pmax(local_max, "cent")
    total = lax.psum(jnp.sum(jnp.exp(logits - row_max[:, None]), axis=1), "cent")
    resp = (jnp.exp(logits - row_max[:, None]) / total[:, None]).astype(jnp.bfloat16)
    partition = row_max + jnp.log(total)
    own_rows = lax.dynamic_slice_in_dim(partition, lax.axis_index("cent") * PTS_DEV, PTS_DEV, 0)
    width = D // lax.axis_size("dp")
    partial_sums = lax.dot_general(
        resp, group, (((0,), (0,)), ((), ())), preferred_element_type=jnp.float32
    )
    sums = lax.psum_scatter(partial_sums, "dp", scatter_dimension=1, tiled=True)
    counts = lax.psum(jnp.sum(resp.astype(jnp.float32), axis=0), "dp")
    own_cols = lax.dynamic_slice_in_dim(centroids, lax.axis_index("dp") * width, width, 1).astype(
        jnp.float32
    )
    fresh = ((sums + 0.25 * own_cols) / (counts[:, None] + 0.25)).astype(jnp.bfloat16)
    return (fresh, own_rows)


def solution(mesh):
    placed = (P(("dp", "cent"), None), P("cent", None))
    return jax.shard_map(
        on_device,
        mesh=mesh,
        in_specs=placed,
        out_specs=(P("cent", "dp"), P(("dp", "cent"))),
        check_vma=False,
    )
```

profile of v0, /device:TPU:0, one launch (start us, length us, event | category | flops | bytes accessed | tf_op | source)
XLA Modules:
  0.0 443.8 jit_solution(1115978377201510537)
XLA Ops:
  7.2 0.0 all-gather.2.cloned.1.call-start
  7.2 0.7 all-gather.2.cloned.1.call-update
  7.9 0.0 reduce-scatter.2.cloned.1.call-start
  7.9 2.6 multiply_reduce_fusion
  10.6 159.7 %all-gather.2.cloned.1.call-done = bf16[2048,1024]{1,0:T(8,128)(2,1)} async-done(((bf16[64,1024]{1,0:T(8,128)(2,1)}), bf16[2048,1024]{1,0:T(8,128)(2,1)}) %all-gather.2.cloned.1.call-update) | async-done | bytes 4194320 | tf_op jit(solution)/shard_map/all_gather | solution.py:12
  170.3 12.5 %fusion.1 = (f32[2048]{0:T(1024)S(1)}, f32[2048,1568]{0,1:T(8,128)}) fusion(f32[1568]{0:T(1024)S(1)} %multiply_reduce_fusion, bf16[2048,1024]{1,0:T(8,128)(2,1)} %all-gather.2.cloned.1.call-done, bf16[1568,1024]{1,0:T(8,128)(2,1)} %param.3), kind=kOutput, calls=%fused_computation.10 | convolution fusion | flops 6589511680 | bytes 20265088 | tf_op jit(solution)/shard_map/dot_general | solution.py:14
  182.8 83.5 %pmax.7 = f32[2048]{0:T(1024)S(1)} all-reduce(f32[2048]{0:T(1024)S(1)} %get-tuple-element.4), channel_id=1, replica_groups=mesh['dp'=4,'cent'=32] {'cent'}, use_global_device_ids=true, to_apply=%region_2.0 | all-reduce | flops 2048 | bytes 16384 | tf_op jit(solution)/shard_map/pmax | solution.py:19
  266.3 6.4 %fusion = f32[2048]{0:T(1024)S(1)} fusion(f32[2048,1568]{0,1:T(8,128)} %get-tuple-element.5, f32[2048]{0:T(1024)S(1)} %pmax.7), kind=kLoop, calls=%fused_computation.4 | loop fusion | flops 6420480 | bytes 12861440 | tf_op jit(solution)/shard_map/reduce_sum | solution.py:20
  272.8 77.9 %psum.14 = f32[2048]{0:T(1024)S(1)} all-reduce(f32[2048]{0:T(1024)S(1)} %fusion), channel_id=1, replica_groups=mesh['dp'=4,'cent'=32] {'cent'}, use_global_device_ids=true, to_apply=%region_4.0 | all-reduce | flops 2048 | bytes 16384 | tf_op jit(solution)/shard_map/psum | solution.py:20
  350.6 9.6 %convert_reduce_fusion = (f32[1568]{0:T(1024)S(1)}, bf16[2048,1568]{0,1:T(8,128)(2,1)}) fusion(f32[2048]{0:T(1024)S(1)} %psum.14, f32[2048,1568]{0,1:T(8,128)} %get-tuple-element.5, f32[2048]{0:T(1024)S(1)} %pmax.7), kind=kLoop, calls=%fused_computation | loop fusion | flops 16054752 | bytes 19290240 | tf_op jit(solution)/shard_map/reduce_sum | solution.py:29
  360.2 11.8 %fusion.2 = f32[1568,1024]{1,0:T(8,128)} fusion(bf16[2048,1568]{0,1:T(8,128)(2,1)} %get-tuple-element.3, bf16[2048,1024]{1,0:T(8,128)(2,1)} %all-gather.2.cloned.1.call-done), kind=kOutput, calls=%fused_computation.11 | convolution fusion | flops 6576668672 | bytes 17039360 | tf_op jit(solution)/shard_map/dot_general | solution.py:25
  372.0 0.0 reduce-scatter.2.cloned.1.call-update
  372.1 7.3 %psum.15 = f32[1568]{0:T(1024)S(1)} all-reduce(f32[1568]{0:T(1024)S(1)} %get-tuple-element.2), channel_id=1, replica_groups=mesh['dp'=4,'cent'=32] {'dp'}, use_global_device_ids=true, to_apply=%region_7.0 | all-reduce | flops 1568 | bytes 12544 | tf_op jit(solution)/shard_map/psum | solution.py:29
  379.3 0.6 dynamic-slice_add_fusion
  379.9 54.3 %reduce-scatter.2.cloned.1.call-done = f32[1568,256]{1,0:T(8,128)} async-done(((f32[1568,1024]{1,0:T(8,128)}), f32[1568,256]{1,0:T(8,128)}) %reduce-scatter.2.cloned.1.call-update) | async-done | bytes 1605648 | tf_op jit(solution)/shard_map/reduce_scatter | solution.py:28
  434.2 2.8 divide_convert_fusion.1
  (1 shorter events, 0.0 us)
Async XLA Ops:
  7.2 163.1 %all-gather.2.cloned.1.call-start = ((), (), s32[]{:S(2)}) async-start(), calls=%async_computation.1 | async-start | bytes 4325376 | tf_op jit(solution)/shard_map/all_gather | solution.py:12
  7.9 426.3 %reduce-scatter.2.cloned.1.call-start = ((), (), s32[]{:S(2)}) async-start(), calls=%async_computation.2 | async-start | bytes 8028160 | tf_op jit(solution)/shard_map/reduce_scatter | solution.py:28
Sparse Core Ops, SparseCore 0:
  9.6 160.5 all-gather.1
  372.2 61.9 reduce-scatter.1
where the time goes:
time: 445 us; the launch traced here: 444 us
  waiting for transfers between devices  215 us (48%)
  blocking collectives  169 us (38%)
  matrix products  24.3 us (5%)
  other arithmetic  22 us (5%)
  between operations  14.1 us (3%)
    all_gather x1, waiting for transfers between devices, on_device(): group = lax.all_gather(points, 'cent', axis=0, tiled=True)  160 us
    pmax x1, blocking collectives, on_device(): row_max = lax.pmax(local_max, 'cent')  83.5 us
    psum x1, blocking collectives, on_device(): lax.psum(jnp.sum(jnp.exp(logits - row_max[:, None]), axis=1), 'cent')  77.9 us
    reduce_scatter x1, waiting for transfers between devices, on_device(): sums = lax.psum_scatter(partial_sums, 'dp', scatter_dimension=1, tiled=True)  54.3 us
    dot_general x1, matrix products, on_device(): lax.dot_general(group, centroids, (((1,), (1,)), ((), ())), preferred_ele...  12.5 us
    dot_general x1, matrix products, on_device(): lax.dot_general(resp, group, (((0,), (0,)), ((), ())), preferred_element_...  11.8 us
    reduce_sum x1, other arithmetic, on_device(): counts = lax.psum(jnp.sum(resp.astype(jnp.float32), axis=0), 'dp')  9.56 us
  transfers between devices with their start and end apart: 2, of which 2 were waited for; matrix products, arithmetic and copies ran while one was open for 1% of the time, Pallas kernels for 0%

commit v1 on v0

v1 whole, which is shorter than its diff:
```python
import functools

import jax
import jax.numpy as jnp
from jax import lax
from jax.experimental import pallas as pl
from jax.experimental.pallas import tpu as pltpu
from jax.sharding import PartitionSpec as P

D = 1024
PTS_DEV = 64
N_CENT = 32
K_DEV = 1568
ROWS = PTS_DEV * N_CENT
WIDTH = D // 4
SCALE = 1.0 / D**0.5
VMEM = 56 * 1024 * 1024
SPAN = 256.0


def logits_body(sub, cent, cnorm, pts, logits, stats):
    p = pts[...]
    top, total = None, None
    for j in range(K_DEV // sub):
        rows = slice(j * sub, (j + 1) * sub)
        cross = lax.dot_general(
            cent[rows, :], p, (((1,), (1,)), ((), ())), preferred_element_type=jnp.float32
        )
        part = (2.0 * cross - cnorm[rows, :]) * SCALE
        logits[rows, :] = part
        part_top = jnp.max(part, axis=0, keepdims=True)
        new_top = part_top if top is None else jnp.maximum(top, part_top)
        part_total = jnp.sum(jnp.exp(part - new_top), axis=0, keepdims=True)
        total = part_total if top is None else total * jnp.exp(top - new_top) + part_total
        top = new_top
    stats[0:1, :] = top
    stats[1:2, :] = total


def local_logits(centroids, cnorm, points, tile=512, sub=784):
    rows = points.shape[0]
    return pl.pallas_call(
        functools.partial(logits_body, sub),
        grid=(rows // tile,),
        in_specs=[
            pl.BlockSpec((K_DEV, D), lambda i: (0, 0)),
            pl.BlockSpec((K_DEV, 1), lambda i: (0, 0)),
            pl.BlockSpec((tile, D), lambda i: (i, 0)),
        ],
        out_specs=[
            pl.BlockSpec((K_DEV, tile), lambda i: (0, i)),
            pl.BlockSpec((2, tile), lambda i: (0, i)),
        ],
        out_shape=[
            jax.ShapeDtypeStruct((K_DEV, rows), jnp.float32),
            jax.ShapeDtypeStruct((2, rows), jnp.float32),
        ],
        compiler_params=pltpu.CompilerParams(vmem_limit_bytes=VMEM),
        name="logits",
    )(centroids, cnorm, points)


def far_body(csub, half, logits, stats, pts, sums, counts, resp):
    acc, cnt = None, None
    for j in range(ROWS // csub):
        cols = slice(j * csub, (j + 1) * csub)
        r = (jnp.exp(logits[:, cols] - stats[0:1, cols]) * stats[1:2, cols]).astype(jnp.bfloat16)
        resp[:, cols] = r
        wide = r.astype(jnp.float32)
        for k in range(csub // 128):
            lanes = wide[:, k * 128 : (k + 1) * 128]
            cnt = lanes if cnt is None else cnt + lanes
        part = jnp.dot(r, pts[cols, :], preferred_element_type=jnp.float32)
        acc = part if acc is None else acc + part
    sums[...] = acc
    counts[...] = jnp.sum(cnt, axis=1, keepdims=True)


def far_sums(half, logits, stats, points, tile=784, csub=512):
    return pl.pallas_call(
        functools.partial(far_body, csub),
        grid_spec=pltpu.PrefetchScalarGridSpec(
            num_scalar_prefetch=1,
            grid=(K_DEV // tile,),
            in_specs=[
                pl.BlockSpec((tile, ROWS), lambda i, h: (i, 0)),
                pl.BlockSpec((2, ROWS), lambda i, h: (0, 0)),
                pl.BlockSpec((ROWS, D // 2), lambda i, h: (0, h[0])),
            ],
            out_specs=[
                pl.BlockSpec((tile, D // 2), lambda i, h: (i, 0)),
                pl.BlockSpec((tile, 1), lambda i, h: (i, 0)),
                pl.BlockSpec((tile, ROWS), lambda i, h: (i, 0)),
            ],
        ),
        out_shape=[
            jax.ShapeDtypeStruct((K_DEV, D // 2), jnp.float32),
            jax.ShapeDtypeStruct((K_DEV, 1), jnp.float32),
            jax.ShapeDtypeStruct((K_DEV, ROWS), jnp.bfloat16),
        ],
        compiler_params=pltpu.CompilerParams(vmem_limit_bytes=VMEM),
        name="far_sums",
    )(half, logits, stats, points)


def near_body(half, resp, pts, sums):
    sums[...] = jnp.dot(resp[...], pts[...], preferred_element_type=jnp.float32)


def near_sums(half, resp, points, tile=784):
    return pl.pallas_call(
        near_body,
        grid_spec=pltpu.PrefetchScalarGridSpec(
            num_scalar_prefetch=1,
            grid=(K_DEV // tile,),
            in_specs=[
                pl.BlockSpec((tile, ROWS), lambda i, h: (i, 0)),
                pl.BlockSpec((ROWS, D // 2), lambda i, h: (0, h[0])),
            ],
            out_specs=pl.BlockSpec((tile, D // 2), lambda i, h: (i, 0)),
        ),
        out_shape=jax.ShapeDtypeStruct((K_DEV, D // 2), jnp.float32),
        compiler_params=pltpu.CompilerParams(vmem_limit_bytes=VMEM),
        name="near_sums",
    )(half, resp, points)


TO_CORE = [(i, i ^ 1) for i in range(4)]
TO_Y = [(i, i ^ 2) for i in range(4)]


def on_device(points, centroids):
    dp = lax.axis_index("dp")
    core, y_hi = dp % 2, dp // 2
    cnorm = jnp.sum(jnp.square(centroids.astype(jnp.float32)), axis=1, keepdims=True)

    group = lax.all_to_all(
        jnp.broadcast_to(points[None], (N_CENT, PTS_DEV, D)), "cent", 0, 0
    ).reshape(ROWS, D)

    logits, stats = local_logits(centroids, cnorm, group)

    every = lax.all_to_all(jnp.broadcast_to(stats[None], (N_CENT, 2, ROWS)), "cent", 0, 0)
    row_max = jnp.max(every[:, 0], axis=0)
    total = jnp.sum(every[:, 1] * jnp.exp(every[:, 0] - row_max[None]), axis=0)
    partition = row_max + jnp.log(total)
    own_rows = lax.dynamic_slice_in_dim(partition, lax.axis_index("cent") * PTS_DEV, PTS_DEV, 0)
    scaled = jnp.stack([row_max, 1.0 / total])

    far, counts, resp = far_sums((1 - y_hi)[None], logits, scaled, group)

    def exchange_cores(sums):
        own = lax.dynamic_slice_in_dim(sums, core * WIDTH, WIDTH, 1)
        other = lax.dynamic_slice_in_dim(sums, (1 - core) * WIDTH, WIDTH, 1)
        return own + lax.ppermute(other, "dp", TO_CORE)

    chip_counts = counts + lax.ppermute(counts, "dp", TO_CORE)
    far_chip = exchange_cores(far)
    packed = (far_chip * (SPAN / (chip_counts + 0.25))).astype(jnp.float16)
    got = lax.ppermute(packed, "dp", TO_Y)
    far_counts = lax.ppermute(chip_counts, "dp", TO_Y)

    near_chip = exchange_cores(near_sums(y_hi[None], resp, group))
    own_cols = lax.dynamic_slice_in_dim(centroids, dp * WIDTH, WIDTH, 1).astype(jnp.float32)
    sums = near_chip + got.astype(jnp.float32) * ((far_counts + 0.25) * (1.0 / SPAN))
    fresh = (sums + 0.25 * own_cols) / (chip_counts + far_counts + 0.25)
    return fresh.astype(jnp.bfloat16), own_rows


def solution(mesh):
    placed = (P(("dp", "cent"), None), P("cent", None))
    return jax.shard_map(
        on_device,
        mesh=mesh,
        in_specs=placed,
        out_specs=(P("cent", "dp"), P(("dp", "cent"))),
        check_vma=False,
    )
```

time: 445 us -> 164 us (0.37)
  blocking collectives: 169 us -> 0 us
  waiting for transfers between devices: 215 us -> 84.3 us
  Pallas kernels: 0 us -> 30 us
  matrix products: 24.3 us -> 0 us
  starting transfers between devices: 0.08 us -> 23.3 us
  local copies, waits for them, and re-layouts: 0 us -> 14.1 us
  between operations: 14.1 us -> 0.77 us
  other arithmetic: 22 us -> 11.2 us
    all_gather x1 -> x0, waiting for transfers between devices: 160 us -> none  [on_device(): group = lax.all_gather(points, 'cent', axis=0, tiled=True)]
    psum x2 -> x0, blocking collectives: 85.1 us -> none  [the longest x1 77.9 us: on_device(): lax.psum(jnp.sum(jnp.exp(logits - row_max[:, None]), axis=1), 'cent')]
    pmax x1 -> x0, blocking collectives: 83.5 us -> none  [on_device(): row_max = lax.pmax(local_max, 'cent')]
    all_to_all x0 -> x2, waiting for transfers between devices: none -> 64.6 us  [the longest x1 52.2 us: on_device(): lax.all_to_all(jnp.broadcast_to(points[None], (N_CENT, PTS_DEV, D)), 'cen...]
    reduce_scatter x1 -> x0, waiting for transfers between devices: 54.3 us -> none  [on_device(): sums = lax.psum_scatter(partial_sums, 'dp', scatter_dimension=1, tiled=True)]
    pallas_call x0 -> x3, Pallas kernels: none -> 30 us  [the longest x1 13 us: local_logits(): pl.pallas_call(functools.partial(logits_body, sub), grid=(rows // tile,),...]
    dot_general x2 -> x0, matrix products: 24.3 us -> none  [the longest x1 12.5 us: on_device(): lax.dot_general(group, centroids, (((1,), (1,)), ((), ())), preferred_ele...]
    ppermute x0 -> x5, waiting for transfers between devices: none -> 19.6 us  [the longest x1 14.7 us: on_device(): got = lax.ppermute(packed, 'dp', TO_Y)]
  transfers between devices with their start and end apart: 2 -> 7, of which waited for: 2 -> 5; matrix products, arithmetic and copies ran while one was open for 1% -> 8% of each run, Pallas kernels for 0% -> 5%
where the time goes in v1:
time: 164 us
  waiting for transfers between devices  84.3 us (51%)
  Pallas kernels  30 us (18%)
  starting transfers between devices  23.3 us (14%)
  local copies, waits for them, and re-layouts  14.1 us (9%)
  other arithmetic  11.2 us (7%)
    all_to_all x1, waiting for transfers between devices, on_device(): lax.all_to_all(jnp.broadcast_to(points[None], (N_CENT, PTS_DEV, D)), 'cen...  52.2 us
    ppermute x1, waiting for transfers between devices, on_device(): got = lax.ppermute(packed, 'dp', TO_Y)  14.7 us
    pallas_call x1, Pallas kernels, local_logits(): pl.pallas_call(functools.partial(logits_body, sub), grid=(rows // tile,),...  13 us
    all_to_all x1, waiting for transfers between devices, on_device(): lax.all_to_all(jnp.broadcast_to(stats[None], (N_CENT, 2, ROWS)), 'cent',...  12.4 us
    pallas_call x1, Pallas kernels, far_sums(): pl.pallas_call(functools.partial(far_body, csub), grid_spec=pltpu.Prefetc...  9.7 us
    all_to_all x1, starting transfers between devices, on_device(): lax.all_to_all(jnp.broadcast_to(points[None], (N_CENT, PTS_DEV, D)), 'cen...  9.65 us
    pallas_call x1, Pallas kernels, near_sums(): pl.pallas_call(near_body, grid_spec=pltpu.PrefetchScalarGridSpec(num_scal...  7.39 us
    all_to_all x1, starting transfers between devices, on_device(): lax.all_to_all(jnp.broadcast_to(stats[None], (N_CENT, 2, ROWS)), 'cent',...  7.23 us
  transfers between devices with their start and end apart: 7, of which 5 were waited for; matrix products, arithmetic and copies ran while one was open for 8% of the time, Pallas kernels for 5%

profile of v1, /device:TPU:0, one launch (start us, length us, event | category | flops | bytes accessed | tf_op | source)
XLA Modules:
  0.0 163.8 jit_solution(3627779338201997103)
XLA Ops:
  0.6 3.4 %broadcast_in_dim.25 = bf16[32,64,1024]{2,1,0:T(8,128)(2,1)} broadcast(bf16[64,1024]{1,0:T(8,128)(2,1)} %param.2), dimensions={1,2} | broadcast | bytes 4325376 | tf_op jit(solution)/shard_map/broadcast_in_dim | solution.py:138
  4.0 0.0 copy-start
  4.0 9.7 %all-to-all-start = ((bf16[32,64,1024]{2,1,0:T(8,128)(2,1)}), bf16[32,64,1024]{2,1,0:T(8,128)(2,1)}, u32[]{:S(2)}, u32[]{:S(2)}) async-start(bf16[32,64,1024]{2,1,0:T(8,128)(2,1)} %broadcast_in_dim.25), calls=%async_computation | async-start | bytes 8388608 | tf_op jit(solution)/shard_map/all_to_all | solution.py:137
  13.7 0.0 copy-done
  13.7 0.7 multiply_reduce_fusion
  14.4 1.2 broadcast_in_dim.27.cnorm
  15.5 52.2 %all-to-all-done = bf16[32,64,1024]{2,1,0:T(8,128)(2,1)} async-done(((bf16[32,64,1024]{2,1,0:T(8,128)(2,1)}), bf16[32,64,1024]{2,1,0:T(8,128)(2,1)}, u32[]{:S(2)}, u32[]{:S(2)}) %all-to-all-start) | async-done | bytes 4194336 | tf_op jit(solution)/shard_map/all_to_all | solution.py:137
  67.8 13.0 %logits.1 = (f32[1568,2048]{1,0:T(8,128)}, f32[2,2048]{1,0:T(2,128)}) custom-call(bf16[1568,1024]{1,0:T(8,128)(2,1)} %cent.1, f32[1568,1]{1,0:T(8,128)} %broadcast_in_dim.27.cnorm, bf16[2048,1024]{1,0:T(8,128)(2,1)} %bitcast.2.pts), custom_call_target="tpu_custom_call" | custom-call | tf_op jit(solution)/shard_map/logits/pallas_call | solution.py:42
  80.7 1.7 %broadcast_in_dim.26 = f32[32,2,2048]{2,1,0:T(2,128)} broadcast(f32[2,2048]{1,0:T(2,128)} %get-tuple-element.8), dimensions={1,2} | broadcast | bytes 540672 | tf_op jit(solution)/shard_map/broadcast_in_dim | solution.py:143
  82.5 7.2 %all-to-all-start.1 = ((f32[32,2,2048]{2,1,0:T(2,128)}), f32[32,2,2048]{2,1,0:T(2,128)S(1)}, u32[]{:S(2)}, u32[]{:S(2)}) async-start(f32[32,2,2048]{2,1,0:T(2,128)} %broadcast_in_dim.26), calls=%async_computation.1 | async-start | bytes 1048576 | tf_op jit(solution)/shard_map/all_to_all | solution.py:143
  89.8 12.4 %all-to-all-done.1 = f32[32,2,2048]{2,1,0:T(2,128)S(1)} async-done(((f32[32,2,2048]{2,1,0:T(2,128)}), f32[32,2,2048]{2,1,0:T(2,128)S(1)}, u32[]{:S(2)}, u32[]{:S(2)}) %all-to-all-start.1) | async-done | bytes 524320 | tf_op jit(solution)/shard_map/all_to_all | solution.py:143
  102.1 0.5 slice_reduce_fusion
  102.6 0.2 fusion.4
  102.8 0.6 pad_maximum_fusion.stats
  103.4 9.7 %far_sums.1 = (f32[1568,512]{1,0:T(8,128)}, f32[1568,1]{1,0:T(8,128)}, bf16[1568,2048]{1,0:T(8,128)(2,1)}) custom-call(s32[1]{0:T(128)} %bitcast.1.half, f32[1568,2048]{1,0:T(8,128)} %get-tuple-element.7.logits, f32[2,2048]{1,0:T(2,128)} %pad_maximum_fusion.stats, bf16[2048,1024]{1,0:T(8,128)(2,1)} %bitcast.2.pts), custom_call_target="tpu_custom_call" | custom-call | tf_op jit(solution)/shard_map/far_sums/pallas_call | solution.py:80
  113.1 2.8 %constant_dynamic-slice_fusion = f32[1568,256]{1,0:T(8,128)} fusion(f32[1568,512]{1,0:T(8,128)} %get-tuple-element.10, s32[]{:T(128)S(6)} %select_n.28), kind=kLoop, calls=%fused_computation.15 | loop fusion | bytes 3211268 | tf_op jit(solution)/shard_map/dynamic_slice | solution.py:154
  115.9 0.0 collective-permute-start.1
  115.9 7.4 %near_sums.1 = f32[1568,512]{1,0:T(8,128)} custom-call(s32[1]{0:T(128)} %bitcast.half, bf16[1568,2048]{1,0:T(8,128)(2,1)} %get-tuple-element.9.resp, bf16[2048,1024]{1,0:T(8,128)(2,1)} %bitcast.2.pts), custom_call_target="tpu_custom_call" | custom-call | tf_op jit(solution)/shard_map/near_sums/pallas_call | solution.py:111
  123.3 0.0 copy-start.2
  123.3 2.8 %constant_dynamic-slice_fusion.1 = f32[1568,256]{1,0:T(8,128)} fusion(f32[1568,512]{1,0:T(8,128)} %near_sums.1, s32[]{:T(128)S(6)} %select_n.28), kind=kLoop, calls=%fused_computation.16 | loop fusion | bytes 3211268 | tf_op jit(solution)/shard_map/dynamic_slice | solution.py:154
  126.0 0.5 collective-permute-start
  126.5 0.0 copy-done.2
  126.5 0.3 copy.24
  126.8 0.1 collective-permute-start.2
  126.9 2.7 %collective-permute-done.2 = f32[1568,1]{0,1:T(1,128)S(1)} collective-permute-done((f32[1568,1]{0,1:T(1,128)S(1)}, f32[1568,1]{0,1:T(1,128)S(1)}, u32[]{:S(2)}, u32[]{:S(2)}) %collective-permute-start.2) | collective-permute-done | bytes 6304 | tf_op jit(solution)/shard_map/ppermute | solution.py:157
  129.6 0.3 copy.25
  129.9 0.1 add.54
  130.0 0.3 copy.26
  130.3 3.0 %collective-permute-start.4 = (f32[1568,1]{0,1:T(1,128)S(1)}, f32[1568,1]{0,1:T(1,128)S(1)}, u32[]{:S(2)}, u32[]{:S(2)}) collective-permute-start(f32[1568,1]{0,1:T(1,128)S(1)} %copy.26), channel_id=1, source_target_pairs={{0,64},{32,96},{64,0},{96,32},{1,65},{33,97},{65,1},{97,33},{2,66}... | collective-permute-start | bytes 18824 | tf_op jit(solution)/shard_map/ppermute | solution.py:161
  133.3 2.2 %collective-permute-done.4 = f32[1568,1]{0,1:T(1,128)S(1)} collective-permute-done((f32[1568,1]{0,1:T(1,128)S(1)}, f32[1568,1]{0,1:T(1,128)S(1)}, u32[]{:S(2)}, u32[]{:S(2)}) %collective-permute-start.4) | collective-permute-done | bytes 6304 | tf_op jit(solution)/shard_map/ppermute | solution.py:161
  135.5 0.3 copy.29
  135.8 0.5 add_reduce_fusion
  136.3 0.0 collective-permute-done.1
  136.3 0.0 copy-start.1
  136.4 3.2 %multiply_convert_fusion = f16[1568,256]{1,0:T(8,128)(2,1)} fusion(f32[1568,256]{1,0:T(8,128)} %collective-permute-done.1, f32[1568,512]{1,0:T(8,128)} %get-tuple-element.10, s32[]{:T(128)S(6)} %select_n.27, f32[1568]{0:T(1024)S(1)} %get-tuple-element.13), kind=kLoop, calls=%fused_computation.2 | loop fusion | flops 1204224 | bytes 4020356 | tf_op jit(solution)/shard_map/convert_element_type | solution.py:159
  139.6 2.9 %collective-permute-start.3 = (f16[1568,256]{1,0:T(8,128)(2,1)}, f16[1568,256]{1,0:T(8,128)(2,1)}, u32[]{:S(2)}, u32[]{:S(2)}) collective-permute-start(f16[1568,256]{1,0:T(8,128)(2,1)} %multiply_convert_fusion), channel_id=1, source_target_pairs={{0,64},{32,96},{64,0},{96,32},{1,65},{33,97},{65,1},{97,33},{2,66}... | collective-permute-start | bytes 2408456 | tf_op jit(solution)/shard_map/ppermute | solution.py:160
  142.5 0.6 dynamic-slice_add_fusion
  143.1 1.2 copy.28
  144.3 1.4 multiply_reduce_fusion.1
  145.7 0.0 collective-permute-done
  145.7 14.7 %collective-permute-done.3 = f16[1568,256]{1,0:T(8,128)(2,1)} collective-permute-done((f16[1568,256]{1,0:T(8,128)(2,1)}, f16[1568,256]{1,0:T(8,128)(2,1)}, u32[]{:S(2)}, u32[]{:S(2)}) %collective-permute-start.3) | collective-permute-done | bytes 802848 | tf_op jit(solution)/shard_map/ppermute | solution.py:160
  160.4 0.0 copy-done.1
  160.4 3.4 %divide_convert_fusion = bf16[1568,256]{1,0:T(8,128)(2,1)} fusion(f16[1568,256]{1,0:T(8,128)(2,1)} %collective-permute-done.3, f32[1568,256]{1,0:T(8,128)} %collective-permute-done, f32[1568,512]{1,0:T(8,128)S(1)} %copy-done.1, s32[]{:T(128)S(6)} %select_n.27, f32[1568]{0:T(1024)S(1)} %get-tuple-element.12, bf16[1568,1024]{1,0:T(8,128)(2,1)} %cent.1, ...), kind=kLoop, calls=%fused_computation.1 | loop fusion | flops 3612672 | bytes 5632264 | tf_op jit(solution)/shard_map/convert_element_type | solution.py:167
  (2 shorter events, 0.0 us)
Async XLA Ops:
  4.0 9.7 %copy-start = (bf16[1568,1024]{1,0:T(8,128)(2,1)S(1)}, bf16[1568,1024]{1,0:T(8,128)(2,1)}, u32[]{:S(2)}) copy-start(bf16[1568,1024]{1,0:T(8,128)(2,1)} %cent.1) | copy-start | bytes 9633796
  4.0 63.8 %all-to-all-start = ((bf16[32,64,1024]{2,1,0:T(8,128)(2,1)}), bf16[32,64,1024]{2,1,0:T(8,128)(2,1)}, u32[]{:S(2)}, u32[]{:S(2)}) async-start(bf16[32,64,1024]{2,1,0:T(8,128)(2,1)} %broadcast_in_dim.25), calls=%async_computation | async-start | bytes 8388608 | tf_op jit(solution)/shard_map/all_to_all | solution.py:137
  82.5 19.6 %all-to-all-start.1 = ((f32[32,2,2048]{2,1,0:T(2,128)}), f32[32,2,2048]{2,1,0:T(2,128)S(1)}, u32[]{:S(2)}, u32[]{:S(2)}) async-start(f32[32,2,2048]{2,1,0:T(2,128)} %broadcast_in_dim.26), calls=%async_computation.1 | async-start | bytes 1048576 | tf_op jit(solution)/shard_map/all_to_all | solution.py:143
  115.9 20.5 %collective-permute-start.1 = (f32[1568,256]{1,0:T(8,128)}, f32[1568,256]{1,0:T(8,128)}, u32[]{:S(2)}, u32[]{:S(2)}) collective-permute-start(f32[1568,256]{1,0:T(8,128)} %constant_dynamic-slice_fusion), channel_id=1, source_target_pairs={{0,32},{32,0},{64,96},{96,64},{1,33},{33,1},{65,97},{97,65},{2,34}... | collective-permute-start | bytes 4816904 | tf_op jit(solution)/shard_map/ppermute | solution.py:155
  123.3 3.3 %copy-start.2 = (f32[1568,1]{1,0:T(8,128)S(1)}, f32[1568,1]{1,0:T(8,128)}, u32[]{:S(2)}) copy-start(f32[1568,1]{1,0:T(8,128)} %get-tuple-element.11) | copy-start | bytes 18820
  126.0 19.7 %collective-permute-start = (f32[1568,256]{1,0:T(8,128)}, f32[1568,256]{1,0:T(8,128)}, u32[]{:S(2)}, u32[]{:S(2)}) collective-permute-start(f32[1568,256]{1,0:T(8,128)} %constant_dynamic-slice_fusion.1), channel_id=1, source_target_pairs={{0,32},{32,0},{64,96},{96,64},{1,33},{33,1},{65,97},{97,65},{2,34}... | collective-permute-start | bytes 4816904 | tf_op jit(solution)/shard_map/ppermute | solution.py:155
  126.8 2.8 %collective-permute-start.2 = (f32[1568,1]{0,1:T(1,128)S(1)}, f32[1568,1]{0,1:T(1,128)S(1)}, u32[]{:S(2)}, u32[]{:S(2)}) collective-permute-start(f32[1568,1]{0,1:T(1,128)S(1)} %copy.24), channel_id=1, source_target_pairs={{0,32},{32,0},{64,96},{96,64},{1,33},{33,1},{65,97},{97,65},{2,34}... | collective-permute-start | bytes 18824 | tf_op jit(solution)/shard_map/ppermute | solution.py:157
  130.3 5.2 %collective-permute-start.4 = (f32[1568,1]{0,1:T(1,128)S(1)}, f32[1568,1]{0,1:T(1,128)S(1)}, u32[]{:S(2)}, u32[]{:S(2)}) collective-permute-start(f32[1568,1]{0,1:T(1,128)S(1)} %copy.26), channel_id=1, source_target_pairs={{0,64},{32,96},{64,0},{96,32},{1,65},{33,97},{65,1},{97,33},{2,66}... | collective-permute-start | bytes 18824 | tf_op jit(solution)/shard_map/ppermute | solution.py:161
  136.3 24.1 %copy-start.1 = (f32[1568,512]{1,0:T(8,128)S(1)}, f32[1568,512]{1,0:T(8,128)}, u32[]{:S(2)}) copy-start(f32[1568,512]{1,0:T(8,128)} %near_sums.1) | copy-start | bytes 9633796
  139.6 20.8 %collective-permute-start.3 = (f16[1568,256]{1,0:T(8,128)(2,1)}, f16[1568,256]{1,0:T(8,128)(2,1)}, u32[]{:S(2)}, u32[]{:S(2)}) collective-permute-start(f16[1568,256]{1,0:T(8,128)(2,1)} %multiply_convert_fusion), channel_id=1, source_target_pairs={{0,64},{32,96},{64,0},{96,32},{1,65},{33,97},{65,1},{97,33},{2,66}... | collective-permute-start | bytes 2408456 | tf_op jit(solution)/shard_map/ppermute | solution.py:160

commit v2 on v0

v2 whole, which is shorter than its diff:
```python
import functools

import jax
import jax.numpy as jnp
from jax import lax
from jax.experimental import pallas as pl
from jax.experimental.pallas import tpu as pltpu
from jax.sharding import PartitionSpec as P

D = 1024
PTS_DEV = 64
N_CENT = 32
K_DEV = 1568
ROWS = PTS_DEV * N_CENT
WIDTH = D // 4
HALF = K_DEV // 2
SCALE = 1.0 / D**0.5
VMEM = 8 * 1024 * 1024
SPAN = 256.0

STEPS = (0, 1, 3, 2)
PIECES = tuple(
    tuple(("a", d, s) if part == "a" else ("b", s, d) for s in STEPS)
    for part, d in (
        ("a", 0), ("b", 0),
        ("a", 1), ("a", 3), ("b", 1), ("b", 3),
        ("a", 2), ("b", 2),
    )
)
UNIT = PTS_DEV
PIECE = 4 * UNIT
BLOCKS = 2 * 16


def block_of(unit, z, x):
    part, dz, dx = unit
    return (0 if part == "a" else 16) + ((z + dz) % 4) * 4 + (x + dx) % 4


def low_lanes():
    return lax.broadcasted_iota(jnp.int32, (8, 128), 1) < UNIT


IN_VMEM = pl.BlockSpec(memory_space=pltpu.VMEM)
IN_SMEM = pl.BlockSpec(memory_space=pltpu.SMEM)
ANYWHERE = pl.BlockSpec(memory_space=pl.ANY)


def call(body, name, pos, args, outs, scratch=(), flops=0, exps=0, far_args=(), after=(), far_outs=0):
    moved = sum(a.size * a.dtype.itemsize for a in (*args, *far_args, *outs))
    near = len(outs) - far_outs
    n = len(after)
    return pl.pallas_call(
        lambda p, *refs: body(p, *refs[n:]),
        in_specs=[IN_SMEM]
        + [ANYWHERE] * n
        + [IN_VMEM] * len(args)
        + [ANYWHERE] * len(far_args),
        out_specs=[IN_VMEM] * near + [ANYWHERE] * far_outs,
        out_shape=list(outs),
        scratch_shapes=list(scratch),
        compiler_params=pltpu.CompilerParams(vmem_limit_bytes=VMEM),
        cost_estimate=pl.CostEstimate(flops=flops, bytes_accessed=moved, transcendentals=exps),
        name=name,
    )(pos, *after, *args, *far_args)


def f32(*shape):
    return jax.ShapeDtypeStruct(shape, jnp.float32)


def bf16(*shape):
    return jax.ShapeDtypeStruct(shape, jnp.bfloat16)


def join_body(pos, *refs):
    ins, outs = refs[:-2], refs[-2:]
    n = len(ins) // 2
    for k, out in enumerate(outs):
        at = 0
        for ref in ins[k * n : (k + 1) * n]:
            out[at : at + ref.shape[0], :] = ref[...]
            at += ref.shape[0]


def join(pos, a, b):
    return call(join_body, "join", pos, (*a, *b), (bf16(PIECE, D), bf16(PIECE, D)))


def logits_body(n, units, prior, pos, *refs):
    cent, pts, before, refs = refs[0], refs[1 : 1 + n], refs[1 + n : 1 + n + prior], refs[1 + n + prior :]
    if prior:
        cnorm, out, weights, tops, place = refs
    elif units:
        cnorm, out, weights, tops = refs
    else:
        out, cnorm, weights, tops = refs
        for j in range(2):
            here = slice(j * HALF, (j + 1) * HALF)
            wide = cent[here, :].astype(jnp.float32)
            cnorm[here, :] = jnp.sum(wide * wide, axis=1, keepdims=True)
    low = low_lanes()
    rows = []
    for i in range(n):
        cols = slice(i * PIECE, (i + 1) * PIECE)
        top, total = [], []
        for j in range(2):
            here = slice(j * HALF, (j + 1) * HALF)
            cross = lax.dot_general(
                cent[here, :],
                pts[i][...],
                (((1,), (1,)), ((), ())),
                preferred_element_type=jnp.float32,
            )
            part = (2.0 * cross - cnorm[here, :]) * SCALE
            top.append(jnp.max(part, axis=0, keepdims=True))
            part = jnp.exp(part - top[j])
            weights[here, cols] = part
            tops[j : j + 1, cols] = top[j]
            total.append(jnp.sum(part, axis=0, keepdims=True))
        peak = jnp.maximum(top[0], top[1])
        whole = total[0] * jnp.exp(top[0] - peak) + total[1] * jnp.exp(top[1] - peak)
        for h in range(2):
            lanes = slice(h * 128, (h + 1) * 128)
            t = jnp.broadcast_to(peak[:, lanes], (8, 128))
            s = jnp.broadcast_to(whole[:, lanes], (8, 128))
            rows.append(jnp.where(low, t, pltpu.roll(s, UNIT, 1))[0:1])
            rows.append(jnp.where(low, pltpu.roll(t, UNIT, 1), s)[0:1])
    if not prior:
        for i, row in enumerate(rows):
            out[i : i + 1, :] = row
    else:
        all_rows = [b[i : i + 1, :] for b in before for i in range(b.shape[0])] + rows
        for unit, row in zip(units, all_rows):
            place[pl.ds(block_of(unit, pos[0], pos[1]), 1), :] = row
        whole = place[...]
        for j in range(N_CENT):
            out[j] = whole


def local_weights(pos, centroids, pts, cnorm=None, before=()):
    n = len(pts)
    units = sum(PIECES, ()) if cnorm is not None else ()
    stats = f32(N_CENT, BLOCKS, 128) if before else f32(4 * n, 128)
    args = (centroids, *pts, *before) + (() if cnorm is None else (cnorm,))
    outs = (stats,) + ((f32(K_DEV, 1),) if cnorm is None else ())
    outs += (f32(K_DEV, n * PIECE), f32(2, n * PIECE))
    return call(
        functools.partial(logits_body, n, units, len(before)),
        "weights",
        pos,
        args,
        outs,
        [pltpu.VMEM((BLOCKS, 128), jnp.float32)] if before else [],
        flops=2 * K_DEV * n * PIECE * D,
        exps=K_DEV * n * PIECE,
    )


def merge_stats(pos, every, tops, place, turned, rows):
    low = low_lanes()[0:1]
    peak = every[0]
    for j in range(1, N_CENT):
        peak = jnp.maximum(peak, every[j])
    total = jnp.zeros_like(peak)
    for j in range(N_CENT):
        e = every[j]
        total = total + jnp.exp(e - peak) * pltpu.roll(e, UNIT, 1)
    valid = lax.broadcasted_iota(jnp.int32, peak.shape, 1) < UNIT
    total = jnp.where(valid, total, 1.0)
    both = []
    for value in (peak, 1.0 / total):
        place[...] = value
        turned[...] = pltpu.roll(value, UNIT, 1)
        parts = []
        for units in PIECES:
            for h in range(2):
                first = place[pl.ds(block_of(units[2 * h], pos[0], pos[1]), 1), :]
                second = turned[pl.ds(block_of(units[2 * h + 1], pos[0], pos[1]), 1), :]
                parts.append(jnp.where(low, first, second))
        both.append(parts)
    at = 0
    for ref in tops:
        for h in range(ref.shape[1] // 128):
            lanes = slice(h * 128, (h + 1) * 128)
            rows[0:2, at * 128 : (at + 1) * 128] = jnp.exp(ref[:, lanes] - both[0][at]) * both[1][at]
            at += 1
    return peak + jnp.log(total)


def columns(pos, which):
    return pl.ds(pl.multiple_of(pos[which] * WIDTH, WIDTH), WIDTH)


def sums_body(chunk, pos, *refs):
    weights, pts, refs = refs[:3], refs[3:11], refs[11:]
    if chunk == 0:
        every, tops, sums = refs[0], refs[1:4], refs[4:8]
        partition, rows, resp, place, turned = refs[8:]
        partition[...] = merge_stats(pos, every, tops, place, turned, rows)
    else:
        rows, sums, resp = refs[0], refs[1:5], refs[5]
    half = slice(chunk * HALF, (chunk + 1) * HALF)
    cnt, p = None, 0
    for ref in weights:
        for j in range(ref.shape[1] // PIECE):
            here = slice(p * PIECE, (p + 1) * PIECE)
            part = ref[half, j * PIECE : (j + 1) * PIECE]
            r = (part * rows[chunk : chunk + 1, here]).astype(jnp.bfloat16)
            resp[:, here] = r
            wide = r.astype(jnp.float32)
            two = wide[:, :128] + wide[:, 128:]
            cnt = cnt + two if p else two
            p += 1
    for k in range(4):
        acc = None
        for p in range(8):
            d = jnp.dot(
                resp[:, p * PIECE : (p + 1) * PIECE],
                pts[p][:, columns(pos, 2 + k)],
                preferred_element_type=jnp.float32,
            )
            acc = acc + d if p else d
        sums[k][:, :WIDTH] = acc
    sums[0][:, WIDTH:] = jnp.broadcast_to(jnp.sum(cnt, axis=1, keepdims=True), (HALF, 128))


def chunk_sums(pos, chunk, weights, pts, stats):
    outs = [f32(HALF, WIDTH + 128)] + [f32(HALF, WIDTH)] * 3
    scratch = [pltpu.VMEM((HALF, ROWS), jnp.bfloat16)]
    if chunk == 0:
        outs += [f32(BLOCKS, 128), f32(8, ROWS)]
        scratch += [pltpu.VMEM((BLOCKS, 128), jnp.float32)] * 2
    return call(
        functools.partial(sums_body, chunk),
        "sums",
        pos,
        (*weights, *pts, *stats),
        outs,
        scratch,
        flops=2 * HALF * ROWS * D,
    )


def one_hot(shape):
    return (lax.broadcasted_iota(jnp.int32, shape, 0) == 0).astype(jnp.float32)


def pack_body(pos, first, second, got, *refs):
    packed, counts, row = refs[-3:]
    cnt = first[:, WIDTH:] + got[:, WIDTH:]
    counts[...] = cnt
    here = lax.dot_general(
        one_hot((128, 8)),
        cnt,
        (((0,), (1,)), ((), ())),
        precision=lax.Precision.HIGHEST,
        preferred_element_type=jnp.float32,
    )
    if len(refs) > 3:
        row[:8, :] = refs[0][...]
        row[8:, :] = here
    else:
        row[...] = here
    factor = SPAN / (cnt + 0.25)
    for k in range(2):
        lanes = slice(k * 128, (k + 1) * 128)
        packed[:, lanes] = (second[:, lanes] + got[:, lanes]) * factor


def pack(pos, first, second, got, after, before=()):
    outs = (f32(HALF, WIDTH), f32(HALF, 128), f32(16 if before else 8, HALF))
    return call(pack_body, "pack", pos, (first, second, got, *before), outs, after=after)


def near_body(pos, *refs):
    cent, near = refs[4:]
    for c in range(2):
        here = slice(c * HALF, (c + 1) * HALF)
        for k in range(2):
            lanes = slice(k * 128, (k + 1) * 128)
            own = cent[here, pl.ds(pl.multiple_of(pos[6] * WIDTH + k * 128, 128), 128)]
            total = refs[c][:, lanes] + refs[2 + c][:, lanes]
            near[here, lanes] = total + 0.25 * own.astype(jnp.float32)


def fresh_body(pos, near, counts0, counts1, far_row, far0, far1, out):
    for c, (counts, far) in enumerate(((counts0, far0), (counts1, far1))):
        here = slice(c * HALF, (c + 1) * HALF)
        far_counts = lax.dot_general(
            far_row[8 * c : 8 * (c + 1), :],
            one_hot((8, 128)),
            (((0,), (0,)), ((), ())),
            precision=lax.Precision.HIGHEST,
            preferred_element_type=jnp.float32,
        )
        weight = 1.0 / (counts[...] + far_counts + 0.25)
        factor = (far_counts + 0.25) * (1.0 / SPAN)
        for k in range(2):
            lanes = slice(k * 128, (k + 1) * 128)
            total = near[here, lanes] + far[:, lanes] * factor
            out[here, lanes] = (total * weight).astype(out.dtype)


FROM_PAIR = [(i, i ^ 1) for i in range(N_CENT)]


def from_x(d):
    return [(i, i - i % 8 + (i % 8 - 2 * d) % 8) for i in range(N_CENT)]


def from_z(d):
    return [(i, (i - 8 * d) % N_CENT) for i in range(N_CENT)]


TO_CORE = [(i, i ^ 1) for i in range(4)]
TO_Y = [(i, i ^ 2) for i in range(4)]


def on_device(points, centroids):
    dp, cent = lax.axis_index("dp"), lax.axis_index("cent")
    core, y_hi = dp % 2, dp // 2
    z, x, y_lo = cent // 8, cent // 2 % 4, cent % 2
    far, near = 2 * (1 - y_hi), 2 * y_hi
    pos = jnp.stack([z, x, far + 1 - core, far + core, near + 1 - core, near + core, dp])

    other = lax.ppermute(points, "cent", FROM_PAIR)
    first = jnp.where(y_lo == 0, points, other)
    second = jnp.where(y_lo == 0, other, points)
    half = PTS_DEV // 2
    a = jnp.concatenate([first[:half], second[:half]])
    b = jnp.concatenate([first[half:], second[half:]])
    a4, b4 = join(
        pos,
        [a] + [lax.ppermute(a, "cent", from_x(d)) for d in STEPS[1:]],
        [b] + [lax.ppermute(b, "cent", from_z(d)) for d in STEPS[1:]],
    )
    a1, b1 = lax.ppermute(a4, "cent", from_z(1)), lax.ppermute(b4, "cent", from_x(1))
    a3, b3 = lax.ppermute(a4, "cent", from_z(3)), lax.ppermute(b4, "cent", from_x(3))
    mid = PIECE // 2
    a2, b2 = join(
        pos,
        [lax.ppermute(a1[:mid], "cent", from_z(1)), lax.ppermute(a3[mid:], "cent", from_z(3))],
        [lax.ppermute(b1[:mid], "cent", from_x(1)), lax.ppermute(b3[mid:], "cent", from_x(3))],
    )
    pts = [a4, b4, a1, a3, b1, b3, a2, b2]

    st0, cnorm, w0, top0 = local_weights(pos, centroids, pts[:2])
    st1, w1, top1 = local_weights(pos, centroids, pts[2:6], cnorm)
    stats, w2, top2 = local_weights(pos, centroids, pts[6:], cnorm, (st0, st1))

    every = lax.all_to_all(stats, "cent", 0, 0)

    weights = (w0, w1, w2)
    *sums0, partition, rows = chunk_sums(pos, 0, weights, pts, (every, top0, top1, top2))
    sums1 = chunk_sums(pos, 1, weights, pts, (rows,))
    got0 = lax.ppermute(sums0[0], "dp", TO_CORE)
    got1 = lax.ppermute(sums1[0], "dp", TO_CORE)
    packed0, counts0, row = pack(pos, sums0[0], sums0[1], got0, (sums1[0],))
    packed1, counts1, row = pack(pos, sums1[0], sums1[1], got1, (), (row,))
    far = [lax.ppermute(p.astype(jnp.float16), "dp", TO_Y) for p in (packed0, packed1)]
    far_row = lax.ppermute(row, "dp", TO_Y)

    near_got = [lax.ppermute(s[2], "dp", TO_CORE) for s in (sums0, sums1)]
    (near,) = call(
        near_body,
        "near",
        pos,
        (sums0[3], sums1[3], *near_got, centroids),
        (f32(K_DEV, WIDTH),),
        after=(packed1,),
    )
    far = [f.astype(jnp.float32) for f in far]
    args = (near, counts0, counts1, far_row, *far)
    (fresh,) = call(fresh_body, "fresh", pos, args, (bf16(K_DEV, WIDTH),))

    mine = 4 * z + x
    own_rows = jnp.concatenate(
        [
            lax.dynamic_slice(partition, (mine + 16 * i, y_lo * half), (1, half))[0]
            for i in range(2)
        ]
    )
    return fresh, own_rows


def solution(mesh):
    placed = (P(("dp", "cent"), None), P("cent", None))
    return jax.shard_map(
        on_device,
        mesh=mesh,
        in_specs=placed,
        out_specs=(P("cent", "dp"), P(("dp", "cent"))),
        check_vma=False,
    )
```

time: 445 us -> 110 us (0.25)
  waiting for transfers between devices: 215 us -> 15.6 us
  blocking collectives: 169 us -> 15.7 us
  starting transfers between devices: 0.08 us -> 36.4 us
  Pallas kernels: 0 us -> 30.8 us
  matrix products: 24.3 us -> 0 us
  other arithmetic: 22 us -> 5.39 us
  between operations: 14.1 us -> 0.84 us
  local copies, waits for them, and re-layouts: 0 us -> 4.87 us
    all_gather x1 -> x0, waiting for transfers between devices: 160 us -> none  [on_device(): group = lax.all_gather(points, 'cent', axis=0, tiled=True)]
    psum x2 -> x0, blocking collectives: 85.1 us -> none  [the longest x1 77.9 us: on_device(): lax.psum(jnp.sum(jnp.exp(logits - row_max[:, None]), axis=1), 'cent')]
    pmax x1 -> x0, blocking collectives: 83.5 us -> none  [on_device(): row_max = lax.pmax(local_max, 'cent')]
    reduce_scatter x1 -> x0, waiting for transfers between devices: 54.3 us -> none  [on_device(): sums = lax.psum_scatter(partial_sums, 'dp', scatter_dimension=1, tiled=True)]
    ppermute x0 -> x22, starting transfers between devices: none -> 36.4 us  [the longest x3 7.19 us: on_device(): lax.ppermute(b, 'cent', from_z(d))]
    pallas_call x0 -> x11, Pallas kernels: none -> 30.8 us  [call(): pl.pallas_call(lambda p, *refs: body(p, *refs[n:]), in_specs=[IN_SMEM] +...]
    dot_general x2 -> x0, matrix products: 24.3 us -> none  [the longest x1 12.5 us: on_device(): lax.dot_general(group, centroids, (((1,), (1,)), ((), ())), preferred_ele...]
    reduce_sum x3 -> x0, other arithmetic: 18.6 us -> none  [the longest x1 9.56 us: on_device(): counts = lax.psum(jnp.sum(resp.astype(jnp.float32), axis=0), 'dp')]
  transfers between devices with their start and end apart: 2 -> 22, of which waited for: 2 -> 6; matrix products, arithmetic and copies ran while one was open for 1% -> 4% of each run, Pallas kernels for 0% -> 16%
where the time goes in v2:
time: 110 us
  starting transfers between devices  36.4 us (33%)
  Pallas kernels  30.8 us (28%)
  blocking collectives  15.7 us (14%)
  waiting for transfers between devices  15.6 us (14%)
  other arithmetic  5.39 us (5%)
  local copies, waits for them, and re-layouts  4.87 us (4%)
    pallas_call x11, Pallas kernels, call(): pl.pallas_call(lambda p, *refs: body(p, *refs[n:]), in_specs=[IN_SMEM] +...  30.8 us
    all_to_all x1, blocking collectives, on_device(): every = lax.all_to_all(stats, 'cent', 0, 0)  15.7 us
    ppermute x2, waiting for transfers between devices, on_device(): lax.ppermute(p.astype(jnp.float16), 'dp', TO_Y)  7.95 us
    ppermute x3, starting transfers between devices, on_device(): lax.ppermute(b, 'cent', from_z(d))  7.19 us
    ppermute x3, starting transfers between devices, on_device(): lax.ppermute(a, 'cent', from_x(d))  6.5 us
    unnamed x14, local copies, waits for them, and re-layouts  4.61 us
    ppermute x2, starting transfers between devices, on_device(): lax.ppermute(p.astype(jnp.float16), 'dp', TO_Y)  4.58 us
    ppermute x1, waiting for transfers between devices, on_device(): other = lax.ppermute(points, 'cent', FROM_PAIR)  3.71 us
  transfers between devices with their start and end apart: 22, of which 6 were waited for; matrix products, arithmetic and copies ran while one was open for 4% of the time, Pallas kernels for 16%

profile of v2, /device:TPU:0, one launch (start us, length us, event | category | flops | bytes accessed | tf_op | source)
XLA Modules:
  0.0 109.6 jit_solution(14471289828524656247)
XLA Ops:
  0.6 1.7 %collective-permute-start = (bf16[64,1024]{1,0:T(8,128)(2,1)}, bf16[64,1024]{1,0:T(8,128)(2,1)S(1)}, u32[]{:S(2)}, u32[]{:S(2)}) collective-permute-start(bf16[64,1024]{1,0:T(8,128)(2,1)} %param.2), channel_id=1, source_target_pairs={{0,1},{1,0},{2,3},{3,2},{4,5},{5,4},{6,7},{7,6},{8,9},{9,8},{10,11... | collective-permute-start | bytes 393224 | tf_op jit(solution)/shard_map/ppermute | solution.py:327
  2.4 3.7 %collective-permute-done = bf16[64,1024]{1,0:T(8,128)(2,1)S(1)} collective-permute-done((bf16[64,1024]{1,0:T(8,128)(2,1)}, bf16[64,1024]{1,0:T(8,128)(2,1)S(1)}, u32[]{:S(2)}, u32[]{:S(2)}) %collective-permute-start) | collective-permute-done | bytes 131104 | tf_op jit(solution)/shard_map/ppermute | solution.py:327
  6.1 0.9 broadcast_select_fusion.1
  7.0 3.3 %collective-permute-start.3 = (bf16[64,1024]{1,0:T(8,128)(2,1)S(1)}, bf16[64,1024]{1,0:T(8,128)(2,1)S(1)}, u32[]{:S(2)}, u32[]{:S(2)}) collective-permute-start(bf16[64,1024]{1,0:T(8,128)(2,1)S(1)} %pad_maximum_fusion.refs_0_), channel_id=1, source_target_pairs={{0,4},{1,5},{2,6},{3,7},{4,0},{5,1},{6,2},{7,3},{8,12},{9,13},{10,... | collective-permute-start | bytes 393224 | tf_op jit(solution)/shard_map/ppermute | solution.py:335
  10.3 0.6 collective-permute-start.2
  10.9 2.6 %collective-permute-start.1 = (bf16[64,1024]{1,0:T(8,128)(2,1)S(1)}, bf16[64,1024]{1,0:T(8,128)(2,1)S(1)}, u32[]{:S(2)}, u32[]{:S(2)}) collective-permute-start(bf16[64,1024]{1,0:T(8,128)(2,1)S(1)} %pad_maximum_fusion.refs_0_), channel_id=1, source_target_pairs={{0,6},{1,7},{2,0},{3,1},{4,2},{5,3},{6,4},{7,5},{8,14},{9,15},{10,... | collective-permute-start | bytes 393224 | tf_op jit(solution)/shard_map/ppermute | solution.py:335
  13.6 4.0 %collective-permute-start.6 = (bf16[64,1024]{1,0:T(8,128)(2,1)S(1)}, bf16[64,1024]{1,0:T(8,128)(2,1)S(1)}, u32[]{:S(2)}, u32[]{:S(2)}) collective-permute-start(bf16[64,1024]{1,0:T(8,128)(2,1)S(1)} %pad_maximum_fusion.1.refs_4_), channel_id=1, source_target_pairs={{0,16},{1,17},{2,18},{3,19},{4,20},{5,21},{6,22},{7,23},{8,24},{9,... | collective-permute-start | bytes 393224 | tf_op jit(solution)/shard_map/ppermute | solution.py:336
  17.5 1.0 collective-permute-start.5
  18.5 0.0 collective-permute-done.3.refs_3_
  18.5 2.2 %collective-permute-start.4 = (bf16[64,1024]{1,0:T(8,128)(2,1)S(1)}, bf16[64,1024]{1,0:T(8,128)(2,1)S(1)}, u32[]{:S(2)}, u32[]{:S(2)}) collective-permute-start(bf16[64,1024]{1,0:T(8,128)(2,1)S(1)} %pad_maximum_fusion.1.refs_4_), channel_id=1, source_target_pairs={{0,24},{1,25},{2,26},{3,27},{4,28},{5,29},{6,30},{7,31},{8,0},{9,1... | collective-permute-start | bytes 393224 | tf_op jit(solution)/shard_map/ppermute | solution.py:336
  20.8 0.1 stack.31.p
  20.9 0.0 collective-permute-done.2.refs_2_
  20.9 0.0 collective-permute-done.1.refs_1_
  20.9 0.2 collective-permute-done.6.refs_7_
  21.0 2.7 %collective-permute-done.5.refs_6_ = bf16[64,1024]{1,0:T(8,128)(2,1)S(1)} collective-permute-done((bf16[64,1024]{1,0:T(8,128)(2,1)S(1)}, bf16[64,1024]{1,0:T(8,128)(2,1)S(1)}, u32[]{:S(2)}, u32[]{:S(2)}) %collective-permute-start.5) | collective-permute-done | bytes 131104 | tf_op jit(solution)/shard_map/ppermute | solution.py:336
  23.7 0.0 collective-permute-done.4.refs_5_
  23.7 0.6 join.2
  24.3 0.5 collective-permute-start.8
  24.8 2.9 %collective-permute-start.7 = (bf16[256,1024]{1,0:T(8,128)(2,1)S(1)}, bf16[256,1024]{1,0:T(8,128)(2,1)S(1)}, u32[]{:S(2)}, u32[]{:S(2)}) collective-permute-start(bf16[256,1024]{1,0:T(8,128)(2,1)S(1)} %get-tuple-element.32.refs_1_.refs_3_), channel_id=1, source_target_pairs={{0,24},{1,25},{2,26},{3,27},{4,28},{5,29},{6,30},{7,31},{8,0},{9,1... | collective-permute-start | bytes 1572872 | tf_op jit(solution)/shard_map/ppermute | solution.py:338
  27.7 0.0 collective-permute-start.10
  27.7 3.2 %collective-permute-start.9 = (bf16[256,1024]{1,0:T(8,128)(2,1)S(1)}, bf16[256,1024]{1,0:T(8,128)(2,1)S(1)}, u32[]{:S(2)}, u32[]{:S(2)}) collective-permute-start(bf16[256,1024]{1,0:T(8,128)(2,1)S(1)} %get-tuple-element.33.refs_2_.refs_4_), channel_id=1, source_target_pairs={{0,6},{1,7},{2,0},{3,1},{4,2},{5,3},{6,4},{7,5},{8,14},{9,15},{10,... | collective-permute-start | bytes 1572872 | tf_op jit(solution)/shard_map/ppermute | solution.py:338
  31.0 1.9 %copy-done = bf16[1568,1024]{1,0:T(8,128)(2,1)S(1)} copy-done((bf16[1568,1024]{1,0:T(8,128)(2,1)S(1)}, bf16[1568,1024]{1,0:T(8,128)(2,1)}, u32[]{:S(2)}) %copy-start) | copy-done | bytes 3211288
  32.9 3.6 %weights.3 = (f32[8,128]{1,0:T(8,128)S(1)}, f32[1568,1]{1,0:T(8,128)S(1)}, f32[1568,512]{1,0:T(8,128)S(1)}, f32[2,512]{1,0:T(2,128)S(1)}) custom-call(s32[7]{0:T(128)S(1)} %stack.31.p, bf16[1568,1024]{1,0:T(8,128)(2,1)S(1)} %copy-done, bf16[256,1024]{1,0:T(8,128)(2,1)S(1)} %get-tuple-element.32.refs_1_.refs_3_, ...), custom_call_target="tpu_custom_call" | custom-call | flops 1644167168 | bytes 7485568 | tf_op jit(solution)/shard_map/weights/pallas_call | solution.py:53
  36.5 1.0 collective-permute-done.8.refs_2_.refs_6_
  37.6 0.1 collective-permute-start.12
  37.6 0.0 collective-permute-done.7.refs_1_.refs_5_
  37.7 3.3 %collective-permute-start.11 = (bf16[128,1024]{1,0:T(8,128)(2,1)S(1)}, bf16[128,1024]{1,0:T(8,128)(2,1)S(1)}, u32[]{:S(2)}, u32[]{:S(2)}) collective-permute-start(bf16[128,1024]{1,0:T(8,128)(2,1)S(1)} %slice.36), channel_id=1, source_target_pairs={{0,24},{1,25},{2,26},{3,27},{4,28},{5,29},{6,30},{7,31},{8,0},{9,1... | collective-permute-start | bytes 786440 | tf_op jit(solution)/shard_map/ppermute | solution.py:343
  41.0 0.0 collective-permute-done.10.refs_4_.refs_8_
  41.0 0.1 collective-permute-start.14
  41.1 0.0 collective-permute-done.9.refs_3_.refs_7_
  41.1 3.5 %collective-permute-start.13 = (bf16[128,1024]{1,0:T(8,128)(2,1)S(1)}, bf16[128,1024]{1,0:T(8,128)(2,1)S(1)}, u32[]{:S(2)}, u32[]{:S(2)}) collective-permute-start(bf16[128,1024]{1,0:T(8,128)(2,1)S(1)} %slice.38), channel_id=1, source_target_pairs={{0,6},{1,7},{2,0},{3,1},{4,2},{5,3},{6,4},{7,5},{8,14},{9,15},{10,... | collective-permute-start | bytes 786440 | tf_op jit(solution)/shard_map/ppermute | solution.py:344
  44.6 5.6 %weights.4 = (f32[16,128]{1,0:T(8,128)S(1)}, f32[1568,1024]{1,0:T(8,128)S(1)}, f32[2,1024]{1,0:T(2,128)S(1)}) custom-call(s32[7]{0:T(128)S(1)} %stack.31.p, bf16[1568,1024]{1,0:T(8,128)(2,1)S(1)} %copy-done.1, bf16[256,1024]{1,0:T(8,128)(2,1)S(1)} %collective-permute-done.7.refs_1_.refs_5_, bf16[256,1024]{1,0:T(8,128)(2,1)S(1)} %collective-permute-done.8.refs_2_.refs_6_, ...), custom_call_target="tpu_custom_call" | custom-call | flops 3288334336 | bytes 11753600 | tf_op jit(solution)/shard_map/weights/pallas_call | solution.py:53
  50.2 0.0 collective-permute-done.12.refs_1_
  50.2 0.0 collective-permute-done.11.refs_0_
  50.2 0.0 collective-permute-done.14.refs_3_
  50.2 0.0 collective-permute-done.13.refs_2_
  50.2 0.6 join.3
  50.8 3.3 %weights.5 = (f32[32,32,128]{2,1,0:T(8,128)S(1)}, f32[1568,512]{1,0:T(8,128)S(1)}, f32[2,512]{1,0:T(2,128)S(1)}) custom-call(s32[7]{0:T(128)S(1)} %stack.31.p, bf16[1568,1024]{1,0:T(8,128)(2,1)S(1)} %copy-done.1, bf16[256,1024]{1,0:T(8,128)(2,1)S(1)} %get-tuple-element.37.refs_1_.refs_9_, bf16[256,1024]{1,0:T(8,128)(2,1)S(1)} %get-tuple-element.38.refs_2_.refs_10_, ...), custom_call_target="tpu_custom_call" | custom-call | flops 1644167168 | bytes 8018048 | tf_op jit(solution)/shard_map/weights/pallas_call | solution.py:53
  54.1 15.7 %all_to_all.5.refs_11_ = f32[32,32,128]{2,1,0:T(8,128)S(1)} all-to-all(f32[32,32,128]{2,1,0:T(8,128)S(1)} %get-tuple-element.42), channel_id=1, replica_groups=mesh['dp'=4,'cent'=32] {'cent'}, dimensions={0} | all-to-all | bytes 1048576 | tf_op jit(solution)/shard_map/all_to_all | solution.py:352
  69.8 5.8 %sums.2 = (f32[784,384]{1,0:T(8,128)S(1)}, f32[784,256]{1,0:T(8,128)S(1)}, f32[784,256]{1,0:T(8,128)}, f32[784,256]{1,0:T(8,128)S(1)}, f32[32,128]{1,0:T(8,128)S(1)}, /*index=5*/f32[8,2048]{1,0:T(8,128)S(1)}) custom-call(s32[7]{0:T(128)S(1)} %stack.31.p, f32[1568,512]{1,0:T(8,128)S(1)} %get-tuple-element.34.refs_0_, ...), custom_call_target="tpu_custom_call" | custom-call | flops 3288334336 | bytes 21274624 | tf_op jit(solution)/shard_map/sums/pallas_call | solution.py:53
  75.5 0.0 collective-permute-start.16
  75.5 5.1 %sums.3 = (f32[784,384]{1,0:T(8,128)S(1)}, f32[784,256]{1,0:T(8,128)S(1)}, f32[784,256]{1,0:T(8,128)}, f32[784,256]{1,0:T(8,128)S(1)}) custom-call(s32[7]{0:T(128)S(1)} %stack.31.p, f32[1568,512]{1,0:T(8,128)S(1)} %get-tuple-element.34.refs_0_, f32[1568,1024]{1,0:T(8,128)S(1)} %get-tuple-element.36.refs_1_, f32[1568,512]{1,0:T(8,128)S(1)} %get-tuple-element.41.refs_2_, ...), custom_call_target="tpu_custom_call" | custom-call | flops 3288334336 | bytes 20717568 | tf_op jit(solution)/shard_map/sums/pallas_call | solution.py:53
  80.6 0.5 collective-permute-start.15
  81.1 0.0 collective-permute-start.18
  81.1 0.5 collective-permute-start.17
  81.7 1.0 pack.2
  82.7 0.9 convert_element_type.12
  83.6 2.9 %collective-permute-start.20 = (f16[784,256]{1,0:T(8,128)(2,1)}, f16[784,256]{1,0:T(8,128)(2,1)}, u32[]{:S(2)}, u32[]{:S(2)}) collective-permute-start(f16[784,256]{1,0:T(8,128)(2,1)} %convert_element_type.12), channel_id=1, source_target_pairs={{0,64},{32,96},{64,0},{96,32},{1,65},{33,97},{65,1},{97,33},{2,66}... | collective-permute-start | bytes 1204232 | tf_op jit(solution)/shard_map/ppermute | solution.py:361
  86.5 0.0 collective-permute-done.15.refs_2_
  86.5 1.0 pack.3
  87.6 0.8 copy-done.5
  88.3 0.8 convert_element_type.14
  89.2 1.7 %collective-permute-start.21 = (f16[784,256]{1,0:T(8,128)(2,1)}, f16[784,256]{1,0:T(8,128)(2,1)}, u32[]{:S(2)}, u32[]{:S(2)}) collective-permute-start(f16[784,256]{1,0:T(8,128)(2,1)} %convert_element_type.14), channel_id=1, source_target_pairs={{0,64},{32,96},{64,0},{96,32},{1,65},{33,97},{65,1},{97,33},{2,66}... | collective-permute-start | bytes 1204232 | tf_op jit(solution)/shard_map/ppermute | solution.py:361
  90.8 0.1 dynamic-slice_bitcast_fusion.1
  90.9 1.8 %collective-permute-start.19 = (f32[16,784]{1,0:T(8,128)S(1)}, f32[16,784]{1,0:T(8,128)S(1)}, u32[]{:S(2)}, u32[]{:S(2)}) collective-permute-start(f32[16,784]{1,0:T(8,128)S(1)} %get-tuple-element.59), channel_id=1, source_target_pairs={{0,64},{32,96},{64,0},{96,32},{1,65},{33,97},{65,1},{97,33},{2,66}... | collective-permute-start | bytes 150536 | tf_op jit(solution)/shard_map/ppermute | solution.py:362
  92.8 0.6 pad_maximum_fusion.2
  93.4 0.0 collective-permute-done.17.refs_3_
  93.4 1.9 %copy-done.2 = bf16[1568,1024]{1,0:T(8,128)(2,1)S(1)} copy-done((bf16[1568,1024]{1,0:T(8,128)(2,1)S(1)}, bf16[1568,1024]{1,0:T(8,128)(2,1)}, u32[]{:S(2)}) %copy-start.2) | copy-done | bytes 3211288
  95.3 1.6 %near.1.refs_0_ = f32[1568,256]{1,0:T(8,128)S(1)} custom-call(s32[7]{0:T(128)S(1)} %stack.31.p, f32[784,256]{1,0:T(8,128)S(1)} %get-tuple-element.52.refs_0_, f32[784,256]{1,0:T(8,128)S(1)} %get-tuple-element.53.refs_1_, f32[784,256]{1,0:T(8,128)S(1)} %get-tuple-element.54.refs_2_, f32[784,256]{1,0:T(8,128)} %collective-permute-done.17.refs_3_, ...), custom_call_target="tpu_custom_call" | custom-call | bytes 8028160 | tf_op jit(solution)/shard_map/near/pallas_call | solution.py:53
  96.9 0.8 collective-permute-done.20
  97.6 1.1 convert_element_type.13.refs_4_
  98.7 7.2 %collective-permute-done.21 = f16[784,256]{1,0:T(8,128)(2,1)} collective-permute-done((f16[784,256]{1,0:T(8,128)(2,1)}, f16[784,256]{1,0:T(8,128)(2,1)}, u32[]{:S(2)}, u32[]{:S(2)}) %collective-permute-start.21) | collective-permute-done | bytes 401440 | tf_op jit(solution)/shard_map/ppermute | solution.py:361
  105.9 1.1 convert_element_type.15.refs_5_
  107.0 2.6 %fresh.1 = bf16[1568,256]{1,0:T(8,128)(2,1)} custom-call(s32[7]{0:T(128)S(1)} %stack.31.p, f32[1568,256]{1,0:T(8,128)S(1)} %near.1.refs_0_, f32[784,128]{1,0:T(8,128)S(1)} %copy-done.4, f32[784,128]{1,0:T(8,128)S(1)} %copy-done.6, f32[16,784]{1,0:T(8,128)S(1)} %collective-permute-done.19.refs_3_, f32[784,256]{1,0:T(8,128)S(1)} %convert_element_type.13.refs_4_, ...), custom_call_target="tpu_custom_call" | custom-call | bytes 4867072 | tf_op jit(solution)/shard_map/fresh/pallas_call | solution.py:53
  (21 shorter events, 0.1 us)
Async XLA Ops:
  0.6 5.4 %collective-permute-start = (bf16[64,1024]{1,0:T(8,128)(2,1)}, bf16[64,1024]{1,0:T(8,128)(2,1)S(1)}, u32[]{:S(2)}, u32[]{:S(2)}) collective-permute-start(bf16[64,1024]{1,0:T(8,128)(2,1)} %param.2), channel_id=1, source_target_pairs={{0,1},{1,0},{2,3},{3,2},{4,5},{5,4},{6,7},{7,6},{8,9},{9,8},{10,11... | collective-permute-start | bytes 393224 | tf_op jit(solution)/shard_map/ppermute | solution.py:327
  7.0 11.5 %collective-permute-start.3 = (bf16[64,1024]{1,0:T(8,128)(2,1)S(1)}, bf16[64,1024]{1,0:T(8,128)(2,1)S(1)}, u32[]{:S(2)}, u32[]{:S(2)}) collective-permute-start(bf16[64,1024]{1,0:T(8,128)(2,1)S(1)} %pad_maximum_fusion.refs_0_), channel_id=1, source_target_pairs={{0,4},{1,5},{2,6},{3,7},{4,0},{5,1},{6,2},{7,3},{8,12},{9,13},{10,... | collective-permute-start | bytes 393224 | tf_op jit(solution)/shard_map/ppermute | solution.py:335
  10.3 10.5 %collective-permute-start.2 = (bf16[64,1024]{1,0:T(8,128)(2,1)S(1)}, bf16[64,1024]{1,0:T(8,128)(2,1)S(1)}, u32[]{:S(2)}, u32[]{:S(2)}) collective-permute-start(bf16[64,1024]{1,0:T(8,128)(2,1)S(1)} %pad_maximum_fusion.refs_0_), channel_id=1, source_target_pairs={{0,2},{1,3},{2,4},{3,5},{4,6},{5,7},{6,0},{7,1},{8,10},{9,11},{10,... | collective-permute-start | bytes 393224 | tf_op jit(solution)/shard_map/ppermute | solution.py:335
  10.9 9.9 %collective-permute-start.1 = (bf16[64,1024]{1,0:T(8,128)(2,1)S(1)}, bf16[64,1024]{1,0:T(8,128)(2,1)S(1)}, u32[]{:S(2)}, u32[]{:S(2)}) collective-permute-start(bf16[64,1024]{1,0:T(8,128)(2,1)S(1)} %pad_maximum_fusion.refs_0_), channel_id=1, source_target_pairs={{0,6},{1,7},{2,0},{3,1},{4,2},{5,3},{6,4},{7,5},{8,14},{9,15},{10,... | collective-permute-start | bytes 393224 | tf_op jit(solution)/shard_map/ppermute | solution.py:335
  13.6 7.5 %collective-permute-start.6 = (bf16[64,1024]{1,0:T(8,128)(2,1)S(1)}, bf16[64,1024]{1,0:T(8,128)(2,1)S(1)}, u32[]{:S(2)}, u32[]{:S(2)}) collective-permute-start(bf16[64,1024]{1,0:T(8,128)(2,1)S(1)} %pad_maximum_fusion.1.refs_4_), channel_id=1, source_target_pairs={{0,16},{1,17},{2,18},{3,19},{4,20},{5,21},{6,22},{7,23},{8,24},{9,... | collective-permute-start | bytes 393224 | tf_op jit(solution)/shard_map/ppermute | solution.py:336
  17.5 6.2 %collective-permute-start.5 = (bf16[64,1024]{1,0:T(8,128)(2,1)S(1)}, bf16[64,1024]{1,0:T(8,128)(2,1)S(1)}, u32[]{:S(2)}, u32[]{:S(2)}) collective-permute-start(bf16[64,1024]{1,0:T(8,128)(2,1)S(1)} %pad_maximum_fusion.1.refs_4_), channel_id=1, source_target_pairs={{0,8},{1,9},{2,10},{3,11},{4,12},{5,13},{6,14},{7,15},{8,16},{9,17... | collective-permute-start | bytes 393224 | tf_op jit(solution)/shard_map/ppermute | solution.py:336
  18.5 5.2 %collective-permute-start.4 = (bf16[64,1024]{1,0:T(8,128)(2,1)S(1)}, bf16[64,1024]{1,0:T(8,128)(2,1)S(1)}, u32[]{:S(2)}, u32[]{:S(2)}) collective-permute-start(bf16[64,1024]{1,0:T(8,128)(2,1)S(1)} %pad_maximum_fusion.1.refs_4_), channel_id=1, source_target_pairs={{0,24},{1,25},{2,26},{3,27},{4,28},{5,29},{6,30},{7,31},{8,0},{9,1... | collective-permute-start | bytes 393224 | tf_op jit(solution)/shard_map/ppermute | solution.py:336
  24.3 13.2 %collective-permute-start.8 = (bf16[256,1024]{1,0:T(8,128)(2,1)S(1)}, bf16[256,1024]{1,0:T(8,128)(2,1)S(1)}, u32[]{:S(2)}, u32[]{:S(2)}) collective-permute-start(bf16[256,1024]{1,0:T(8,128)(2,1)S(1)} %get-tuple-element.32.refs_1_.refs_3_), channel_id=1, source_target_pairs={{0,8},{1,9},{2,10},{3,11},{4,12},{5,13},{6,14},{7,15},{8,16},{9,17... | collective-permute-start | bytes 1572872 | tf_op jit(solution)/shard_map/ppermute | solution.py:339
  24.8 12.8 %collective-permute-start.7 = (bf16[256,1024]{1,0:T(8,128)(2,1)S(1)}, bf16[256,1024]{1,0:T(8,128)(2,1)S(1)}, u32[]{:S(2)}, u32[]{:S(2)}) collective-permute-start(bf16[256,1024]{1,0:T(8,128)(2,1)S(1)} %get-tuple-element.32.refs_1_.refs_3_), channel_id=1, source_target_pairs={{0,24},{1,25},{2,26},{3,27},{4,28},{5,29},{6,30},{7,31},{8,0},{9,1... | collective-permute-start | bytes 1572872 | tf_op jit(solution)/shard_map/ppermute | solution.py:338
  27.7 13.2 %collective-permute-start.10 = (bf16[256,1024]{1,0:T(8,128)(2,1)S(1)}, bf16[256,1024]{1,0:T(8,128)(2,1)S(1)}, u32[]{:S(2)}, u32[]{:S(2)}) collective-permute-start(bf16[256,1024]{1,0:T(8,128)(2,1)S(1)} %get-tuple-element.33.refs_2_.refs_4_), channel_id=1, source_target_pairs={{0,2},{1,3},{2,4},{3,5},{4,6},{5,7},{6,0},{7,1},{8,10},{9,11},{10,... | collective-permute-start | bytes 1572872 | tf_op jit(solution)/shard_map/ppermute | solution.py:339
  27.7 13.4 %collective-permute-start.9 = (bf16[256,1024]{1,0:T(8,128)(2,1)S(1)}, bf16[256,1024]{1,0:T(8,128)(2,1)S(1)}, u32[]{:S(2)}, u32[]{:S(2)}) collective-permute-start(bf16[256,1024]{1,0:T(8,128)(2,1)S(1)} %get-tuple-element.33.refs_2_.refs_4_), channel_id=1, source_target_pairs={{0,6},{1,7},{2,0},{3,1},{4,2},{5,3},{6,4},{7,5},{8,14},{9,15},{10,... | collective-permute-start | bytes 1572872 | tf_op jit(solution)/shard_map/ppermute | solution.py:338
  30.9 1.9 %copy-start = (bf16[1568,1024]{1,0:T(8,128)(2,1)S(1)}, bf16[1568,1024]{1,0:T(8,128)(2,1)}, u32[]{:S(2)}) copy-start(bf16[1568,1024]{1,0:T(8,128)(2,1)} %refs_5_.1) | copy-start | bytes 9633796
  32.9 11.7 %copy-start.1 = (bf16[1568,1024]{1,0:T(8,128)(2,1)S(1)}, bf16[1568,1024]{1,0:T(8,128)(2,1)}, u32[]{:S(2)}) copy-start(bf16[1568,1024]{1,0:T(8,128)(2,1)} %refs_5_.1) | copy-start | bytes 9633796
  37.6 12.6 %collective-permute-start.12 = (bf16[128,1024]{1,0:T(8,128)(2,1)S(1)}, bf16[128,1024]{1,0:T(8,128)(2,1)S(1)}, u32[]{:S(2)}, u32[]{:S(2)}) collective-permute-start(bf16[128,1024]{1,0:T(8,128)(2,1)S(1)} %slice.37), channel_id=1, source_target_pairs={{0,8},{1,9},{2,10},{3,11},{4,12},{5,13},{6,14},{7,15},{8,16},{9,17... | collective-permute-start | bytes 786440 | tf_op jit(solution)/shard_map/ppermute | solution.py:343
  37.7 12.5 %collective-permute-start.11 = (bf16[128,1024]{1,0:T(8,128)(2,1)S(1)}, bf16[128,1024]{1,0:T(8,128)(2,1)S(1)}, u32[]{:S(2)}, u32[]{:S(2)}) collective-permute-start(bf16[128,1024]{1,0:T(8,128)(2,1)S(1)} %slice.36), channel_id=1, source_target_pairs={{0,24},{1,25},{2,26},{3,27},{4,28},{5,29},{6,30},{7,31},{8,0},{9,1... | collective-permute-start | bytes 786440 | tf_op jit(solution)/shard_map/ppermute | solution.py:343
  41.0 9.2 %collective-permute-start.14 = (bf16[128,1024]{1,0:T(8,128)(2,1)S(1)}, bf16[128,1024]{1,0:T(8,128)(2,1)S(1)}, u32[]{:S(2)}, u32[]{:S(2)}) collective-permute-start(bf16[128,1024]{1,0:T(8,128)(2,1)S(1)} %slice.39), channel_id=1, source_target_pairs={{0,2},{1,3},{2,4},{3,5},{4,6},{5,7},{6,0},{7,1},{8,10},{9,11},{10,... | collective-permute-start | bytes 786440 | tf_op jit(solution)/shard_map/ppermute | solution.py:344
  41.1 9.1 %collective-permute-start.13 = (bf16[128,1024]{1,0:T(8,128)(2,1)S(1)}, bf16[128,1024]{1,0:T(8,128)(2,1)S(1)}, u32[]{:S(2)}, u32[]{:S(2)}) collective-permute-start(bf16[128,1024]{1,0:T(8,128)(2,1)S(1)} %slice.38), channel_id=1, source_target_pairs={{0,6},{1,7},{2,0},{3,1},{4,2},{5,3},{6,4},{7,5},{8,14},{9,15},{10,... | collective-permute-start | bytes 786440 | tf_op jit(solution)/shard_map/ppermute | solution.py:344
  75.5 6.1 %collective-permute-start.16 = (f32[784,384]{1,0:T(8,128)S(1)}, f32[784,384]{1,0:T(8,128)S(1)}, u32[]{:S(2)}, u32[]{:S(2)}) collective-permute-start(f32[784,384]{1,0:T(8,128)S(1)} %get-tuple-element.49.refs_1_), channel_id=1, source_target_pairs={{0,32},{32,0},{64,96},{96,64},{1,33},{33,1},{65,97},{97,65},{2,34}... | collective-permute-start | bytes 3612680 | tf_op jit(solution)/shard_map/ppermute | solution.py:357
  80.6 5.9 %collective-permute-start.15 = (f32[784,384]{1,0:T(8,128)S(1)}, f32[784,384]{1,0:T(8,128)S(1)}, u32[]{:S(2)}, u32[]{:S(2)}) collective-permute-start(f32[784,384]{1,0:T(8,128)S(1)} %get-tuple-element.47.refs_0_), channel_id=1, source_target_pairs={{0,32},{32,0},{64,96},{96,64},{1,33},{33,1},{65,97},{97,65},{2,34}... | collective-permute-start | bytes 3612680 | tf_op jit(solution)/shard_map/ppermute | solution.py:358
  81.1 12.2 %collective-permute-start.18 = (f32[784,256]{1,0:T(8,128)}, f32[784,256]{1,0:T(8,128)S(1)}, u32[]{:S(2)}, u32[]{:S(2)}) collective-permute-start(f32[784,256]{1,0:T(8,128)} %get-tuple-element.56), channel_id=1, source_target_pairs={{0,32},{32,0},{64,96},{96,64},{1,33},{33,1},{65,97},{97,65},{2,34}... | collective-permute-start | bytes 2408456 | tf_op jit(solution)/shard_map/ppermute | solution.py:364
  81.1 12.2 %collective-permute-start.17 = (f32[784,256]{1,0:T(8,128)}, f32[784,256]{1,0:T(8,128)}, u32[]{:S(2)}, u32[]{:S(2)}) collective-permute-start(f32[784,256]{1,0:T(8,128)} %get-tuple-element.55), channel_id=1, source_target_pairs={{0,32},{32,0},{64,96},{96,64},{1,33},{33,1},{65,97},{97,65},{2,34}... | collective-permute-start | bytes 2408456 | tf_op jit(solution)/shard_map/ppermute | solution.py:364
  82.7 4.9 %copy-start.3 = (f32[784,128]{1,0:T(8,128)}, f32[784,128]{1,0:T(8,128)S(1)}, u32[]{:S(2)}) copy-start(f32[784,128]{1,0:T(8,128)S(1)} %get-tuple-element.57.refs_1_) | copy-start | bytes 1204228
  83.6 14.0 %collective-permute-start.20 = (f16[784,256]{1,0:T(8,128)(2,1)}, f16[784,256]{1,0:T(8,128)(2,1)}, u32[]{:S(2)}, u32[]{:S(2)}) collective-permute-start(f16[784,256]{1,0:T(8,128)(2,1)} %convert_element_type.12), channel_id=1, source_target_pairs={{0,64},{32,96},{64,0},{96,32},{1,65},{33,97},{65,1},{97,33},{2,66}... | collective-permute-start | bytes 1204232 | tf_op jit(solution)/shard_map/ppermute | solution.py:361
  87.5 0.8 copy-start.5
  89.2 16.7 %collective-permute-start.21 = (f16[784,256]{1,0:T(8,128)(2,1)}, f16[784,256]{1,0:T(8,128)(2,1)}, u32[]{:S(2)}, u32[]{:S(2)}) collective-permute-start(f16[784,256]{1,0:T(8,128)(2,1)} %convert_element_type.14), channel_id=1, source_target_pairs={{0,64},{32,96},{64,0},{96,32},{1,65},{33,97},{65,1},{97,33},{2,66}... | collective-permute-start | bytes 1204232 | tf_op jit(solution)/shard_map/ppermute | solution.py:361
  90.9 16.0 %collective-permute-start.19 = (f32[16,784]{1,0:T(8,128)S(1)}, f32[16,784]{1,0:T(8,128)S(1)}, u32[]{:S(2)}, u32[]{:S(2)}) collective-permute-start(f32[16,784]{1,0:T(8,128)S(1)} %get-tuple-element.59), channel_id=1, source_target_pairs={{0,64},{32,96},{64,0},{96,32},{1,65},{33,97},{65,1},{97,33},{2,66}... | collective-permute-start | bytes 150536 | tf_op jit(solution)/shard_map/ppermute | solution.py:362
  93.4 1.9 %copy-start.2 = (bf16[1568,1024]{1,0:T(8,128)(2,1)S(1)}, bf16[1568,1024]{1,0:T(8,128)(2,1)}, u32[]{:S(2)}) copy-start(bf16[1568,1024]{1,0:T(8,128)(2,1)} %refs_5_.1) | copy-start | bytes 9633796
  96.8 10.1 %copy-start.4 = (f32[784,128]{1,0:T(8,128)S(1)}, f32[784,128]{1,0:T(8,128)}, u32[]{:S(2)}) copy-start(f32[784,128]{1,0:T(8,128)} %copy-done.3) | copy-start | bytes 1204228
  96.8 10.1 %copy-start.6 = (f32[784,128]{1,0:T(8,128)S(1)}, f32[784,128]{1,0:T(8,128)}, u32[]{:S(2)}) copy-start(f32[784,128]{1,0:T(8,128)} %copy-done.5) | copy-start | bytes 1204228

commit v3 on v2

--- a/solution.py
+++ b/solution.py
@@ -29,12 +29,12 @@
 )
 UNIT = PTS_DEV
 PIECE = 4 * UNIT
-BLOCKS = 2 * 16
+BLOCKS = 16
 
 
 def block_of(unit, z, x):
-    part, dz, dx = unit
-    return (0 if part == "a" else 16) + ((z + dz) % 4) * 4 + (x + dx) % 4
+    _, dz, dx = unit
+    return (z ^ dz) * 4 + (x ^ dx)
 
 
 def low_lanes():
@@ -73,6 +73,15 @@
     return jax.ShapeDtypeStruct(shape, jnp.bfloat16)
 
 
+def pair_body(pos, mine, other, a, b):
+    mid = UNIT // 2
+    for k, out in enumerate((a, b)):
+        rows = slice(k * mid, (k + 1) * mid)
+        m, o = mine[rows, :], other[rows, :]
+        out[:mid, :] = jnp.where(pos[7] == 0, m, o)
+        out[mid:, :] = jnp.where(pos[7] == 0, o, m)
+
+
 def join_body(pos, *refs):
     ins, outs = refs[:-2], refs[-2:]
     n = len(ins) // 2
@@ -90,11 +99,11 @@
 def logits_body(n, units, prior, pos, *refs):
     cent, pts, before, refs = refs[0], refs[1 : 1 + n], refs[1 + n : 1 + n + prior], refs[1 + n + prior :]
     if prior:
-        cnorm, out, weights, tops, place = refs
+        cnorm, out, *weights, tops, place = refs
     elif units:
-        cnorm, out, weights, tops = refs
+        cnorm, out, *weights, tops = refs
     else:
-        out, cnorm, weights, tops = refs
+        out, cnorm, *weights, tops = refs
         for j in range(2):
             here = slice(j * HALF, (j + 1) * HALF)
             wide = cent[here, :].astype(jnp.float32)
@@ -115,24 +124,28 @@
             part = (2.0 * cross - cnorm[here, :]) * SCALE
             top.append(jnp.max(part, axis=0, keepdims=True))
             part = jnp.exp(part - top[j])
-            weights[here, cols] = part
+            weights[j][:, cols] = part
             tops[j : j + 1, cols] = top[j]
             total.append(jnp.sum(part, axis=0, keepdims=True))
         peak = jnp.maximum(top[0], top[1])
         whole = total[0] * jnp.exp(top[0] - peak) + total[1] * jnp.exp(top[1] - peak)
+        logs = peak + jnp.log(whole)
         for h in range(2):
-            lanes = slice(h * 128, (h + 1) * 128)
-            t = jnp.broadcast_to(peak[:, lanes], (8, 128))
-            s = jnp.broadcast_to(whole[:, lanes], (8, 128))
-            rows.append(jnp.where(low, t, pltpu.roll(s, UNIT, 1))[0:1])
-            rows.append(jnp.where(low, pltpu.roll(t, UNIT, 1), s)[0:1])
+            rows.append(logs[:, h * 128 : (h + 1) * 128])
     if not prior:
         for i, row in enumerate(rows):
             out[i : i + 1, :] = row
     else:
         all_rows = [b[i : i + 1, :] for b in before for i in range(b.shape[0])] + rows
-        for unit, row in zip(units, all_rows):
-            place[pl.ds(block_of(unit, pos[0], pos[1]), 1), :] = row
+        for i, row in enumerate(all_rows):
+            straight = jnp.broadcast_to(row, (8, 128))
+            turned = pltpu.roll(straight, UNIT, 1)
+            for h in range(2):
+                unit = units[2 * i + h]
+                a = unit[0] == "a"
+                value = straight if (h == 0) == a else turned
+                lanes = slice(0, UNIT) if a else slice(UNIT, 128)
+                place[pl.ds(block_of(unit, pos[0], pos[1]), 1), lanes] = value[0:1, lanes]
         whole = place[...]
         for j in range(N_CENT):
             out[j] = whole
@@ -141,10 +154,10 @@
 def local_weights(pos, centroids, pts, cnorm=None, before=()):
     n = len(pts)
     units = sum(PIECES, ()) if cnorm is not None else ()
-    stats = f32(N_CENT, BLOCKS, 128) if before else f32(4 * n, 128)
+    stats = f32(N_CENT, BLOCKS, 128) if before else f32(2 * n, 128)
     args = (centroids, *pts, *before) + (() if cnorm is None else (cnorm,))
     outs = (stats,) + ((f32(K_DEV, 1),) if cnorm is None else ())
-    outs += (f32(K_DEV, n * PIECE), f32(2, n * PIECE))
+    outs += (f32(HALF, n * PIECE), f32(HALF, n * PIECE), f32(2, n * PIECE))
     return call(
         functools.partial(logits_body, n, units, len(before)),
         "weights",
@@ -164,10 +177,7 @@
         peak = jnp.maximum(peak, every[j])
     total = jnp.zeros_like(peak)
     for j in range(N_CENT):
-        e = every[j]
-        total = total + jnp.exp(e - peak) * pltpu.roll(e, UNIT, 1)
-    valid = lax.broadcasted_iota(jnp.int32, peak.shape, 1) < UNIT
-    total = jnp.where(valid, total, 1.0)
+        total = total + jnp.exp(every[j] - peak)
     both = []
     for value in (peak, 1.0 / total):
         place[...] = value
@@ -175,8 +185,12 @@
         parts = []
         for units in PIECES:
             for h in range(2):
-                first = place[pl.ds(block_of(units[2 * h], pos[0], pos[1]), 1), :]
-                second = turned[pl.ds(block_of(units[2 * h + 1], pos[0], pos[1]), 1), :]
+                pair = units[2 * h : 2 * h + 2]
+                refs = (place, turned) if pair[0][0] == "a" else (turned, place)
+                first, second = (
+                    ref[pl.ds(block_of(unit, pos[0], pos[1]), 1), :]
+                    for ref, unit in zip(refs, pair)
+                )
                 parts.append(jnp.where(low, first, second))
         both.append(parts)
     at = 0
@@ -200,12 +214,11 @@
         partition[...] = merge_stats(pos, every, tops, place, turned, rows)
     else:
         rows, sums, resp = refs[0], refs[1:5], refs[5]
-    half = slice(chunk * HALF, (chunk + 1) * HALF)
     cnt, p = None, 0
     for ref in weights:
         for j in range(ref.shape[1] // PIECE):
             here = slice(p * PIECE, (p + 1) * PIECE)
-            part = ref[half, j * PIECE : (j + 1) * PIECE]
+            part = ref[:, j * PIECE : (j + 1) * PIECE]
             r = (part * rows[chunk : chunk + 1, here]).astype(jnp.bfloat16)
             resp[:, here] = r
             wide = r.astype(jnp.float32)
@@ -306,11 +319,11 @@
 
 
 def from_x(d):
-    return [(i, i - i % 8 + (i % 8 - 2 * d) % 8) for i in range(N_CENT)]
+    return [(i, i ^ 2 * d) for i in range(N_CENT)]
 
 
 def from_z(d):
-    return [(i, (i - 8 * d) % N_CENT) for i in range(N_CENT)]
+    return [(i, i ^ 8 * d) for i in range(N_CENT)]
 
 
 TO_CORE = [(i, i ^ 1) for i in range(4)]
@@ -322,14 +335,11 @@
     core, y_hi = dp % 2, dp // 2
     z, x, y_lo = cent // 8, cent // 2 % 4, cent % 2
     far, near = 2 * (1 - y_hi), 2 * y_hi
-    pos = jnp.stack([z, x, far + 1 - core, far + core, near + 1 - core, near + core, dp])
+    pos = jnp.stack([z, x, far + 1 - core, far + core, near + 1 - core, near + core, dp, y_lo])
 
     other = lax.ppermute(points, "cent", FROM_PAIR)
-    first = jnp.where(y_lo == 0, points, other)
-    second = jnp.where(y_lo == 0, other, points)
     half = PTS_DEV // 2
-    a = jnp.concatenate([first[:half], second[:half]])
-    b = jnp.concatenate([first[half:], second[half:]])
+    a, b = call(pair_body, "pair", pos, (points, other), (bf16(UNIT, D), bf16(UNIT, D)))
     a4, b4 = join(
         pos,
         [a] + [lax.ppermute(a, "cent", from_x(d)) for d in STEPS[1:]],
@@ -340,20 +350,20 @@
     mid = PIECE // 2
     a2, b2 = join(
         pos,
-        [lax.ppermute(a1[:mid], "cent", from_z(1)), lax.ppermute(a3[mid:], "cent", from_z(3))],
-        [lax.ppermute(b1[:mid], "cent", from_x(1)), lax.ppermute(b3[mid:], "cent", from_x(3))],
+        [lax.ppermute(a3[:mid], "cent", from_z(1)), lax.ppermute(a1[mid:], "cent", from_z(3))],
+        [lax.ppermute(b3[:mid], "cent", from_x(1)), lax.ppermute(b1[mid:], "cent", from_x(3))],
     )
     pts = [a4, b4, a1, a3, b1, b3, a2, b2]
 
-    st0, cnorm, w0, top0 = local_weights(pos, centroids, pts[:2])
-    st1, w1, top1 = local_weights(pos, centroids, pts[2:6], cnorm)
-    stats, w2, top2 = local_weights(pos, centroids, pts[6:], cnorm, (st0, st1))
+    st0, cnorm, *w0, top0 = local_weights(pos, centroids, pts[:2])
+    st1, *w1, top1 = local_weights(pos, centroids, pts[2:6], cnorm)
+    stats, *w2, top2 = local_weights(pos, centroids, pts[6:], cnorm, (st0, st1))
 
     every = lax.all_to_all(stats, "cent", 0, 0)
 
-    weights = (w0, w1, w2)
-    *sums0, partition, rows = chunk_sums(pos, 0, weights, pts, (every, top0, top1, top2))
-    sums1 = chunk_sums(pos, 1, weights, pts, (rows,))
+    weights = list(zip(w0, w1, w2))
+    *sums0, partition, rows = chunk_sums(pos, 0, weights[0], pts, (every, top0, top1, top2))
+    sums1 = chunk_sums(pos, 1, weights[1], pts, (rows,))
     got0 = lax.ppermute(sums0[0], "dp", TO_CORE)
     got1 = lax.ppermute(sums1[0], "dp", TO_CORE)
     packed0, counts0, row = pack(pos, sums0[0], sums0[1], got0, (sums1[0],))
@@ -377,7 +387,7 @@
     mine = 4 * z + x
     own_rows = jnp.concatenate(
         [
-            lax.dynamic_slice(partition, (mine + 16 * i, y_lo * half), (1, half))[0]
+            lax.dynamic_slice(partition, (mine, y_lo * half + UNIT * i), (1, half))[0]
             for i in range(2)
         ]
     )

time: 110 us -> 108 us (0.982)
  starting transfers between devices: 36.4 us -> 32.5 us
  waiting for transfers between devices: 15.6 us -> 18.9 us
  blocking collectives: 15.7 us -> 14 us
    ppermute x1, starting transfers between devices: 0.01 us -> 3.32 us  [on_device(): lax.ppermute(b4, 'cent', from_x(3))]
    ppermute x1, starting transfers between devices: 3.23 us -> 0.14 us  [on_device(): lax.ppermute(b4, 'cent', from_x(1))]
    ppermute x1, starting transfers between devices: 2.87 us -> 0.01 us  [on_device(): lax.ppermute(a4, 'cent', from_z(1))]
    ppermute x3, starting transfers between devices: 7.19 us -> 4.9 us  [on_device(): lax.ppermute(b, 'cent', from_z(d))]
    ppermute x3, starting transfers between devices: 6.5 us -> 4.41 us  [on_device(): lax.ppermute(a, 'cent', from_x(d))]
    ppermute x3, waiting for transfers between devices: 2.85 us -> 4.86 us  [on_device(): lax.ppermute(b, 'cent', from_z(d))]
    all_to_all x1, blocking collectives: 15.7 us -> 14 us  [on_device(): every = lax.all_to_all(stats, 'cent', 0, 0)]
    ppermute x1, starting transfers between devices: 0.51 us -> 2.16 us  [on_device(): lax.ppermute(a4, 'cent', from_z(3))]
  transfers between devices with their start and end apart: 22 -> 22, of which waited for: 6 -> 9; matrix products, arithmetic and copies ran while one was open for 4% -> 4% of each run, Pallas kernels for 16% -> 16%
where the time goes in v3:
time: 108 us; the launch traced here: 107 us
  starting transfers between devices  32.5 us (30%)
  Pallas kernels  31 us (29%)
  waiting for transfers between devices  18.9 us (17%)
  blocking collectives  14 us (13%)
  local copies, waits for them, and re-layouts  5.75 us (5%)
  other arithmetic  4.45 us (4%)
    pallas_call x12, Pallas kernels, call(): pl.pallas_call(lambda p, *refs: body(p, *refs[n:]), in_specs=[IN_SMEM] +...  31 us
    all_to_all x1, blocking collectives, on_device(): every = lax.all_to_all(stats, 'cent', 0, 0)  14 us
    ppermute x2, waiting for transfers between devices, on_device(): lax.ppermute(p.astype(jnp.float16), 'dp', TO_Y)  7.88 us
    unnamed x16, local copies, waits for them, and re-layouts  5.52 us
    ppermute x3, starting transfers between devices, on_device(): lax.ppermute(b, 'cent', from_z(d))  4.9 us
    ppermute x3, waiting for transfers between devices, on_device(): lax.ppermute(b, 'cent', from_z(d))  4.86 us
    ppermute x2, starting transfers between devices, on_device(): lax.ppermute(p.astype(jnp.float16), 'dp', TO_Y)  4.64 us
    ppermute x3, starting transfers between devices, on_device(): lax.ppermute(a, 'cent', from_x(d))  4.41 us
  transfers between devices with their start and end apart: 22, of which 9 were waited for; matrix products, arithmetic and copies ran while one was open for 4% of the time, Pallas kernels for 16%

profile of v3, /device:TPU:0, one launch (start us, length us, event | category | flops | bytes accessed | tf_op | source)
XLA Modules:
  0.0 107.4 jit_solution(11775689225195372896)
XLA Ops:
  0.6 1.7 %collective-permute-start = (bf16[64,1024]{1,0:T(8,128)(2,1)}, bf16[64,1024]{1,0:T(8,128)(2,1)S(1)}, u32[]{:S(2)}, u32[]{:S(2)}) collective-permute-start(bf16[64,1024]{1,0:T(8,128)(2,1)} %refs_0_.4), channel_id=1, source_target_pairs={{0,1},{1,0},{2,3},{3,2},{4,5},{5,4},{6,7},{7,6},{8,9},{9,8},{10,11... | collective-permute-start | bytes 393224 | tf_op jit(solution)/shard_map/ppermute | solution.py:340
  2.4 0.1 stack.35.p
  2.5 3.6 %collective-permute-done.refs_1_ = bf16[64,1024]{1,0:T(8,128)(2,1)S(1)} collective-permute-done((bf16[64,1024]{1,0:T(8,128)(2,1)}, bf16[64,1024]{1,0:T(8,128)(2,1)S(1)}, u32[]{:S(2)}, u32[]{:S(2)}) %collective-permute-start) | collective-permute-done | bytes 131104 | tf_op jit(solution)/shard_map/ppermute | solution.py:340
  6.1 0.9 copy-done.7
  7.0 0.6 pair.1
  7.6 3.3 %collective-permute-start.3 = (bf16[64,1024]{1,0:T(8,128)(2,1)S(1)}, bf16[64,1024]{1,0:T(8,128)(2,1)S(1)}, u32[]{:S(2)}, u32[]{:S(2)}) collective-permute-start(bf16[64,1024]{1,0:T(8,128)(2,1)S(1)} %get-tuple-element.37.refs_0_), channel_id=1, source_target_pairs={{0,4},{1,5},{2,6},{3,7},{4,0},{5,1},{6,2},{7,3},{8,12},{9,13},{10,... | collective-permute-start | bytes 393224 | tf_op jit(solution)/shard_map/ppermute | solution.py:345
  10.8 1.1 %collective-permute-start.2 = (bf16[64,1024]{1,0:T(8,128)(2,1)S(1)}, bf16[64,1024]{1,0:T(8,128)(2,1)S(1)}, u32[]{:S(2)}, u32[]{:S(2)}) collective-permute-start(bf16[64,1024]{1,0:T(8,128)(2,1)S(1)} %get-tuple-element.37.refs_0_), channel_id=1, source_target_pairs={{0,6},{1,7},{2,4},{3,5},{4,2},{5,3},{6,0},{7,1},{8,14},{9,15},{10,... | collective-permute-start | bytes 393224 | tf_op jit(solution)/shard_map/ppermute | solution.py:345
  12.0 0.0 collective-permute-start.1
  12.0 3.9 %collective-permute-start.6 = (bf16[64,1024]{1,0:T(8,128)(2,1)S(1)}, bf16[64,1024]{1,0:T(8,128)(2,1)S(1)}, u32[]{:S(2)}, u32[]{:S(2)}) collective-permute-start(bf16[64,1024]{1,0:T(8,128)(2,1)S(1)} %get-tuple-element.38.refs_4_), channel_id=1, source_target_pairs={{0,16},{1,17},{2,18},{3,19},{4,20},{5,21},{6,22},{7,23},{8,24},{9,... | collective-permute-start | bytes 393224 | tf_op jit(solution)/shard_map/ppermute | solution.py:346
  15.8 0.7 collective-permute-start.5
  16.6 0.0 collective-permute-done.3.refs_3_
  16.6 0.3 collective-permute-start.4
  16.9 0.1 collective-permute-done.2.refs_2_
  17.0 0.2 collective-permute-done.1.refs_1_
  17.2 1.7 %collective-permute-done.6.refs_7_ = bf16[64,1024]{1,0:T(8,128)(2,1)S(1)} collective-permute-done((bf16[64,1024]{1,0:T(8,128)(2,1)S(1)}, bf16[64,1024]{1,0:T(8,128)(2,1)S(1)}, u32[]{:S(2)}, u32[]{:S(2)}) %collective-permute-start.6) | collective-permute-done | bytes 131104 | tf_op jit(solution)/shard_map/ppermute | solution.py:346
  18.9 3.1 %collective-permute-done.5.refs_6_ = bf16[64,1024]{1,0:T(8,128)(2,1)S(1)} collective-permute-done((bf16[64,1024]{1,0:T(8,128)(2,1)S(1)}, bf16[64,1024]{1,0:T(8,128)(2,1)S(1)}, u32[]{:S(2)}, u32[]{:S(2)}) %collective-permute-start.5) | collective-permute-done | bytes 131104 | tf_op jit(solution)/shard_map/ppermute | solution.py:346
  22.0 0.0 collective-permute-done.4.refs_5_
  22.0 0.6 join.2
  22.6 2.2 %collective-permute-start.8 = (bf16[256,1024]{1,0:T(8,128)(2,1)S(1)}, bf16[256,1024]{1,0:T(8,128)(2,1)S(1)}, u32[]{:S(2)}, u32[]{:S(2)}) collective-permute-start(bf16[256,1024]{1,0:T(8,128)(2,1)S(1)} %get-tuple-element.39.refs_1_.refs_3_), channel_id=1, source_target_pairs={{0,24},{1,25},{2,26},{3,27},{4,28},{5,29},{6,30},{7,31},{8,16},{9,... | collective-permute-start | bytes 1572872 | tf_op jit(solution)/shard_map/ppermute | solution.py:349
  24.8 0.0 collective-permute-start.7
  24.8 3.3 %collective-permute-start.10 = (bf16[256,1024]{1,0:T(8,128)(2,1)S(1)}, bf16[256,1024]{1,0:T(8,128)(2,1)S(1)}, u32[]{:S(2)}, u32[]{:S(2)}) collective-permute-start(bf16[256,1024]{1,0:T(8,128)(2,1)S(1)} %get-tuple-element.40.refs_2_.refs_4_), channel_id=1, source_target_pairs={{0,6},{1,7},{2,4},{3,5},{4,2},{5,3},{6,0},{7,1},{8,14},{9,15},{10,... | collective-permute-start | bytes 1572872 | tf_op jit(solution)/shard_map/ppermute | solution.py:349
  28.1 0.1 collective-permute-start.9
  28.3 1.9 %copy-done = bf16[1568,1024]{1,0:T(8,128)(2,1)S(1)} copy-done((bf16[1568,1024]{1,0:T(8,128)(2,1)S(1)}, bf16[1568,1024]{1,0:T(8,128)(2,1)}, u32[]{:S(2)}) %copy-start) | copy-done | bytes 3211288
  30.2 3.5 %weights.3 = (f32[4,128]{1,0:T(4,128)S(1)}, f32[1568,1]{1,0:T(8,128)S(1)}, f32[784,512]{1,0:T(8,128)S(1)}, f32[784,512]{1,0:T(8,128)S(1)}, f32[2,512]{1,0:T(2,128)S(1)}) custom-call(s32[8]{0:T(128)S(1)} %stack.35.p, bf16[1568,1024]{1,0:T(8,128)(2,1)S(1)} %copy-done, bf16[256,1024]{1,0:T(8,128)(2,1)S(1)} %get-tuple-element.39.refs_1_.refs_3_, ...), custom_call_target="tpu_custom_call" | custom-call | flops 1644167168 | bytes 7483520 | tf_op jit(solution)/shard_map/weights/pallas_call | solution.py:53
  33.7 2.0 %collective-permute-done.8.refs_2_.refs_6_ = bf16[256,1024]{1,0:T(8,128)(2,1)S(1)} collective-permute-done((bf16[256,1024]{1,0:T(8,128)(2,1)S(1)}, bf16[256,1024]{1,0:T(8,128)(2,1)S(1)}, u32[]{:S(2)}, u32[]{:S(2)}) %collective-permute-start.8) | collective-permute-done | bytes 524320 | tf_op jit(solution)/shard_map/ppermute | solution.py:349
  35.8 0.1 collective-permute-start.11
  35.9 0.2 collective-permute-done.7.refs_1_.refs_5_
  36.1 2.4 %collective-permute-start.12 = (bf16[128,1024]{1,0:T(8,128)(2,1)S(1)}, bf16[128,1024]{1,0:T(8,128)(2,1)S(1)}, u32[]{:S(2)}, u32[]{:S(2)}) collective-permute-start(bf16[128,1024]{1,0:T(8,128)(2,1)S(1)} %slice.17), channel_id=1, source_target_pairs={{0,24},{1,25},{2,26},{3,27},{4,28},{5,29},{6,30},{7,31},{8,16},{9,... | collective-permute-start | bytes 786440 | tf_op jit(solution)/shard_map/ppermute | solution.py:353
  38.5 0.0 collective-permute-done.10.refs_4_.refs_8_
  38.5 3.5 %collective-permute-start.13 = (bf16[128,1024]{1,0:T(8,128)(2,1)S(1)}, bf16[128,1024]{1,0:T(8,128)(2,1)S(1)}, u32[]{:S(2)}, u32[]{:S(2)}) collective-permute-start(bf16[128,1024]{1,0:T(8,128)(2,1)S(1)} %slice.18), channel_id=1, source_target_pairs={{0,2},{1,3},{2,0},{3,1},{4,6},{5,7},{6,4},{7,5},{8,10},{9,11},{10,... | collective-permute-start | bytes 786440 | tf_op jit(solution)/shard_map/ppermute | solution.py:354
  42.0 0.0 collective-permute-done.9.refs_3_.refs_7_
  42.1 2.3 %collective-permute-start.14 = (bf16[128,1024]{1,0:T(8,128)(2,1)S(1)}, bf16[128,1024]{1,0:T(8,128)(2,1)S(1)}, u32[]{:S(2)}, u32[]{:S(2)}) collective-permute-start(bf16[128,1024]{1,0:T(8,128)(2,1)S(1)} %slice.19), channel_id=1, source_target_pairs={{0,6},{1,7},{2,4},{3,5},{4,2},{5,3},{6,0},{7,1},{8,14},{9,15},{10,... | collective-permute-start | bytes 786440 | tf_op jit(solution)/shard_map/ppermute | solution.py:354
  44.4 5.4 %weights.4 = (f32[8,128]{1,0:T(8,128)S(1)}, f32[784,1024]{1,0:T(8,128)S(1)}, f32[784,1024]{1,0:T(8,128)S(1)}, f32[2,1024]{1,0:T(2,128)S(1)}) custom-call(s32[8]{0:T(128)S(1)} %stack.35.p, bf16[1568,1024]{1,0:T(8,128)(2,1)S(1)} %copy-done.1, bf16[256,1024]{1,0:T(8,128)(2,1)S(1)} %collective-permute-done.7.refs_1_.refs_5_, ...), custom_call_target="tpu_custom_call" | custom-call | flops 3288334336 | bytes 11749504 | tf_op jit(solution)/shard_map/weights/pallas_call | solution.py:53
  49.8 0.0 collective-permute-done.11.refs_0_
  49.8 0.0 collective-permute-done.12.refs_1_
  49.9 0.0 collective-permute-done.14.refs_3_
  49.9 0.6 join.3
  50.5 3.2 %weights.5 = (f32[32,16,128]{2,1,0:T(8,128)S(1)}, f32[784,512]{1,0:T(8,128)S(1)}, f32[784,512]{1,0:T(8,128)S(1)}, f32[2,512]{1,0:T(2,128)S(1)}) custom-call(s32[8]{0:T(128)S(1)} %stack.35.p, bf16[1568,1024]{1,0:T(8,128)(2,1)S(1)} %copy-done.1, bf16[256,1024]{1,0:T(8,128)(2,1)S(1)} %get-tuple-element.44.refs_1_.refs_9_, ...), custom_call_target="tpu_custom_call" | custom-call | flops 1644167168 | bytes 7749760 | tf_op jit(solution)/shard_map/weights/pallas_call | solution.py:53
  53.8 14.0 %all_to_all.5.refs_11_ = f32[32,16,128]{2,1,0:T(8,128)S(1)} all-to-all(f32[32,16,128]{2,1,0:T(8,128)S(1)} %get-tuple-element.52), channel_id=1, replica_groups=mesh['dp'=4,'cent'=32] {'cent'}, dimensions={0} | all-to-all | bytes 524288 | tf_op jit(solution)/shard_map/all_to_all | solution.py:362
  67.8 5.7 %sums.2 = (f32[784,384]{1,0:T(8,128)S(1)}, f32[784,256]{1,0:T(8,128)S(1)}, f32[784,256]{1,0:T(8,128)}, f32[784,256]{1,0:T(8,128)S(1)}, f32[16,128]{1,0:T(8,128)S(1)}, /*index=5*/f32[8,2048]{1,0:T(8,128)S(1)}) custom-call(s32[8]{0:T(128)S(1)} %stack.35.p, f32[784,512]{1,0:T(8,128)S(1)} %get-tuple-element.49.refs_0_, ...), custom_call_target="tpu_custom_call" | custom-call | flops 3288334336 | bytes 14581760 | tf_op jit(solution)/shard_map/sums/pallas_call | solution.py:53
  73.4 0.0 collective-permute-start.16
  73.4 5.1 %sums.3 = (f32[784,384]{1,0:T(8,128)S(1)}, f32[784,256]{1,0:T(8,128)S(1)}, f32[784,256]{1,0:T(8,128)}, f32[784,256]{1,0:T(8,128)S(1)}) custom-call(s32[8]{0:T(128)S(1)} %stack.35.p, f32[784,512]{1,0:T(8,128)S(1)} %get-tuple-element.41.refs_0_, f32[784,1024]{1,0:T(8,128)S(1)} %get-tuple-element.43.refs_1_, f32[784,512]{1,0:T(8,128)S(1)} %get-tuple-element.48.refs_2_, ...), custom_call_target="tpu_custom_call" | custom-call | flops 3288334336 | bytes 14295040 | tf_op jit(solution)/shard_map/sums/pallas_call | solution.py:53
  78.5 0.5 collective-permute-start.15
  79.0 0.0 collective-permute-start.18
  79.0 0.5 collective-permute-start.17
  79.5 1.0 pack.2
  80.6 0.9 convert_element_type.12
  81.5 2.9 %collective-permute-start.20 = (f16[784,256]{1,0:T(8,128)(2,1)}, f16[784,256]{1,0:T(8,128)(2,1)}, u32[]{:S(2)}, u32[]{:S(2)}) collective-permute-start(f16[784,256]{1,0:T(8,128)(2,1)} %convert_element_type.12), channel_id=1, source_target_pairs={{0,64},{32,96},{64,0},{96,32},{1,65},{33,97},{65,1},{97,33},{2,66}... | collective-permute-start | bytes 1204232 | tf_op jit(solution)/shard_map/ppermute | solution.py:371
  84.4 0.0 collective-permute-done.15.refs_2_
  84.4 1.1 pack.3
  85.5 0.8 copy-done.5
  86.3 0.8 convert_element_type.14
  87.1 1.7 %collective-permute-start.21 = (f16[784,256]{1,0:T(8,128)(2,1)}, f16[784,256]{1,0:T(8,128)(2,1)}, u32[]{:S(2)}, u32[]{:S(2)}) collective-permute-start(f16[784,256]{1,0:T(8,128)(2,1)} %convert_element_type.14), channel_id=1, source_target_pairs={{0,64},{32,96},{64,0},{96,32},{1,65},{33,97},{65,1},{97,33},{2,66}... | collective-permute-start | bytes 1204232 | tf_op jit(solution)/shard_map/ppermute | solution.py:371
  88.8 0.1 dynamic-slice_bitcast_fusion.1
  88.9 1.8 %collective-permute-start.19 = (f32[16,784]{1,0:T(8,128)S(1)}, f32[16,784]{1,0:T(8,128)S(1)}, u32[]{:S(2)}, u32[]{:S(2)}) collective-permute-start(f32[16,784]{1,0:T(8,128)S(1)} %get-tuple-element.69), channel_id=1, source_target_pairs={{0,64},{32,96},{64,0},{96,32},{1,65},{33,97},{65,1},{97,33},{2,66}... | collective-permute-start | bytes 150536 | tf_op jit(solution)/shard_map/ppermute | solution.py:372
  90.7 0.6 pad_maximum_fusion
  91.3 1.9 %copy-done.2 = bf16[1568,1024]{1,0:T(8,128)(2,1)S(1)} copy-done((bf16[1568,1024]{1,0:T(8,128)(2,1)S(1)}, bf16[1568,1024]{1,0:T(8,128)(2,1)}, u32[]{:S(2)}) %copy-start.2) | copy-done | bytes 3211288
  93.2 1.6 %near.1.refs_0_ = f32[1568,256]{1,0:T(8,128)S(1)} custom-call(s32[8]{0:T(128)S(1)} %stack.35.p, f32[784,256]{1,0:T(8,128)S(1)} %get-tuple-element.62.refs_0_, f32[784,256]{1,0:T(8,128)S(1)} %get-tuple-element.63.refs_1_, f32[784,256]{1,0:T(8,128)S(1)} %get-tuple-element.64.refs_2_, f32[784,256]{1,0:T(8,128)} %collective-permute-done.17.refs_3_, ...), custom_call_target="tpu_custom_call" | custom-call | bytes 8028160 | tf_op jit(solution)/shard_map/near/pallas_call | solution.py:53
  94.8 0.7 collective-permute-done.20
  95.5 1.1 convert_element_type.13.refs_4_
  96.5 7.2 %collective-permute-done.21 = f16[784,256]{1,0:T(8,128)(2,1)} collective-permute-done((f16[784,256]{1,0:T(8,128)(2,1)}, f16[784,256]{1,0:T(8,128)(2,1)}, u32[]{:S(2)}, u32[]{:S(2)}) %collective-permute-start.21) | collective-permute-done | bytes 401440 | tf_op jit(solution)/shard_map/ppermute | solution.py:371
  103.7 1.1 convert_element_type.15.refs_5_
  104.8 0.0 collective-permute-done.19.refs_3_
  104.8 2.6 %fresh.1 = bf16[1568,256]{1,0:T(8,128)(2,1)} custom-call(s32[8]{0:T(128)S(1)} %stack.35.p, f32[1568,256]{1,0:T(8,128)S(1)} %near.1.refs_0_, f32[784,128]{1,0:T(8,128)S(1)} %copy-done.4, f32[784,128]{1,0:T(8,128)S(1)} %copy-done.6, f32[16,784]{1,0:T(8,128)S(1)} %collective-permute-done.19.refs_3_, f32[784,256]{1,0:T(8,128)S(1)} %convert_element_type.13.refs_4_, ...), custom_call_target="tpu_custom_call" | custom-call | bytes 4867072 | tf_op jit(solution)/shard_map/fresh/pallas_call | solution.py:53
  (20 shorter events, 0.1 us)
Async XLA Ops:
  0.6 5.4 %collective-permute-start = (bf16[64,1024]{1,0:T(8,128)(2,1)}, bf16[64,1024]{1,0:T(8,128)(2,1)S(1)}, u32[]{:S(2)}, u32[]{:S(2)}) collective-permute-start(bf16[64,1024]{1,0:T(8,128)(2,1)} %refs_0_.4), channel_id=1, source_target_pairs={{0,1},{1,0},{2,3},{3,2},{4,5},{5,4},{6,7},{7,6},{8,9},{9,8},{10,11... | collective-permute-start | bytes 393224 | tf_op jit(solution)/shard_map/ppermute | solution.py:340
  6.1 0.9 copy-start.7
  7.6 9.0 %collective-permute-start.3 = (bf16[64,1024]{1,0:T(8,128)(2,1)S(1)}, bf16[64,1024]{1,0:T(8,128)(2,1)S(1)}, u32[]{:S(2)}, u32[]{:S(2)}) collective-permute-start(bf16[64,1024]{1,0:T(8,128)(2,1)S(1)} %get-tuple-element.37.refs_0_), channel_id=1, source_target_pairs={{0,4},{1,5},{2,6},{3,7},{4,0},{5,1},{6,2},{7,3},{8,12},{9,13},{10,... | collective-permute-start | bytes 393224 | tf_op jit(solution)/shard_map/ppermute | solution.py:345
  10.8 6.2 %collective-permute-start.2 = (bf16[64,1024]{1,0:T(8,128)(2,1)S(1)}, bf16[64,1024]{1,0:T(8,128)(2,1)S(1)}, u32[]{:S(2)}, u32[]{:S(2)}) collective-permute-start(bf16[64,1024]{1,0:T(8,128)(2,1)S(1)} %get-tuple-element.37.refs_0_), channel_id=1, source_target_pairs={{0,6},{1,7},{2,4},{3,5},{4,2},{5,3},{6,0},{7,1},{8,14},{9,15},{10,... | collective-permute-start | bytes 393224 | tf_op jit(solution)/shard_map/ppermute | solution.py:345
  12.0 5.2 %collective-permute-start.1 = (bf16[64,1024]{1,0:T(8,128)(2,1)S(1)}, bf16[64,1024]{1,0:T(8,128)(2,1)S(1)}, u32[]{:S(2)}, u32[]{:S(2)}) collective-permute-start(bf16[64,1024]{1,0:T(8,128)(2,1)S(1)} %get-tuple-element.37.refs_0_), channel_id=1, source_target_pairs={{0,2},{1,3},{2,0},{3,1},{4,6},{5,7},{6,4},{7,5},{8,10},{9,11},{10,... | collective-permute-start | bytes 393224 | tf_op jit(solution)/shard_map/ppermute | solution.py:345
  12.0 6.9 %collective-permute-start.6 = (bf16[64,1024]{1,0:T(8,128)(2,1)S(1)}, bf16[64,1024]{1,0:T(8,128)(2,1)S(1)}, u32[]{:S(2)}, u32[]{:S(2)}) collective-permute-start(bf16[64,1024]{1,0:T(8,128)(2,1)S(1)} %get-tuple-element.38.refs_4_), channel_id=1, source_target_pairs={{0,16},{1,17},{2,18},{3,19},{4,20},{5,21},{6,22},{7,23},{8,24},{9,... | collective-permute-start | bytes 393224 | tf_op jit(solution)/shard_map/ppermute | solution.py:346
  15.8 6.2 %collective-permute-start.5 = (bf16[64,1024]{1,0:T(8,128)(2,1)S(1)}, bf16[64,1024]{1,0:T(8,128)(2,1)S(1)}, u32[]{:S(2)}, u32[]{:S(2)}) collective-permute-start(bf16[64,1024]{1,0:T(8,128)(2,1)S(1)} %get-tuple-element.38.refs_4_), channel_id=1, source_target_pairs={{0,24},{1,25},{2,26},{3,27},{4,28},{5,29},{6,30},{7,31},{8,16},{9,... | collective-permute-start | bytes 393224 | tf_op jit(solution)/shard_map/ppermute | solution.py:346
  16.6 5.5 %collective-permute-start.4 = (bf16[64,1024]{1,0:T(8,128)(2,1)S(1)}, bf16[64,1024]{1,0:T(8,128)(2,1)S(1)}, u32[]{:S(2)}, u32[]{:S(2)}) collective-permute-start(bf16[64,1024]{1,0:T(8,128)(2,1)S(1)} %get-tuple-element.38.refs_4_), channel_id=1, source_target_pairs={{0,8},{1,9},{2,10},{3,11},{4,12},{5,13},{6,14},{7,15},{8,0},{9,1},... | collective-permute-start | bytes 393224 | tf_op jit(solution)/shard_map/ppermute | solution.py:346
  22.6 13.1 %collective-permute-start.8 = (bf16[256,1024]{1,0:T(8,128)(2,1)S(1)}, bf16[256,1024]{1,0:T(8,128)(2,1)S(1)}, u32[]{:S(2)}, u32[]{:S(2)}) collective-permute-start(bf16[256,1024]{1,0:T(8,128)(2,1)S(1)} %get-tuple-element.39.refs_1_.refs_3_), channel_id=1, source_target_pairs={{0,24},{1,25},{2,26},{3,27},{4,28},{5,29},{6,30},{7,31},{8,16},{9,... | collective-permute-start | bytes 1572872 | tf_op jit(solution)/shard_map/ppermute | solution.py:349
  24.8 11.2 %collective-permute-start.7 = (bf16[256,1024]{1,0:T(8,128)(2,1)S(1)}, bf16[256,1024]{1,0:T(8,128)(2,1)S(1)}, u32[]{:S(2)}, u32[]{:S(2)}) collective-permute-start(bf16[256,1024]{1,0:T(8,128)(2,1)S(1)} %get-tuple-element.39.refs_1_.refs_3_), channel_id=1, source_target_pairs={{0,8},{1,9},{2,10},{3,11},{4,12},{5,13},{6,14},{7,15},{8,0},{9,1},... | collective-permute-start | bytes 1572872 | tf_op jit(solution)/shard_map/ppermute | solution.py:348
  24.8 13.7 %collective-permute-start.10 = (bf16[256,1024]{1,0:T(8,128)(2,1)S(1)}, bf16[256,1024]{1,0:T(8,128)(2,1)S(1)}, u32[]{:S(2)}, u32[]{:S(2)}) collective-permute-start(bf16[256,1024]{1,0:T(8,128)(2,1)S(1)} %get-tuple-element.40.refs_2_.refs_4_), channel_id=1, source_target_pairs={{0,6},{1,7},{2,4},{3,5},{4,2},{5,3},{6,0},{7,1},{8,14},{9,15},{10,... | collective-permute-start | bytes 1572872 | tf_op jit(solution)/shard_map/ppermute | solution.py:349
  28.1 13.9 %collective-permute-start.9 = (bf16[256,1024]{1,0:T(8,128)(2,1)S(1)}, bf16[256,1024]{1,0:T(8,128)(2,1)S(1)}, u32[]{:S(2)}, u32[]{:S(2)}) collective-permute-start(bf16[256,1024]{1,0:T(8,128)(2,1)S(1)} %get-tuple-element.40.refs_2_.refs_4_), channel_id=1, source_target_pairs={{0,2},{1,3},{2,0},{3,1},{4,6},{5,7},{6,4},{7,5},{8,10},{9,11},{10,... | collective-permute-start | bytes 1572872 | tf_op jit(solution)/shard_map/ppermute | solution.py:348
  28.3 1.9 %copy-start = (bf16[1568,1024]{1,0:T(8,128)(2,1)S(1)}, bf16[1568,1024]{1,0:T(8,128)(2,1)}, u32[]{:S(2)}) copy-start(bf16[1568,1024]{1,0:T(8,128)(2,1)} %refs_5_.1) | copy-start | bytes 9633796
  30.2 14.2 %copy-start.1 = (bf16[1568,1024]{1,0:T(8,128)(2,1)S(1)}, bf16[1568,1024]{1,0:T(8,128)(2,1)}, u32[]{:S(2)}) copy-start(bf16[1568,1024]{1,0:T(8,128)(2,1)} %refs_5_.1) | copy-start | bytes 9633796
  35.8 14.1 %collective-permute-start.11 = (bf16[128,1024]{1,0:T(8,128)(2,1)S(1)}, bf16[128,1024]{1,0:T(8,128)(2,1)S(1)}, u32[]{:S(2)}, u32[]{:S(2)}) collective-permute-start(bf16[128,1024]{1,0:T(8,128)(2,1)S(1)} %slice.16), channel_id=1, source_target_pairs={{0,8},{1,9},{2,10},{3,11},{4,12},{5,13},{6,14},{7,15},{8,0},{9,1},... | collective-permute-start | bytes 786440 | tf_op jit(solution)/shard_map/ppermute | solution.py:353
  36.1 13.8 %collective-permute-start.12 = (bf16[128,1024]{1,0:T(8,128)(2,1)S(1)}, bf16[128,1024]{1,0:T(8,128)(2,1)S(1)}, u32[]{:S(2)}, u32[]{:S(2)}) collective-permute-start(bf16[128,1024]{1,0:T(8,128)(2,1)S(1)} %slice.17), channel_id=1, source_target_pairs={{0,24},{1,25},{2,26},{3,27},{4,28},{5,29},{6,30},{7,31},{8,16},{9,... | collective-permute-start | bytes 786440 | tf_op jit(solution)/shard_map/ppermute | solution.py:353
  38.5 11.3 %collective-permute-start.13 = (bf16[128,1024]{1,0:T(8,128)(2,1)S(1)}, bf16[128,1024]{1,0:T(8,128)(2,1)S(1)}, u32[]{:S(2)}, u32[]{:S(2)}) collective-permute-start(bf16[128,1024]{1,0:T(8,128)(2,1)S(1)} %slice.18), channel_id=1, source_target_pairs={{0,2},{1,3},{2,0},{3,1},{4,6},{5,7},{6,4},{7,5},{8,10},{9,11},{10,... | collective-permute-start | bytes 786440 | tf_op jit(solution)/shard_map/ppermute | solution.py:354
  42.1 7.8 %collective-permute-start.14 = (bf16[128,1024]{1,0:T(8,128)(2,1)S(1)}, bf16[128,1024]{1,0:T(8,128)(2,1)S(1)}, u32[]{:S(2)}, u32[]{:S(2)}) collective-permute-start(bf16[128,1024]{1,0:T(8,128)(2,1)S(1)} %slice.19), channel_id=1, source_target_pairs={{0,6},{1,7},{2,4},{3,5},{4,2},{5,3},{6,0},{7,1},{8,14},{9,15},{10,... | collective-permute-start | bytes 786440 | tf_op jit(solution)/shard_map/ppermute | solution.py:354
  73.4 6.1 %collective-permute-start.16 = (f32[784,384]{1,0:T(8,128)S(1)}, f32[784,384]{1,0:T(8,128)S(1)}, u32[]{:S(2)}, u32[]{:S(2)}) collective-permute-start(f32[784,384]{1,0:T(8,128)S(1)} %get-tuple-element.59.refs_1_), channel_id=1, source_target_pairs={{0,32},{32,0},{64,96},{96,64},{1,33},{33,1},{65,97},{97,65},{2,34}... | collective-permute-start | bytes 3612680 | tf_op jit(solution)/shard_map/ppermute | solution.py:367
  78.5 5.9 %collective-permute-start.15 = (f32[784,384]{1,0:T(8,128)S(1)}, f32[784,384]{1,0:T(8,128)S(1)}, u32[]{:S(2)}, u32[]{:S(2)}) collective-permute-start(f32[784,384]{1,0:T(8,128)S(1)} %get-tuple-element.57.refs_0_), channel_id=1, source_target_pairs={{0,32},{32,0},{64,96},{96,64},{1,33},{33,1},{65,97},{97,65},{2,34}... | collective-permute-start | bytes 3612680 | tf_op jit(solution)/shard_map/ppermute | solution.py:368
  79.0 12.3 %collective-permute-start.18 = (f32[784,256]{1,0:T(8,128)}, f32[784,256]{1,0:T(8,128)S(1)}, u32[]{:S(2)}, u32[]{:S(2)}) collective-permute-start(f32[784,256]{1,0:T(8,128)} %get-tuple-element.66), channel_id=1, source_target_pairs={{0,32},{32,0},{64,96},{96,64},{1,33},{33,1},{65,97},{97,65},{2,34}... | collective-permute-start | bytes 2408456 | tf_op jit(solution)/shard_map/ppermute | solution.py:374
  79.0 12.3 %collective-permute-start.17 = (f32[784,256]{1,0:T(8,128)}, f32[784,256]{1,0:T(8,128)}, u32[]{:S(2)}, u32[]{:S(2)}) collective-permute-start(f32[784,256]{1,0:T(8,128)} %get-tuple-element.65), channel_id=1, source_target_pairs={{0,32},{32,0},{64,96},{96,64},{1,33},{33,1},{65,97},{97,65},{2,34}... | collective-permute-start | bytes 2408456 | tf_op jit(solution)/shard_map/ppermute | solution.py:374
  80.6 4.9 %copy-start.3 = (f32[784,128]{1,0:T(8,128)}, f32[784,128]{1,0:T(8,128)S(1)}, u32[]{:S(2)}) copy-start(f32[784,128]{1,0:T(8,128)S(1)} %get-tuple-element.67.refs_1_) | copy-start | bytes 1204228
  81.5 14.0 %collective-permute-start.20 = (f16[784,256]{1,0:T(8,128)(2,1)}, f16[784,256]{1,0:T(8,128)(2,1)}, u32[]{:S(2)}, u32[]{:S(2)}) collective-permute-start(f16[784,256]{1,0:T(8,128)(2,1)} %convert_element_type.12), channel_id=1, source_target_pairs={{0,64},{32,96},{64,0},{96,32},{1,65},{33,97},{65,1},{97,33},{2,66}... | collective-permute-start | bytes 1204232 | tf_op jit(solution)/shard_map/ppermute | solution.py:371
  85.5 0.8 copy-start.5
  87.1 16.6 %collective-permute-start.21 = (f16[784,256]{1,0:T(8,128)(2,1)}, f16[784,256]{1,0:T(8,128)(2,1)}, u32[]{:S(2)}, u32[]{:S(2)}) collective-permute-start(f16[784,256]{1,0:T(8,128)(2,1)} %convert_element_type.14), channel_id=1, source_target_pairs={{0,64},{32,96},{64,0},{96,32},{1,65},{33,97},{65,1},{97,33},{2,66}... | collective-permute-start | bytes 1204232 | tf_op jit(solution)/shard_map/ppermute | solution.py:371
  88.9 15.9 %collective-permute-start.19 = (f32[16,784]{1,0:T(8,128)S(1)}, f32[16,784]{1,0:T(8,128)S(1)}, u32[]{:S(2)}, u32[]{:S(2)}) collective-permute-start(f32[16,784]{1,0:T(8,128)S(1)} %get-tuple-element.69), channel_id=1, source_target_pairs={{0,64},{32,96},{64,0},{96,32},{1,65},{33,97},{65,1},{97,33},{2,66}... | collective-permute-start | bytes 150536 | tf_op jit(solution)/shard_map/ppermute | solution.py:372
  91.3 1.9 %copy-start.2 = (bf16[1568,1024]{1,0:T(8,128)(2,1)S(1)}, bf16[1568,1024]{1,0:T(8,128)(2,1)}, u32[]{:S(2)}) copy-start(bf16[1568,1024]{1,0:T(8,128)(2,1)} %refs_5_.1) | copy-start | bytes 9633796
  94.8 10.0 %copy-start.4 = (f32[784,128]{1,0:T(8,128)S(1)}, f32[784,128]{1,0:T(8,128)}, u32[]{:S(2)}) copy-start(f32[784,128]{1,0:T(8,128)} %copy-done.3) | copy-start | bytes 1204228
  94.8 10.0 %copy-start.6 = (f32[784,128]{1,0:T(8,128)S(1)}, f32[784,128]{1,0:T(8,128)}, u32[]{:S(2)}) copy-start(f32[784,128]{1,0:T(8,128)} %copy-done.5) | copy-start | bytes 1204228

commit v4 on v3

--- a/solution.py
+++ b/solution.py
@@ -43,6 +43,7 @@
 
 IN_VMEM = pl.BlockSpec(memory_space=pltpu.VMEM)
 IN_SMEM = pl.BlockSpec(memory_space=pltpu.SMEM)
+IN_HBM = pl.BlockSpec(memory_space=pltpu.HBM)
 ANYWHERE = pl.BlockSpec(memory_space=pl.ANY)
 
 
@@ -55,8 +56,8 @@
         in_specs=[IN_SMEM]
         + [ANYWHERE] * n
         + [IN_VMEM] * len(args)
-        + [ANYWHERE] * len(far_args),
-        out_specs=[IN_VMEM] * near + [ANYWHERE] * far_outs,
+        + [IN_HBM] * len(far_args),
+        out_specs=[IN_VMEM] * near + [IN_HBM] * far_outs,
         out_shape=list(outs),
         scratch_shapes=list(scratch),
         compiler_params=pltpu.CompilerParams(vmem_limit_bytes=VMEM),
@@ -71,15 +72,6 @@
 
 def bf16(*shape):
     return jax.ShapeDtypeStruct(shape, jnp.bfloat16)
-
-
-def pair_body(pos, mine, other, a, b):
-    mid = UNIT // 2
-    for k, out in enumerate((a, b)):
-        rows = slice(k * mid, (k + 1) * mid)
-        m, o = mine[rows, :], other[rows, :]
-        out[:mid, :] = jnp.where(pos[7] == 0, m, o)
-        out[mid:, :] = jnp.where(pos[7] == 0, o, m)
 
 
 def join_body(pos, *refs):
@@ -99,7 +91,12 @@
 def logits_body(n, units, prior, pos, *refs):
     cent, pts, before, refs = refs[0], refs[1 : 1 + n], refs[1 + n : 1 + n + prior], refs[1 + n + prior :]
     if prior:
-        cnorm, out, *weights, tops, place = refs
+        cnorm, *joined, out, weights0, weights1, tops, place = refs
+        weights = (weights0, weights1)
+        mid = PIECE // 2
+        for i, ref in enumerate(pts):
+            joined[i // 2][i % 2 * mid : (i % 2 + 1) * mid, :] = ref[...]
+        n, pts = n // 2, joined
     elif units:
         cnorm, out, *weights, tops = refs
     else:
@@ -152,14 +149,17 @@
 
 
 def local_weights(pos, centroids, pts, cnorm=None, before=()):
-    n = len(pts)
+    m = len(pts)
+    n = m // 2 if before else m
     units = sum(PIECES, ()) if cnorm is not None else ()
     stats = f32(N_CENT, BLOCKS, 128) if before else f32(2 * n, 128)
     args = (centroids, *pts, *before) + (() if cnorm is None else (cnorm,))
     outs = (stats,) + ((f32(K_DEV, 1),) if cnorm is None else ())
+    if before:
+        outs = (bf16(PIECE, D), bf16(PIECE, D), stats)
     outs += (f32(HALF, n * PIECE), f32(HALF, n * PIECE), f32(2, n * PIECE))
     return call(
-        functools.partial(logits_body, n, units, len(before)),
+        functools.partial(logits_body, m, units, len(before)),
         "weights",
         pos,
         args,
@@ -260,29 +260,26 @@
 
 
 def pack_body(pos, first, second, got, *refs):
-    packed, counts, row = refs[-3:]
     cnt = first[:, WIDTH:] + got[:, WIDTH:]
+    packed, counts = refs[1:3] if len(refs) > 2 else refs
     counts[...] = cnt
-    here = lax.dot_general(
-        one_hot((128, 8)),
-        cnt,
-        (((0,), (1,)), ((), ())),
-        precision=lax.Precision.HIGHEST,
-        preferred_element_type=jnp.float32,
-    )
-    if len(refs) > 3:
-        row[:8, :] = refs[0][...]
-        row[8:, :] = here
-    else:
-        row[...] = here
     factor = SPAN / (cnt + 0.25)
     for k in range(2):
         lanes = slice(k * 128, (k + 1) * 128)
         packed[:, lanes] = (second[:, lanes] + got[:, lanes]) * factor
+    if len(refs) > 2:
+        for c, here in enumerate((refs[0][...], cnt)):
+            refs[3][8 * c : 8 * (c + 1), :] = lax.dot_general(
+                one_hot((128, 8)),
+                here,
+                (((0,), (1,)), ((), ())),
+                precision=lax.Precision.HIGHEST,
+                preferred_element_type=jnp.float32,
+            )
 
 
 def pack(pos, first, second, got, after, before=()):
-    outs = (f32(HALF, WIDTH), f32(HALF, 128), f32(16 if before else 8, HALF))
+    outs = (f32(HALF, WIDTH), f32(HALF, 128)) + ((f32(16, HALF),) if before else ())
     return call(pack_body, "pack", pos, (first, second, got, *before), outs, after=after)
 
 
@@ -297,7 +294,8 @@
             near[here, lanes] = total + 0.25 * own.astype(jnp.float32)
 
 
-def fresh_body(pos, near, counts0, counts1, far_row, far0, far1, out):
+def fresh_body(pos, near, counts0, counts1, far_row, far0, far1, fresh, out, sem):
+    copies = []
     for c, (counts, far) in enumerate(((counts0, far0), (counts1, far1))):
         here = slice(c * HALF, (c + 1) * HALF)
         far_counts = lax.dot_general(
@@ -313,6 +311,10 @@
             lanes = slice(k * 128, (k + 1) * 128)
             total = near[here, lanes] + far[:, lanes] * factor
             out[here, lanes] = (total * weight).astype(out.dtype)
+        copies.append(pltpu.make_async_copy(out.at[here], fresh.at[here], sem.at[c]))
+        copies[c].start()
+    for c in copies:
+        c.wait()
 
 
 FROM_PAIR = [(i, i ^ 1) for i in range(N_CENT)]
@@ -335,11 +337,14 @@
     core, y_hi = dp % 2, dp // 2
     z, x, y_lo = cent // 8, cent // 2 % 4, cent % 2
     far, near = 2 * (1 - y_hi), 2 * y_hi
-    pos = jnp.stack([z, x, far + 1 - core, far + core, near + 1 - core, near + core, dp, y_lo])
+    pos = jnp.stack([z, x, far + 1 - core, far + core, near + 1 - core, near + core, dp])
 
     other = lax.ppermute(points, "cent", FROM_PAIR)
     half = PTS_DEV // 2
-    a, b = call(pair_body, "pair", pos, (points, other), (bf16(UNIT, D), bf16(UNIT, D)))
+    first = jnp.where(y_lo == 0, points, other)
+    second = jnp.where(y_lo == 0, other, points)
+    a = jnp.concatenate([first[:half], second[:half]])
+    b = jnp.concatenate([first[half:], second[half:]])
     a4, b4 = join(
         pos,
         [a] + [lax.ppermute(a, "cent", from_x(d)) for d in STEPS[1:]],
@@ -348,16 +353,18 @@
     a1, b1 = lax.ppermute(a4, "cent", from_z(1)), lax.ppermute(b4, "cent", from_x(1))
     a3, b3 = lax.ppermute(a4, "cent", from_z(3)), lax.ppermute(b4, "cent", from_x(3))
     mid = PIECE // 2
-    a2, b2 = join(
-        pos,
-        [lax.ppermute(a3[:mid], "cent", from_z(1)), lax.ppermute(a1[mid:], "cent", from_z(3))],
-        [lax.ppermute(b3[:mid], "cent", from_x(1)), lax.ppermute(b1[mid:], "cent", from_x(3))],
-    )
-    pts = [a4, b4, a1, a3, b1, b3, a2, b2]
+    last = [
+        lax.ppermute(a3[:mid], "cent", from_z(1)),
+        lax.ppermute(a1[mid:], "cent", from_z(3)),
+        lax.ppermute(b3[:mid], "cent", from_x(1)),
+        lax.ppermute(b1[mid:], "cent", from_x(3)),
+    ]
+    pts = [a4, b4, a1, a3, b1, b3]
 
     st0, cnorm, *w0, top0 = local_weights(pos, centroids, pts[:2])
     st1, *w1, top1 = local_weights(pos, centroids, pts[2:6], cnorm)
-    stats, *w2, top2 = local_weights(pos, centroids, pts[6:], cnorm, (st0, st1))
+    a2, b2, stats, *w2, top2 = local_weights(pos, centroids, last, cnorm, (st0, st1))
+    pts += [a2, b2]
 
     every = lax.all_to_all(stats, "cent", 0, 0)
 
@@ -366,8 +373,8 @@
     sums1 = chunk_sums(pos, 1, weights[1], pts, (rows,))
     got0 = lax.ppermute(sums0[0], "dp", TO_CORE)
     got1 = lax.ppermute(sums1[0], "dp", TO_CORE)
-    packed0, counts0, row = pack(pos, sums0[0], sums0[1], got0, (sums1[0],))
-    packed1, counts1, row = pack(pos, sums1[0], sums1[1], got1, (), (row,))
+    packed0, counts0 = pack(pos, sums0[0], sums0[1], got0, (sums1[0],))
+    packed1, counts1, row = pack(pos, sums1[0], sums1[1], got1, (), (counts0,))
     far = [lax.ppermute(p.astype(jnp.float16), "dp", TO_Y) for p in (packed0, packed1)]
     far_row = lax.ppermute(row, "dp", TO_Y)
 
@@ -382,7 +389,9 @@
     )
     far = [f.astype(jnp.float32) for f in far]
     args = (near, counts0, counts1, far_row, *far)
-    (fresh,) = call(fresh_body, "fresh", pos, args, (bf16(K_DEV, WIDTH),))
+    scratch = [pltpu.VMEM((K_DEV, WIDTH), jnp.bfloat16), pltpu.SemaphoreType.DMA((2,))]
+    out = (bf16(K_DEV, WIDTH),)
+    (fresh,) = call(fresh_body, "fresh", pos, args, out, scratch, far_outs=1)
 
     mine = 4 * z + x
     own_rows = jnp.concatenate(

time: 108 us -> 111 us (1.028)
  waiting for transfers between devices: 18.9 us -> 23.7 us
  local copies, waits for them, and re-layouts: 5.75 us -> 4.07 us
    ppermute x1, waiting for transfers between devices: 0.01 us -> 2.94 us  [on_device(): got1 = lax.ppermute(sums1[0], 'dp', TO_CORE)]
    ppermute x2, waiting for transfers between devices: 7.88 us -> 9.75 us  [on_device(): lax.ppermute(p.astype(jnp.float16), 'dp', TO_Y)]
    unnamed x16 -> x6, local copies, waits for them, and re-layouts: 5.52 us -> 3.82 us
    pallas_call x12 -> x10, Pallas kernels: 31 us -> 30.2 us  [call(): pl.pallas_call(lambda p, *refs: body(p, *refs[n:]), in_specs=[IN_SMEM] +...]
where the time goes in v4:
time: 111 us
  starting transfers between devices  32.6 us (29%)
  Pallas kernels  30.2 us (27%)
  waiting for transfers between devices  23.7 us (21%)
  blocking collectives  14 us (13%)
  other arithmetic  5.33 us (5%)
  local copies, waits for them, and re-layouts  4.07 us (4%)
    pallas_call x10, Pallas kernels, call(): pl.pallas_call(lambda p, *refs: body(p, *refs[n:]), in_specs=[IN_SMEM] +...  30.2 us
    all_to_all x1, blocking collectives, on_device(): every = lax.all_to_all(stats, 'cent', 0, 0)  14 us
    ppermute x2, waiting for transfers between devices, on_device(): lax.ppermute(p.astype(jnp.float16), 'dp', TO_Y)  9.75 us
    ppermute x3, starting transfers between devices, on_device(): lax.ppermute(b, 'cent', from_z(d))  4.98 us
    ppermute x3, waiting for transfers between devices, on_device(): lax.ppermute(b, 'cent', from_z(d))  4.95 us
    ppermute x3, starting transfers between devices, on_device(): lax.ppermute(a, 'cent', from_x(d))  4.41 us
    unnamed x6, local copies, waits for them, and re-layouts  3.82 us
    ppermute x1, waiting for transfers between devices, on_device(): other = lax.ppermute(points, 'cent', FROM_PAIR)  3.71 us
  transfers between devices with their start and end apart: 22, of which 9 were waited for; matrix products, arithmetic and copies ran while one was open for 4% of the time, Pallas kernels for 16%

profile of v4, /device:TPU:0, one launch (start us, length us, event | category | flops | bytes accessed | tf_op | source)
XLA Modules:
  0.0 110.9 jit_solution(1045527422830893238)
XLA Ops:
  0.6 1.7 %collective-permute-start = (bf16[64,1024]{1,0:T(8,128)(2,1)}, bf16[64,1024]{1,0:T(8,128)(2,1)S(1)}, u32[]{:S(2)}, u32[]{:S(2)}) collective-permute-start(bf16[64,1024]{1,0:T(8,128)(2,1)} %param.2), channel_id=1, source_target_pairs={{0,1},{1,0},{2,3},{3,2},{4,5},{5,4},{6,7},{7,6},{8,9},{9,8},{10,11... | collective-permute-start | bytes 393224 | tf_op jit(solution)/shard_map/ppermute | solution.py:342
  2.4 3.7 %collective-permute-done = bf16[64,1024]{1,0:T(8,128)(2,1)S(1)} collective-permute-done((bf16[64,1024]{1,0:T(8,128)(2,1)}, bf16[64,1024]{1,0:T(8,128)(2,1)S(1)}, u32[]{:S(2)}, u32[]{:S(2)}) %collective-permute-start) | collective-permute-done | bytes 131104 | tf_op jit(solution)/shard_map/ppermute | solution.py:342
  6.1 0.9 broadcast_select_fusion.1
  7.0 3.3 %collective-permute-start.3 = (bf16[64,1024]{1,0:T(8,128)(2,1)S(1)}, bf16[64,1024]{1,0:T(8,128)(2,1)S(1)}, u32[]{:S(2)}, u32[]{:S(2)}) collective-permute-start(bf16[64,1024]{1,0:T(8,128)(2,1)S(1)} %pad_maximum_fusion.refs_0_), channel_id=1, source_target_pairs={{0,4},{1,5},{2,6},{3,7},{4,0},{5,1},{6,2},{7,3},{8,12},{9,13},{10,... | collective-permute-start | bytes 393224 | tf_op jit(solution)/shard_map/ppermute | solution.py:350
  10.3 1.1 %collective-permute-start.2 = (bf16[64,1024]{1,0:T(8,128)(2,1)S(1)}, bf16[64,1024]{1,0:T(8,128)(2,1)S(1)}, u32[]{:S(2)}, u32[]{:S(2)}) collective-permute-start(bf16[64,1024]{1,0:T(8,128)(2,1)S(1)} %pad_maximum_fusion.refs_0_), channel_id=1, source_target_pairs={{0,6},{1,7},{2,4},{3,5},{4,2},{5,3},{6,0},{7,1},{8,14},{9,15},{10,... | collective-permute-start | bytes 393224 | tf_op jit(solution)/shard_map/ppermute | solution.py:350
  11.5 0.0 collective-permute-start.1
  11.5 4.0 %collective-permute-start.6 = (bf16[64,1024]{1,0:T(8,128)(2,1)S(1)}, bf16[64,1024]{1,0:T(8,128)(2,1)S(1)}, u32[]{:S(2)}, u32[]{:S(2)}) collective-permute-start(bf16[64,1024]{1,0:T(8,128)(2,1)S(1)} %pad_maximum_fusion.1.refs_4_), channel_id=1, source_target_pairs={{0,16},{1,17},{2,18},{3,19},{4,20},{5,21},{6,22},{7,23},{8,24},{9,... | collective-permute-start | bytes 393224 | tf_op jit(solution)/shard_map/ppermute | solution.py:351
  15.4 0.7 collective-permute-start.5
  16.1 0.0 collective-permute-done.3.refs_3_
  16.1 0.3 collective-permute-start.4
  16.5 0.1 stack.31.p
  16.5 0.0 collective-permute-done.2.refs_2_
  16.5 0.1 collective-permute-done.1.refs_1_
  16.7 1.8 %collective-permute-done.6.refs_7_ = bf16[64,1024]{1,0:T(8,128)(2,1)S(1)} collective-permute-done((bf16[64,1024]{1,0:T(8,128)(2,1)S(1)}, bf16[64,1024]{1,0:T(8,128)(2,1)S(1)}, u32[]{:S(2)}, u32[]{:S(2)}) %collective-permute-start.6) | collective-permute-done | bytes 131104 | tf_op jit(solution)/shard_map/ppermute | solution.py:351
  18.5 3.1 %collective-permute-done.5.refs_6_ = bf16[64,1024]{1,0:T(8,128)(2,1)S(1)} collective-permute-done((bf16[64,1024]{1,0:T(8,128)(2,1)S(1)}, bf16[64,1024]{1,0:T(8,128)(2,1)S(1)}, u32[]{:S(2)}, u32[]{:S(2)}) %collective-permute-start.5) | collective-permute-done | bytes 131104 | tf_op jit(solution)/shard_map/ppermute | solution.py:351
  21.6 0.0 collective-permute-done.4.refs_5_
  21.6 0.6 join.1
  22.2 2.2 %collective-permute-start.8 = (bf16[256,1024]{1,0:T(8,128)(2,1)S(1)}, bf16[256,1024]{1,0:T(8,128)(2,1)S(1)}, u32[]{:S(2)}, u32[]{:S(2)}) collective-permute-start(bf16[256,1024]{1,0:T(8,128)(2,1)S(1)} %get-tuple-element.34.refs_1_.refs_3_), channel_id=1, source_target_pairs={{0,24},{1,25},{2,26},{3,27},{4,28},{5,29},{6,30},{7,31},{8,16},{9,... | collective-permute-start | bytes 1572872 | tf_op jit(solution)/shard_map/ppermute | solution.py:354
  24.4 0.0 collective-permute-start.7
  24.4 3.2 %collective-permute-start.10 = (bf16[256,1024]{1,0:T(8,128)(2,1)S(1)}, bf16[256,1024]{1,0:T(8,128)(2,1)S(1)}, u32[]{:S(2)}, u32[]{:S(2)}) collective-permute-start(bf16[256,1024]{1,0:T(8,128)(2,1)S(1)} %get-tuple-element.35.refs_2_.refs_4_), channel_id=1, source_target_pairs={{0,6},{1,7},{2,4},{3,5},{4,2},{5,3},{6,0},{7,1},{8,14},{9,15},{10,... | collective-permute-start | bytes 1572872 | tf_op jit(solution)/shard_map/ppermute | solution.py:354
  27.6 0.2 collective-permute-start.9
  27.9 1.9 %copy-done = bf16[1568,1024]{1,0:T(8,128)(2,1)S(1)} copy-done((bf16[1568,1024]{1,0:T(8,128)(2,1)S(1)}, bf16[1568,1024]{1,0:T(8,128)(2,1)}, u32[]{:S(2)}) %copy-start) | copy-done | bytes 3211288
  29.8 3.5 %weights.3 = (f32[4,128]{1,0:T(4,128)S(1)}, f32[1568,1]{1,0:T(8,128)S(1)}, f32[784,512]{1,0:T(8,128)S(1)}, f32[784,512]{1,0:T(8,128)S(1)}, f32[2,512]{1,0:T(2,128)S(1)}) custom-call(s32[7]{0:T(128)S(1)} %stack.31.p, bf16[1568,1024]{1,0:T(8,128)(2,1)S(1)} %copy-done, bf16[256,1024]{1,0:T(8,128)(2,1)S(1)} %get-tuple-element.34.refs_1_.refs_3_, ...), custom_call_target="tpu_custom_call" | custom-call | flops 1644167168 | bytes 7483520 | tf_op jit(solution)/shard_map/weights/pallas_call | solution.py:54
  33.3 2.0 %collective-permute-done.8.refs_2_.refs_6_ = bf16[256,1024]{1,0:T(8,128)(2,1)S(1)} collective-permute-done((bf16[256,1024]{1,0:T(8,128)(2,1)S(1)}, bf16[256,1024]{1,0:T(8,128)(2,1)S(1)}, u32[]{:S(2)}, u32[]{:S(2)}) %collective-permute-start.8) | collective-permute-done | bytes 524320 | tf_op jit(solution)/shard_map/ppermute | solution.py:354
  35.4 0.1 collective-permute-start.11
  35.5 0.2 collective-permute-done.7.refs_1_.refs_5_
  35.6 2.5 %collective-permute-start.12 = (bf16[128,1024]{1,0:T(8,128)(2,1)S(1)}, bf16[128,1024]{1,0:T(8,128)(2,1)S(1)}, u32[]{:S(2)}, u32[]{:S(2)}) collective-permute-start(bf16[128,1024]{1,0:T(8,128)(2,1)S(1)} %slice.37), channel_id=1, source_target_pairs={{0,24},{1,25},{2,26},{3,27},{4,28},{5,29},{6,30},{7,31},{8,16},{9,... | collective-permute-start | bytes 786440 | tf_op jit(solution)/shard_map/ppermute | solution.py:358
  38.1 0.0 collective-permute-done.10.refs_4_.refs_8_
  38.1 3.5 %collective-permute-start.13 = (bf16[128,1024]{1,0:T(8,128)(2,1)S(1)}, bf16[128,1024]{1,0:T(8,128)(2,1)S(1)}, u32[]{:S(2)}, u32[]{:S(2)}) collective-permute-start(bf16[128,1024]{1,0:T(8,128)(2,1)S(1)} %slice.38), channel_id=1, source_target_pairs={{0,2},{1,3},{2,0},{3,1},{4,6},{5,7},{6,4},{7,5},{8,10},{9,11},{10,... | collective-permute-start | bytes 786440 | tf_op jit(solution)/shard_map/ppermute | solution.py:359
  41.6 0.0 collective-permute-done.9.refs_3_.refs_7_
  41.6 2.4 %collective-permute-start.14 = (bf16[128,1024]{1,0:T(8,128)(2,1)S(1)}, bf16[128,1024]{1,0:T(8,128)(2,1)S(1)}, u32[]{:S(2)}, u32[]{:S(2)}) collective-permute-start(bf16[128,1024]{1,0:T(8,128)(2,1)S(1)} %slice.39), channel_id=1, source_target_pairs={{0,6},{1,7},{2,4},{3,5},{4,2},{5,3},{6,0},{7,1},{8,14},{9,15},{10,... | collective-permute-start | bytes 786440 | tf_op jit(solution)/shard_map/ppermute | solution.py:360
  44.0 5.4 %weights.4 = (f32[8,128]{1,0:T(8,128)S(1)}, f32[784,1024]{1,0:T(8,128)S(1)}, f32[784,1024]{1,0:T(8,128)S(1)}, f32[2,1024]{1,0:T(2,128)S(1)}) custom-call(s32[7]{0:T(128)S(1)} %stack.31.p, bf16[1568,1024]{1,0:T(8,128)(2,1)S(1)} %copy-done.1, bf16[256,1024]{1,0:T(8,128)(2,1)S(1)} %collective-permute-done.7.refs_1_.refs_5_, ...), custom_call_target="tpu_custom_call" | custom-call | flops 3288334336 | bytes 11749504 | tf_op jit(solution)/shard_map/weights/pallas_call | solution.py:54
  49.4 0.0 collective-permute-done.11.refs_1_
  49.4 0.0 collective-permute-done.12.refs_2_
  49.5 0.0 collective-permute-done.13.refs_3_
  49.5 0.0 collective-permute-done.14.refs_4_
  49.5 3.2 %weights.5 = (bf16[256,1024]{1,0:T(8,128)(2,1)S(1)}, bf16[256,1024]{1,0:T(8,128)(2,1)S(1)}, f32[32,16,128]{2,1,0:T(8,128)S(1)}, f32[784,512]{1,0:T(8,128)S(1)}, ...) custom-call(s32[7]{0:T(128)S(1)} %stack.31.p, bf16[1568,1024]{1,0:T(8,128)(2,1)S(1)} %copy-done.1, ...), custom_call_target="tpu_custom_call" | custom-call | flops 1644167168 | bytes 8798336 | tf_op jit(solution)/shard_map/weights/pallas_call | solution.py:54
  52.7 14.0 %all_to_all.5.refs_11_ = f32[32,16,128]{2,1,0:T(8,128)S(1)} all-to-all(f32[32,16,128]{2,1,0:T(8,128)S(1)} %get-tuple-element.47), channel_id=1, replica_groups=mesh['dp'=4,'cent'=32] {'cent'}, dimensions={0} | all-to-all | bytes 524288 | tf_op jit(solution)/shard_map/all_to_all | solution.py:369
  66.7 5.7 %sums.2 = (f32[784,384]{1,0:T(8,128)S(1)}, f32[784,256]{1,0:T(8,128)S(1)}, f32[784,256]{1,0:T(8,128)}, f32[784,256]{1,0:T(8,128)S(1)}, f32[16,128]{1,0:T(8,128)S(1)}, /*index=5*/f32[8,2048]{1,0:T(8,128)S(1)}) custom-call(s32[7]{0:T(128)S(1)} %stack.31.p, f32[784,512]{1,0:T(8,128)S(1)} %get-tuple-element.44.refs_0_, ...), custom_call_target="tpu_custom_call" | custom-call | flops 3288334336 | bytes 14581760 | tf_op jit(solution)/shard_map/sums/pallas_call | solution.py:54
  72.4 0.0 collective-permute-start.16
  72.4 5.1 %sums.3 = (f32[784,384]{1,0:T(8,128)S(1)}, f32[784,256]{1,0:T(8,128)S(1)}, f32[784,256]{1,0:T(8,128)}, f32[784,256]{1,0:T(8,128)S(1)}) custom-call(s32[7]{0:T(128)S(1)} %stack.31.p, f32[784,512]{1,0:T(8,128)S(1)} %get-tuple-element.36.refs_0_, f32[784,1024]{1,0:T(8,128)S(1)} %get-tuple-element.38.refs_1_, f32[784,512]{1,0:T(8,128)S(1)} %get-tuple-element.41.refs_2_, ...), custom_call_target="tpu_custom_call" | custom-call | flops 3288334336 | bytes 14295040 | tf_op jit(solution)/shard_map/sums/pallas_call | solution.py:54
  77.5 0.5 collective-permute-start.15
  78.0 0.0 collective-permute-start.18
  78.0 0.5 collective-permute-start.17
  78.5 0.0 collective-permute-done.16.refs_3_
  78.5 0.7 pack.2
  79.3 2.9 %collective-permute-done.15.refs_2_ = f32[784,384]{1,0:T(8,128)S(1)} collective-permute-done((f32[784,384]{1,0:T(8,128)S(1)}, f32[784,384]{1,0:T(8,128)S(1)}, u32[]{:S(2)}, u32[]{:S(2)}) %collective-permute-start.15) | collective-permute-done | bytes 1204256 | tf_op jit(solution)/shard_map/ppermute | solution.py:375
  82.2 1.4 %pack.3 = (f32[784,256]{1,0:T(8,128)S(1)}, f32[784,128]{1,0:T(8,128)S(1)}, f32[16,784]{1,0:T(8,128)S(1)}) custom-call(s32[7]{0:T(128)S(1)} %stack.31.p, f32[784,384]{1,0:T(8,128)S(1)} %get-tuple-element.52.refs_0_, f32[784,256]{1,0:T(8,128)S(1)} %get-tuple-element.53.refs_1_, f32[784,384]{1,0:T(8,128)S(1)} %collective-permute-done.15.refs_2_, ...), custom_call_target="tpu_custom_call" | custom-call | bytes 4867072 | tf_op jit(solution)/shard_map/pack/pallas_call | solution.py:54
  83.6 0.8 convert_element_type.14
  84.4 2.9 %collective-permute-start.21 = (f16[784,256]{1,0:T(8,128)(2,1)}, f16[784,256]{1,0:T(8,128)(2,1)}, u32[]{:S(2)}, u32[]{:S(2)}) collective-permute-start(f16[784,256]{1,0:T(8,128)(2,1)} %convert_element_type.14), channel_id=1, source_target_pairs={{0,64},{32,96},{64,0},{96,32},{1,65},{33,97},{65,1},{97,33},{2,66}... | collective-permute-start | bytes 1204232 | tf_op jit(solution)/shard_map/ppermute | solution.py:378
  87.3 0.8 convert_element_type.12
  88.2 0.6 collective-permute-start.20
  88.8 0.1 dynamic-slice_bitcast_fusion.1
  88.9 2.9 %collective-permute-start.19 = (f32[16,784]{1,0:T(8,128)S(1)}, f32[16,784]{1,0:T(8,128)S(1)}, u32[]{:S(2)}, u32[]{:S(2)}) collective-permute-start(f32[16,784]{1,0:T(8,128)S(1)} %get-tuple-element.63), channel_id=1, source_target_pairs={{0,64},{32,96},{64,0},{96,32},{1,65},{33,97},{65,1},{97,33},{2,66}... | collective-permute-start | bytes 150536 | tf_op jit(solution)/shard_map/ppermute | solution.py:379
  91.8 0.6 pad_maximum_fusion.2
  92.4 0.0 collective-permute-done.18.refs_4_
  92.4 0.0 collective-permute-done.17.refs_3_
  92.4 1.9 %copy-done.2 = bf16[1568,1024]{1,0:T(8,128)(2,1)S(1)} copy-done((bf16[1568,1024]{1,0:T(8,128)(2,1)S(1)}, bf16[1568,1024]{1,0:T(8,128)(2,1)}, u32[]{:S(2)}) %copy-start.2) | copy-done | bytes 3211288
  94.3 1.8 %near.1.refs_0_ = f32[1568,256]{1,0:T(8,128)S(1)} custom-call(s32[7]{0:T(128)S(1)} %stack.31.p, f32[784,256]{1,0:T(8,128)S(1)} %get-tuple-element.57.refs_0_, f32[784,256]{1,0:T(8,128)S(1)} %get-tuple-element.58.refs_1_, f32[784,256]{1,0:T(8,128)S(1)} %get-tuple-element.59.refs_2_, f32[784,256]{1,0:T(8,128)} %collective-permute-done.17.refs_3_, ...), custom_call_target="tpu_custom_call" | custom-call | bytes 8028160 | tf_op jit(solution)/shard_map/near/pallas_call | solution.py:54
  96.2 2.2 %collective-permute-done.21 = f16[784,256]{1,0:T(8,128)(2,1)} collective-permute-done((f16[784,256]{1,0:T(8,128)(2,1)}, f16[784,256]{1,0:T(8,128)(2,1)}, u32[]{:S(2)}, u32[]{:S(2)}) %collective-permute-start.21) | collective-permute-done | bytes 401440 | tf_op jit(solution)/shard_map/ppermute | solution.py:378
  98.4 1.1 convert_element_type.15.refs_5_
  99.4 7.5 %collective-permute-done.20 = f16[784,256]{1,0:T(8,128)(2,1)} collective-permute-done((f16[784,256]{1,0:T(8,128)(2,1)}, f16[784,256]{1,0:T(8,128)(2,1)}, u32[]{:S(2)}, u32[]{:S(2)}) %collective-permute-start.20) | collective-permute-done | bytes 401440 | tf_op jit(solution)/shard_map/ppermute | solution.py:378
  107.0 1.1 convert_element_type.13.refs_4_
  108.0 2.6 %fresh.1 = bf16[1568,256]{1,0:T(8,128)(2,1)} custom-call(s32[7]{0:T(128)S(1)} %stack.31.p, f32[1568,256]{1,0:T(8,128)S(1)} %near.1.refs_0_, f32[784,128]{1,0:T(8,128)S(1)} %get-tuple-element.56.refs_3_.refs_1_, f32[784,128]{1,0:T(8,128)S(1)} %get-tuple-element.62.refs_2_, f32[16,784]{1,0:T(8,128)S(1)} %collective-permute-done.19.refs_3_, ...), custom_call_target="tpu_custom_call" | custom-call | bytes 4867072 | tf_op jit(solution)/shard_map/fresh/pallas_call | solution.py:54
  (12 shorter events, 0.1 us)
Async XLA Ops:
  0.6 5.4 %collective-permute-start = (bf16[64,1024]{1,0:T(8,128)(2,1)}, bf16[64,1024]{1,0:T(8,128)(2,1)S(1)}, u32[]{:S(2)}, u32[]{:S(2)}) collective-permute-start(bf16[64,1024]{1,0:T(8,128)(2,1)} %param.2), channel_id=1, source_target_pairs={{0,1},{1,0},{2,3},{3,2},{4,5},{5,4},{6,7},{7,6},{8,9},{9,8},{10,11... | collective-permute-start | bytes 393224 | tf_op jit(solution)/shard_map/ppermute | solution.py:342
  7.0 9.1 %collective-permute-start.3 = (bf16[64,1024]{1,0:T(8,128)(2,1)S(1)}, bf16[64,1024]{1,0:T(8,128)(2,1)S(1)}, u32[]{:S(2)}, u32[]{:S(2)}) collective-permute-start(bf16[64,1024]{1,0:T(8,128)(2,1)S(1)} %pad_maximum_fusion.refs_0_), channel_id=1, source_target_pairs={{0,4},{1,5},{2,6},{3,7},{4,0},{5,1},{6,2},{7,3},{8,12},{9,13},{10,... | collective-permute-start | bytes 393224 | tf_op jit(solution)/shard_map/ppermute | solution.py:350
  10.3 6.2 %collective-permute-start.2 = (bf16[64,1024]{1,0:T(8,128)(2,1)S(1)}, bf16[64,1024]{1,0:T(8,128)(2,1)S(1)}, u32[]{:S(2)}, u32[]{:S(2)}) collective-permute-start(bf16[64,1024]{1,0:T(8,128)(2,1)S(1)} %pad_maximum_fusion.refs_0_), channel_id=1, source_target_pairs={{0,6},{1,7},{2,4},{3,5},{4,2},{5,3},{6,0},{7,1},{8,14},{9,15},{10,... | collective-permute-start | bytes 393224 | tf_op jit(solution)/shard_map/ppermute | solution.py:350
  11.5 5.2 %collective-permute-start.1 = (bf16[64,1024]{1,0:T(8,128)(2,1)S(1)}, bf16[64,1024]{1,0:T(8,128)(2,1)S(1)}, u32[]{:S(2)}, u32[]{:S(2)}) collective-permute-start(bf16[64,1024]{1,0:T(8,128)(2,1)S(1)} %pad_maximum_fusion.refs_0_), channel_id=1, source_target_pairs={{0,2},{1,3},{2,0},{3,1},{4,6},{5,7},{6,4},{7,5},{8,10},{9,11},{10,... | collective-permute-start | bytes 393224 | tf_op jit(solution)/shard_map/ppermute | solution.py:350
  11.5 7.0 %collective-permute-start.6 = (bf16[64,1024]{1,0:T(8,128)(2,1)S(1)}, bf16[64,1024]{1,0:T(8,128)(2,1)S(1)}, u32[]{:S(2)}, u32[]{:S(2)}) collective-permute-start(bf16[64,1024]{1,0:T(8,128)(2,1)S(1)} %pad_maximum_fusion.1.refs_4_), channel_id=1, source_target_pairs={{0,16},{1,17},{2,18},{3,19},{4,20},{5,21},{6,22},{7,23},{8,24},{9,... | collective-permute-start | bytes 393224 | tf_op jit(solution)/shard_map/ppermute | solution.py:351
  15.4 6.2 %collective-permute-start.5 = (bf16[64,1024]{1,0:T(8,128)(2,1)S(1)}, bf16[64,1024]{1,0:T(8,128)(2,1)S(1)}, u32[]{:S(2)}, u32[]{:S(2)}) collective-permute-start(bf16[64,1024]{1,0:T(8,128)(2,1)S(1)} %pad_maximum_fusion.1.refs_4_), channel_id=1, source_target_pairs={{0,24},{1,25},{2,26},{3,27},{4,28},{5,29},{6,30},{7,31},{8,16},{9,... | collective-permute-start | bytes 393224 | tf_op jit(solution)/shard_map/ppermute | solution.py:351
  16.1 5.5 %collective-permute-start.4 = (bf16[64,1024]{1,0:T(8,128)(2,1)S(1)}, bf16[64,1024]{1,0:T(8,128)(2,1)S(1)}, u32[]{:S(2)}, u32[]{:S(2)}) collective-permute-start(bf16[64,1024]{1,0:T(8,128)(2,1)S(1)} %pad_maximum_fusion.1.refs_4_), channel_id=1, source_target_pairs={{0,8},{1,9},{2,10},{3,11},{4,12},{5,13},{6,14},{7,15},{8,0},{9,1},... | collective-permute-start | bytes 393224 | tf_op jit(solution)/shard_map/ppermute | solution.py:351
  22.2 13.1 %collective-permute-start.8 = (bf16[256,1024]{1,0:T(8,128)(2,1)S(1)}, bf16[256,1024]{1,0:T(8,128)(2,1)S(1)}, u32[]{:S(2)}, u32[]{:S(2)}) collective-permute-start(bf16[256,1024]{1,0:T(8,128)(2,1)S(1)} %get-tuple-element.34.refs_1_.refs_3_), channel_id=1, source_target_pairs={{0,24},{1,25},{2,26},{3,27},{4,28},{5,29},{6,30},{7,31},{8,16},{9,... | collective-permute-start | bytes 1572872 | tf_op jit(solution)/shard_map/ppermute | solution.py:354
  24.4 11.2 %collective-permute-start.7 = (bf16[256,1024]{1,0:T(8,128)(2,1)S(1)}, bf16[256,1024]{1,0:T(8,128)(2,1)S(1)}, u32[]{:S(2)}, u32[]{:S(2)}) collective-permute-start(bf16[256,1024]{1,0:T(8,128)(2,1)S(1)} %get-tuple-element.34.refs_1_.refs_3_), channel_id=1, source_target_pairs={{0,8},{1,9},{2,10},{3,11},{4,12},{5,13},{6,14},{7,15},{8,0},{9,1},... | collective-permute-start | bytes 1572872 | tf_op jit(solution)/shard_map/ppermute | solution.py:353
  24.4 13.7 %collective-permute-start.10 = (bf16[256,1024]{1,0:T(8,128)(2,1)S(1)}, bf16[256,1024]{1,0:T(8,128)(2,1)S(1)}, u32[]{:S(2)}, u32[]{:S(2)}) collective-permute-start(bf16[256,1024]{1,0:T(8,128)(2,1)S(1)} %get-tuple-element.35.refs_2_.refs_4_), channel_id=1, source_target_pairs={{0,6},{1,7},{2,4},{3,5},{4,2},{5,3},{6,0},{7,1},{8,14},{9,15},{10,... | collective-permute-start | bytes 1572872 | tf_op jit(solution)/shard_map/ppermute | solution.py:354
  27.6 14.0 %collective-permute-start.9 = (bf16[256,1024]{1,0:T(8,128)(2,1)S(1)}, bf16[256,1024]{1,0:T(8,128)(2,1)S(1)}, u32[]{:S(2)}, u32[]{:S(2)}) collective-permute-start(bf16[256,1024]{1,0:T(8,128)(2,1)S(1)} %get-tuple-element.35.refs_2_.refs_4_), channel_id=1, source_target_pairs={{0,2},{1,3},{2,0},{3,1},{4,6},{5,7},{6,4},{7,5},{8,10},{9,11},{10,... | collective-permute-start | bytes 1572872 | tf_op jit(solution)/shard_map/ppermute | solution.py:353
  27.9 1.9 %copy-start = (bf16[1568,1024]{1,0:T(8,128)(2,1)S(1)}, bf16[1568,1024]{1,0:T(8,128)(2,1)}, u32[]{:S(2)}) copy-start(bf16[1568,1024]{1,0:T(8,128)(2,1)} %refs_5_.1) | copy-start | bytes 9633796
  29.8 14.2 %copy-start.1 = (bf16[1568,1024]{1,0:T(8,128)(2,1)S(1)}, bf16[1568,1024]{1,0:T(8,128)(2,1)}, u32[]{:S(2)}) copy-start(bf16[1568,1024]{1,0:T(8,128)(2,1)} %refs_5_.1) | copy-start | bytes 9633796
  35.4 14.1 %collective-permute-start.11 = (bf16[128,1024]{1,0:T(8,128)(2,1)S(1)}, bf16[128,1024]{1,0:T(8,128)(2,1)S(1)}, u32[]{:S(2)}, u32[]{:S(2)}) collective-permute-start(bf16[128,1024]{1,0:T(8,128)(2,1)S(1)} %slice.36), channel_id=1, source_target_pairs={{0,8},{1,9},{2,10},{3,11},{4,12},{5,13},{6,14},{7,15},{8,0},{9,1},... | collective-permute-start | bytes 786440 | tf_op jit(solution)/shard_map/ppermute | solution.py:357
  35.6 13.8 %collective-permute-start.12 = (bf16[128,1024]{1,0:T(8,128)(2,1)S(1)}, bf16[128,1024]{1,0:T(8,128)(2,1)S(1)}, u32[]{:S(2)}, u32[]{:S(2)}) collective-permute-start(bf16[128,1024]{1,0:T(8,128)(2,1)S(1)} %slice.37), channel_id=1, source_target_pairs={{0,24},{1,25},{2,26},{3,27},{4,28},{5,29},{6,30},{7,31},{8,16},{9,... | collective-permute-start | bytes 786440 | tf_op jit(solution)/shard_map/ppermute | solution.py:358
  38.1 11.3 %collective-permute-start.13 = (bf16[128,1024]{1,0:T(8,128)(2,1)S(1)}, bf16[128,1024]{1,0:T(8,128)(2,1)S(1)}, u32[]{:S(2)}, u32[]{:S(2)}) collective-permute-start(bf16[128,1024]{1,0:T(8,128)(2,1)S(1)} %slice.38), channel_id=1, source_target_pairs={{0,2},{1,3},{2,0},{3,1},{4,6},{5,7},{6,4},{7,5},{8,10},{9,11},{10,... | collective-permute-start | bytes 786440 | tf_op jit(solution)/shard_map/ppermute | solution.py:359
  41.6 7.8 %collective-permute-start.14 = (bf16[128,1024]{1,0:T(8,128)(2,1)S(1)}, bf16[128,1024]{1,0:T(8,128)(2,1)S(1)}, u32[]{:S(2)}, u32[]{:S(2)}) collective-permute-start(bf16[128,1024]{1,0:T(8,128)(2,1)S(1)} %slice.39), channel_id=1, source_target_pairs={{0,6},{1,7},{2,4},{3,5},{4,2},{5,3},{6,0},{7,1},{8,14},{9,15},{10,... | collective-permute-start | bytes 786440 | tf_op jit(solution)/shard_map/ppermute | solution.py:360
  72.4 6.1 %collective-permute-start.16 = (f32[784,384]{1,0:T(8,128)S(1)}, f32[784,384]{1,0:T(8,128)S(1)}, u32[]{:S(2)}, u32[]{:S(2)}) collective-permute-start(f32[784,384]{1,0:T(8,128)S(1)} %get-tuple-element.54.refs_1_), channel_id=1, source_target_pairs={{0,32},{32,0},{64,96},{96,64},{1,33},{33,1},{65,97},{97,65},{2,34}... | collective-permute-start | bytes 3612680 | tf_op jit(solution)/shard_map/ppermute | solution.py:374
  77.5 4.7 %collective-permute-start.15 = (f32[784,384]{1,0:T(8,128)S(1)}, f32[784,384]{1,0:T(8,128)S(1)}, u32[]{:S(2)}, u32[]{:S(2)}) collective-permute-start(f32[784,384]{1,0:T(8,128)S(1)} %get-tuple-element.52.refs_0_), channel_id=1, source_target_pairs={{0,32},{32,0},{64,96},{96,64},{1,33},{33,1},{65,97},{97,65},{2,34}... | collective-permute-start | bytes 3612680 | tf_op jit(solution)/shard_map/ppermute | solution.py:375
  78.0 14.4 %collective-permute-start.18 = (f32[784,256]{1,0:T(8,128)}, f32[784,256]{1,0:T(8,128)}, u32[]{:S(2)}, u32[]{:S(2)}) collective-permute-start(f32[784,256]{1,0:T(8,128)} %get-tuple-element.61), channel_id=1, source_target_pairs={{0,32},{32,0},{64,96},{96,64},{1,33},{33,1},{65,97},{97,65},{2,34}... | collective-permute-start | bytes 2408456 | tf_op jit(solution)/shard_map/ppermute | solution.py:381
  78.0 14.4 %collective-permute-start.17 = (f32[784,256]{1,0:T(8,128)}, f32[784,256]{1,0:T(8,128)}, u32[]{:S(2)}, u32[]{:S(2)}) collective-permute-start(f32[784,256]{1,0:T(8,128)} %get-tuple-element.60), channel_id=1, source_target_pairs={{0,32},{32,0},{64,96},{96,64},{1,33},{33,1},{65,97},{97,65},{2,34}... | collective-permute-start | bytes 2408456 | tf_op jit(solution)/shard_map/ppermute | solution.py:381
  84.4 13.9 %collective-permute-start.21 = (f16[784,256]{1,0:T(8,128)(2,1)}, f16[784,256]{1,0:T(8,128)(2,1)}, u32[]{:S(2)}, u32[]{:S(2)}) collective-permute-start(f16[784,256]{1,0:T(8,128)(2,1)} %convert_element_type.14), channel_id=1, source_target_pairs={{0,64},{32,96},{64,0},{96,32},{1,65},{33,97},{65,1},{97,33},{2,66}... | collective-permute-start | bytes 1204232 | tf_op jit(solution)/shard_map/ppermute | solution.py:378
  88.2 18.8 %collective-permute-start.20 = (f16[784,256]{1,0:T(8,128)(2,1)}, f16[784,256]{1,0:T(8,128)(2,1)}, u32[]{:S(2)}, u32[]{:S(2)}) collective-permute-start(f16[784,256]{1,0:T(8,128)(2,1)} %convert_element_type.12), channel_id=1, source_target_pairs={{0,64},{32,96},{64,0},{96,32},{1,65},{33,97},{65,1},{97,33},{2,66}... | collective-permute-start | bytes 1204232 | tf_op jit(solution)/shard_map/ppermute | solution.py:378
  88.9 19.1 %collective-permute-start.19 = (f32[16,784]{1,0:T(8,128)S(1)}, f32[16,784]{1,0:T(8,128)S(1)}, u32[]{:S(2)}, u32[]{:S(2)}) collective-permute-start(f32[16,784]{1,0:T(8,128)S(1)} %get-tuple-element.63), channel_id=1, source_target_pairs={{0,64},{32,96},{64,0},{96,32},{1,65},{33,97},{65,1},{97,33},{2,66}... | collective-permute-start | bytes 150536 | tf_op jit(solution)/shard_map/ppermute | solution.py:379
  92.4 1.9 %copy-start.2 = (bf16[1568,1024]{1,0:T(8,128)(2,1)S(1)}, bf16[1568,1024]{1,0:T(8,128)(2,1)}, u32[]{:S(2)}) copy-start(bf16[1568,1024]{1,0:T(8,128)(2,1)} %refs_5_.1) | copy-start | bytes 9633796

commit v5 on v4

--- a/solution.py
+++ b/solution.py
@@ -374,8 +374,10 @@
     got0 = lax.ppermute(sums0[0], "dp", TO_CORE)
     got1 = lax.ppermute(sums1[0], "dp", TO_CORE)
     packed0, counts0 = pack(pos, sums0[0], sums0[1], got0, (sums1[0],))
-    packed1, counts1, row = pack(pos, sums1[0], sums1[1], got1, (), (counts0,))
-    far = [lax.ppermute(p.astype(jnp.float16), "dp", TO_Y) for p in (packed0, packed1)]
+    moved0 = lax.optimization_barrier(packed0.astype(jnp.float16))
+    after = (moved0[:8, :128].astype(jnp.float32),)
+    packed1, counts1, row = pack(pos, sums1[0], sums1[1], got1, after, (counts0,))
+    far = [lax.ppermute(m, "dp", TO_Y) for m in (moved0, packed1.astype(jnp.float16))]
     far_row = lax.ppermute(row, "dp", TO_Y)
 
     near_got = [lax.ppermute(s[2], "dp", TO_CORE) for s in (sums0, sums1)]

time: 111 us -> 111 us (level)
    ppermute x1, waiting for transfers between devices: 2.94 us -> 1.43 us  [on_device(): got1 = lax.ppermute(sums1[0], 'dp', TO_CORE)]
    convert_element_type x2 -> x3, other arithmetic: 1.69 us -> 2.36 us  [the longest x1 0.84 us: on_device(): packed1.astype(jnp.float16)]
  transfers between devices with their start and end apart: 22 -> 22, of which waited for: 9 -> 9; matrix products, arithmetic and copies ran while one was open for 4% -> 5% of each run, Pallas kernels for 16% -> 16%
where the time goes in v5:
time: 111 us
  starting transfers between devices  32.6 us (29%)
  Pallas kernels  30.2 us (27%)
  waiting for transfers between devices  23 us (21%)
  blocking collectives  14 us (13%)
  other arithmetic  5.99 us (5%)
  local copies, waits for them, and re-layouts  4.07 us (4%)
    pallas_call x10, Pallas kernels, call(): pl.pallas_call(lambda p, *refs: body(p, *refs[n:]), in_specs=[IN_SMEM] +...  30.2 us
    all_to_all x1, blocking collectives, on_device(): every = lax.all_to_all(stats, 'cent', 0, 0)  14 us
    ppermute x2, waiting for transfers between devices, on_device(): lax.ppermute(m, 'dp', TO_Y)  10.6 us
    ppermute x3, starting transfers between devices, on_device(): lax.ppermute(b, 'cent', from_z(d))  4.98 us
    ppermute x3, waiting for transfers between devices, on_device(): lax.ppermute(b, 'cent', from_z(d))  4.95 us
    ppermute x3, starting transfers between devices, on_device(): lax.ppermute(a, 'cent', from_x(d))  4.41 us
    unnamed x6, local copies, waits for them, and re-layouts  3.82 us
    ppermute x1, waiting for transfers between devices, on_device(): other = lax.ppermute(points, 'cent', FROM_PAIR)  3.71 us
  transfers between devices with their start and end apart: 22, of which 9 were waited for; matrix products, arithmetic and copies ran while one was open for 5% of the time, Pallas kernels for 16%

profile of v5, /device:TPU:0, one launch (start us, length us, event | category | flops | bytes accessed | tf_op | source)
XLA Modules:
  0.0 110.9 jit_solution(114371994051920625)
XLA Ops:
  0.6 1.7 %collective-permute-start = (bf16[64,1024]{1,0:T(8,128)(2,1)}, bf16[64,1024]{1,0:T(8,128)(2,1)S(1)}, u32[]{:S(2)}, u32[]{:S(2)}) collective-permute-start(bf16[64,1024]{1,0:T(8,128)(2,1)} %param.2), channel_id=1, source_target_pairs={{0,1},{1,0},{2,3},{3,2},{4,5},{5,4},{6,7},{7,6},{8,9},{9,8},{10,11... | collective-permute-start | bytes 393224 | tf_op jit(solution)/shard_map/ppermute | solution.py:342
  2.4 3.7 %collective-permute-done = bf16[64,1024]{1,0:T(8,128)(2,1)S(1)} collective-permute-done((bf16[64,1024]{1,0:T(8,128)(2,1)}, bf16[64,1024]{1,0:T(8,128)(2,1)S(1)}, u32[]{:S(2)}, u32[]{:S(2)}) %collective-permute-start) | collective-permute-done | bytes 131104 | tf_op jit(solution)/shard_map/ppermute | solution.py:342
  6.1 0.9 broadcast_select_fusion.1
  7.0 3.3 %collective-permute-start.3 = (bf16[64,1024]{1,0:T(8,128)(2,1)S(1)}, bf16[64,1024]{1,0:T(8,128)(2,1)S(1)}, u32[]{:S(2)}, u32[]{:S(2)}) collective-permute-start(bf16[64,1024]{1,0:T(8,128)(2,1)S(1)} %pad_maximum_fusion.refs_0_), channel_id=1, source_target_pairs={{0,4},{1,5},{2,6},{3,7},{4,0},{5,1},{6,2},{7,3},{8,12},{9,13},{10,... | collective-permute-start | bytes 393224 | tf_op jit(solution)/shard_map/ppermute | solution.py:350
  10.3 1.1 %collective-permute-start.2 = (bf16[64,1024]{1,0:T(8,128)(2,1)S(1)}, bf16[64,1024]{1,0:T(8,128)(2,1)S(1)}, u32[]{:S(2)}, u32[]{:S(2)}) collective-permute-start(bf16[64,1024]{1,0:T(8,128)(2,1)S(1)} %pad_maximum_fusion.refs_0_), channel_id=1, source_target_pairs={{0,6},{1,7},{2,4},{3,5},{4,2},{5,3},{6,0},{7,1},{8,14},{9,15},{10,... | collective-permute-start | bytes 393224 | tf_op jit(solution)/shard_map/ppermute | solution.py:350
  11.5 0.0 collective-permute-start.1
  11.5 4.0 %collective-permute-start.6 = (bf16[64,1024]{1,0:T(8,128)(2,1)S(1)}, bf16[64,1024]{1,0:T(8,128)(2,1)S(1)}, u32[]{:S(2)}, u32[]{:S(2)}) collective-permute-start(bf16[64,1024]{1,0:T(8,128)(2,1)S(1)} %pad_maximum_fusion.1.refs_4_), channel_id=1, source_target_pairs={{0,16},{1,17},{2,18},{3,19},{4,20},{5,21},{6,22},{7,23},{8,24},{9,... | collective-permute-start | bytes 393224 | tf_op jit(solution)/shard_map/ppermute | solution.py:351
  15.4 0.7 collective-permute-start.5
  16.1 0.0 collective-permute-done.3.refs_3_
  16.1 0.3 collective-permute-start.4
  16.5 0.1 stack.31.p
  16.5 0.0 collective-permute-done.2.refs_2_
  16.5 0.1 collective-permute-done.1.refs_1_
  16.7 1.8 %collective-permute-done.6.refs_7_ = bf16[64,1024]{1,0:T(8,128)(2,1)S(1)} collective-permute-done((bf16[64,1024]{1,0:T(8,128)(2,1)S(1)}, bf16[64,1024]{1,0:T(8,128)(2,1)S(1)}, u32[]{:S(2)}, u32[]{:S(2)}) %collective-permute-start.6) | collective-permute-done | bytes 131104 | tf_op jit(solution)/shard_map/ppermute | solution.py:351
  18.5 3.1 %collective-permute-done.5.refs_6_ = bf16[64,1024]{1,0:T(8,128)(2,1)S(1)} collective-permute-done((bf16[64,1024]{1,0:T(8,128)(2,1)S(1)}, bf16[64,1024]{1,0:T(8,128)(2,1)S(1)}, u32[]{:S(2)}, u32[]{:S(2)}) %collective-permute-start.5) | collective-permute-done | bytes 131104 | tf_op jit(solution)/shard_map/ppermute | solution.py:351
  21.6 0.0 collective-permute-done.4.refs_5_
  21.6 0.6 join.1
  22.2 2.2 %collective-permute-start.8 = (bf16[256,1024]{1,0:T(8,128)(2,1)S(1)}, bf16[256,1024]{1,0:T(8,128)(2,1)S(1)}, u32[]{:S(2)}, u32[]{:S(2)}) collective-permute-start(bf16[256,1024]{1,0:T(8,128)(2,1)S(1)} %get-tuple-element.34.refs_1_.refs_3_), channel_id=1, source_target_pairs={{0,24},{1,25},{2,26},{3,27},{4,28},{5,29},{6,30},{7,31},{8,16},{9,... | collective-permute-start | bytes 1572872 | tf_op jit(solution)/shard_map/ppermute | solution.py:354
  24.4 0.0 collective-permute-start.7
  24.4 3.2 %collective-permute-start.10 = (bf16[256,1024]{1,0:T(8,128)(2,1)S(1)}, bf16[256,1024]{1,0:T(8,128)(2,1)S(1)}, u32[]{:S(2)}, u32[]{:S(2)}) collective-permute-start(bf16[256,1024]{1,0:T(8,128)(2,1)S(1)} %get-tuple-element.35.refs_2_.refs_4_), channel_id=1, source_target_pairs={{0,6},{1,7},{2,4},{3,5},{4,2},{5,3},{6,0},{7,1},{8,14},{9,15},{10,... | collective-permute-start | bytes 1572872 | tf_op jit(solution)/shard_map/ppermute | solution.py:354
  27.6 0.2 collective-permute-start.9
  27.9 1.9 %copy-done = bf16[1568,1024]{1,0:T(8,128)(2,1)S(1)} copy-done((bf16[1568,1024]{1,0:T(8,128)(2,1)S(1)}, bf16[1568,1024]{1,0:T(8,128)(2,1)}, u32[]{:S(2)}) %copy-start) | copy-done | bytes 3211288
  29.8 3.5 %weights.3 = (f32[4,128]{1,0:T(4,128)S(1)}, f32[1568,1]{1,0:T(8,128)S(1)}, f32[784,512]{1,0:T(8,128)S(1)}, f32[784,512]{1,0:T(8,128)S(1)}, f32[2,512]{1,0:T(2,128)S(1)}) custom-call(s32[7]{0:T(128)S(1)} %stack.31.p, bf16[1568,1024]{1,0:T(8,128)(2,1)S(1)} %copy-done, bf16[256,1024]{1,0:T(8,128)(2,1)S(1)} %get-tuple-element.34.refs_1_.refs_3_, ...), custom_call_target="tpu_custom_call" | custom-call | flops 1644167168 | bytes 7483520 | tf_op jit(solution)/shard_map/weights/pallas_call | solution.py:54
  33.3 2.0 %collective-permute-done.8.refs_2_.refs_6_ = bf16[256,1024]{1,0:T(8,128)(2,1)S(1)} collective-permute-done((bf16[256,1024]{1,0:T(8,128)(2,1)S(1)}, bf16[256,1024]{1,0:T(8,128)(2,1)S(1)}, u32[]{:S(2)}, u32[]{:S(2)}) %collective-permute-start.8) | collective-permute-done | bytes 524320 | tf_op jit(solution)/shard_map/ppermute | solution.py:354
  35.4 0.1 collective-permute-start.11
  35.5 0.2 collective-permute-done.7.refs_1_.refs_5_
  35.6 2.5 %collective-permute-start.12 = (bf16[128,1024]{1,0:T(8,128)(2,1)S(1)}, bf16[128,1024]{1,0:T(8,128)(2,1)S(1)}, u32[]{:S(2)}, u32[]{:S(2)}) collective-permute-start(bf16[128,1024]{1,0:T(8,128)(2,1)S(1)} %slice.41), channel_id=1, source_target_pairs={{0,24},{1,25},{2,26},{3,27},{4,28},{5,29},{6,30},{7,31},{8,16},{9,... | collective-permute-start | bytes 786440 | tf_op jit(solution)/shard_map/ppermute | solution.py:358
  38.1 0.0 collective-permute-done.10.refs_4_.refs_8_
  38.1 3.5 %collective-permute-start.13 = (bf16[128,1024]{1,0:T(8,128)(2,1)S(1)}, bf16[128,1024]{1,0:T(8,128)(2,1)S(1)}, u32[]{:S(2)}, u32[]{:S(2)}) collective-permute-start(bf16[128,1024]{1,0:T(8,128)(2,1)S(1)} %slice.42), channel_id=1, source_target_pairs={{0,2},{1,3},{2,0},{3,1},{4,6},{5,7},{6,4},{7,5},{8,10},{9,11},{10,... | collective-permute-start | bytes 786440 | tf_op jit(solution)/shard_map/ppermute | solution.py:359
  41.6 0.0 collective-permute-done.9.refs_3_.refs_7_
  41.6 2.4 %collective-permute-start.14 = (bf16[128,1024]{1,0:T(8,128)(2,1)S(1)}, bf16[128,1024]{1,0:T(8,128)(2,1)S(1)}, u32[]{:S(2)}, u32[]{:S(2)}) collective-permute-start(bf16[128,1024]{1,0:T(8,128)(2,1)S(1)} %slice.43), channel_id=1, source_target_pairs={{0,6},{1,7},{2,4},{3,5},{4,2},{5,3},{6,0},{7,1},{8,14},{9,15},{10,... | collective-permute-start | bytes 786440 | tf_op jit(solution)/shard_map/ppermute | solution.py:360
  44.0 5.4 %weights.4 = (f32[8,128]{1,0:T(8,128)S(1)}, f32[784,1024]{1,0:T(8,128)S(1)}, f32[784,1024]{1,0:T(8,128)S(1)}, f32[2,1024]{1,0:T(2,128)S(1)}) custom-call(s32[7]{0:T(128)S(1)} %stack.31.p, bf16[1568,1024]{1,0:T(8,128)(2,1)S(1)} %copy-done.1, bf16[256,1024]{1,0:T(8,128)(2,1)S(1)} %collective-permute-done.7.refs_1_.refs_5_, ...), custom_call_target="tpu_custom_call" | custom-call | flops 3288334336 | bytes 11749504 | tf_op jit(solution)/shard_map/weights/pallas_call | solution.py:54
  49.4 0.0 collective-permute-done.11.refs_1_
  49.4 0.0 collective-permute-done.12.refs_2_
  49.5 0.0 collective-permute-done.13.refs_3_
  49.5 0.0 collective-permute-done.14.refs_4_
  49.5 3.2 %weights.5 = (bf16[256,1024]{1,0:T(8,128)(2,1)S(1)}, bf16[256,1024]{1,0:T(8,128)(2,1)S(1)}, f32[32,16,128]{2,1,0:T(8,128)S(1)}, f32[784,512]{1,0:T(8,128)S(1)}, ...) custom-call(s32[7]{0:T(128)S(1)} %stack.31.p, bf16[1568,1024]{1,0:T(8,128)(2,1)S(1)} %copy-done.1, ...), custom_call_target="tpu_custom_call" | custom-call | flops 1644167168 | bytes 8798336 | tf_op jit(solution)/shard_map/weights/pallas_call | solution.py:54
  52.7 14.0 %all_to_all.5.refs_11_ = f32[32,16,128]{2,1,0:T(8,128)S(1)} all-to-all(f32[32,16,128]{2,1,0:T(8,128)S(1)} %get-tuple-element.47), channel_id=1, replica_groups=mesh['dp'=4,'cent'=32] {'cent'}, dimensions={0} | all-to-all | bytes 524288 | tf_op jit(solution)/shard_map/all_to_all | solution.py:369
  66.7 5.7 %sums.2 = (f32[784,384]{1,0:T(8,128)S(1)}, f32[784,256]{1,0:T(8,128)S(1)}, f32[784,256]{1,0:T(8,128)}, f32[784,256]{1,0:T(8,128)S(1)}, f32[16,128]{1,0:T(8,128)S(1)}, /*index=5*/f32[8,2048]{1,0:T(8,128)S(1)}) custom-call(s32[7]{0:T(128)S(1)} %stack.31.p, f32[784,512]{1,0:T(8,128)S(1)} %get-tuple-element.44.refs_0_, ...), custom_call_target="tpu_custom_call" | custom-call | flops 3288334336 | bytes 14581760 | tf_op jit(solution)/shard_map/sums/pallas_call | solution.py:54
  72.4 0.0 collective-permute-start.15
  72.4 5.1 %sums.3 = (f32[784,384]{1,0:T(8,128)S(1)}, f32[784,256]{1,0:T(8,128)S(1)}, f32[784,256]{1,0:T(8,128)}, f32[784,256]{1,0:T(8,128)S(1)}) custom-call(s32[7]{0:T(128)S(1)} %stack.31.p, f32[784,512]{1,0:T(8,128)S(1)} %get-tuple-element.36.refs_0_, f32[784,1024]{1,0:T(8,128)S(1)} %get-tuple-element.38.refs_1_, f32[784,512]{1,0:T(8,128)S(1)} %get-tuple-element.41.refs_2_, ...), custom_call_target="tpu_custom_call" | custom-call | flops 3288334336 | bytes 14295040 | tf_op jit(solution)/shard_map/sums/pallas_call | solution.py:54
  77.5 0.5 collective-permute-start.16
  78.0 0.0 collective-permute-start.18
  78.0 0.5 collective-permute-start.17
  78.5 0.0 collective-permute-done.15.refs_3_
  78.5 0.7 pack.2
  79.3 0.8 convert_element_type.15
  80.1 0.7 slice_convert_fusion.refs_0_
  80.8 1.4 %collective-permute-done.16.refs_3_ = f32[784,384]{1,0:T(8,128)S(1)} collective-permute-done((f32[784,384]{1,0:T(8,128)S(1)}, f32[784,384]{1,0:T(8,128)S(1)}, u32[]{:S(2)}, u32[]{:S(2)}) %collective-permute-start.16) | collective-permute-done | bytes 1204256 | tf_op jit(solution)/shard_map/ppermute | solution.py:375
  82.2 1.4 %pack.3 = (f32[784,256]{1,0:T(8,128)S(1)}, f32[784,128]{1,0:T(8,128)S(1)}, f32[16,784]{1,0:T(8,128)S(1)}) custom-call(s32[7]{0:T(128)S(1)} %stack.31.p, f32[8,128]{1,0:T(8,128)S(1)} %slice_convert_fusion.refs_0_, f32[784,384]{1,0:T(8,128)S(1)} %get-tuple-element.52.refs_0_.refs_1_, f32[784,256]{1,0:T(8,128)S(1)} %get-tuple-element.56.refs_2_, ...), custom_call_target="tpu_custom_call" | custom-call | bytes 4867072 | tf_op jit(solution)/shard_map/pack/pallas_call | solution.py:54
  83.6 0.8 convert_element_type.18
  84.5 2.9 %collective-permute-start.21 = (f16[784,256]{1,0:T(8,128)(2,1)}, f16[784,256]{1,0:T(8,128)(2,1)}, u32[]{:S(2)}, u32[]{:S(2)}) collective-permute-start(f16[784,256]{1,0:T(8,128)(2,1)} %convert_element_type.18), channel_id=1, source_target_pairs={{0,64},{32,96},{64,0},{96,32},{1,65},{33,97},{65,1},{97,33},{2,66}... | collective-permute-start | bytes 1204232 | tf_op jit(solution)/shard_map/ppermute | solution.py:380
  87.4 0.6 collective-permute-start.20
  88.0 0.1 dynamic-slice_bitcast_fusion.1
  88.1 2.9 %collective-permute-start.19 = (f32[16,784]{1,0:T(8,128)S(1)}, f32[16,784]{1,0:T(8,128)S(1)}, u32[]{:S(2)}, u32[]{:S(2)}) collective-permute-start(f32[16,784]{1,0:T(8,128)S(1)} %get-tuple-element.64), channel_id=1, source_target_pairs={{0,64},{32,96},{64,0},{96,32},{1,65},{33,97},{65,1},{97,33},{2,66}... | collective-permute-start | bytes 150536 | tf_op jit(solution)/shard_map/ppermute | solution.py:381
  91.0 0.6 pad_maximum_fusion.2
  91.6 0.0 collective-permute-done.18.refs_4_
  91.6 1.9 %copy-done.2 = bf16[1568,1024]{1,0:T(8,128)(2,1)S(1)} copy-done((bf16[1568,1024]{1,0:T(8,128)(2,1)S(1)}, bf16[1568,1024]{1,0:T(8,128)(2,1)}, u32[]{:S(2)}) %copy-start.2) | copy-done | bytes 3211288
  93.5 1.8 %near.1.refs_0_ = f32[1568,256]{1,0:T(8,128)S(1)} custom-call(s32[7]{0:T(128)S(1)} %stack.31.p, f32[784,256]{1,0:T(8,128)S(1)} %get-tuple-element.58.refs_0_, f32[784,256]{1,0:T(8,128)S(1)} %get-tuple-element.59.refs_1_, f32[784,256]{1,0:T(8,128)S(1)} %get-tuple-element.60.refs_2_, f32[784,256]{1,0:T(8,128)} %collective-permute-done.17.refs_3_, ...), custom_call_target="tpu_custom_call" | custom-call | bytes 8028160 | tf_op jit(solution)/shard_map/near/pallas_call | solution.py:54
  95.3 3.1 %collective-permute-done.21 = f16[784,256]{1,0:T(8,128)(2,1)} collective-permute-done((f16[784,256]{1,0:T(8,128)(2,1)}, f16[784,256]{1,0:T(8,128)(2,1)}, u32[]{:S(2)}, u32[]{:S(2)}) %collective-permute-start.21) | collective-permute-done | bytes 401440 | tf_op jit(solution)/shard_map/ppermute | solution.py:380
  98.4 1.1 convert_element_type.19.refs_5_
  99.5 7.5 %collective-permute-done.20 = f16[784,256]{1,0:T(8,128)(2,1)} collective-permute-done((f16[784,256]{1,0:T(8,128)(2,1)}, f16[784,256]{1,0:T(8,128)(2,1)}, u32[]{:S(2)}, u32[]{:S(2)}) %collective-permute-start.20) | collective-permute-done | bytes 401440 | tf_op jit(solution)/shard_map/ppermute | solution.py:380
  107.0 1.1 convert_element_type.17.refs_4_
  108.1 2.6 %fresh.1 = bf16[1568,256]{1,0:T(8,128)(2,1)} custom-call(s32[7]{0:T(128)S(1)} %stack.31.p, f32[1568,256]{1,0:T(8,128)S(1)} %near.1.refs_0_, f32[784,128]{1,0:T(8,128)S(1)} %get-tuple-element.57.refs_4_.refs_1_, f32[784,128]{1,0:T(8,128)S(1)} %get-tuple-element.63.refs_2_, f32[16,784]{1,0:T(8,128)S(1)} %collective-permute-done.19.refs_3_, ...), custom_call_target="tpu_custom_call" | custom-call | bytes 4867072 | tf_op jit(solution)/shard_map/fresh/pallas_call | solution.py:54
  (13 shorter events, 0.1 us)
Async XLA Ops:
  0.6 5.4 %collective-permute-start = (bf16[64,1024]{1,0:T(8,128)(2,1)}, bf16[64,1024]{1,0:T(8,128)(2,1)S(1)}, u32[]{:S(2)}, u32[]{:S(2)}) collective-permute-start(bf16[64,1024]{1,0:T(8,128)(2,1)} %param.2), channel_id=1, source_target_pairs={{0,1},{1,0},{2,3},{3,2},{4,5},{5,4},{6,7},{7,6},{8,9},{9,8},{10,11... | collective-permute-start | bytes 393224 | tf_op jit(solution)/shard_map/ppermute | solution.py:342
  7.0 9.1 %collective-permute-start.3 = (bf16[64,1024]{1,0:T(8,128)(2,1)S(1)}, bf16[64,1024]{1,0:T(8,128)(2,1)S(1)}, u32[]{:S(2)}, u32[]{:S(2)}) collective-permute-start(bf16[64,1024]{1,0:T(8,128)(2,1)S(1)} %pad_maximum_fusion.refs_0_), channel_id=1, source_target_pairs={{0,4},{1,5},{2,6},{3,7},{4,0},{5,1},{6,2},{7,3},{8,12},{9,13},{10,... | collective-permute-start | bytes 393224 | tf_op jit(solution)/shard_map/ppermute | solution.py:350
  10.3 6.2 %collective-permute-start.2 = (bf16[64,1024]{1,0:T(8,128)(2,1)S(1)}, bf16[64,1024]{1,0:T(8,128)(2,1)S(1)}, u32[]{:S(2)}, u32[]{:S(2)}) collective-permute-start(bf16[64,1024]{1,0:T(8,128)(2,1)S(1)} %pad_maximum_fusion.refs_0_), channel_id=1, source_target_pairs={{0,6},{1,7},{2,4},{3,5},{4,2},{5,3},{6,0},{7,1},{8,14},{9,15},{10,... | collective-permute-start | bytes 393224 | tf_op jit(solution)/shard_map/ppermute | solution.py:350
  11.5 5.2 %collective-permute-start.1 = (bf16[64,1024]{1,0:T(8,128)(2,1)S(1)}, bf16[64,1024]{1,0:T(8,128)(2,1)S(1)}, u32[]{:S(2)}, u32[]{:S(2)}) collective-permute-start(bf16[64,1024]{1,0:T(8,128)(2,1)S(1)} %pad_maximum_fusion.refs_0_), channel_id=1, source_target_pairs={{0,2},{1,3},{2,0},{3,1},{4,6},{5,7},{6,4},{7,5},{8,10},{9,11},{10,... | collective-permute-start | bytes 393224 | tf_op jit(solution)/shard_map/ppermute | solution.py:350
  11.5 7.0 %collective-permute-start.6 = (bf16[64,1024]{1,0:T(8,128)(2,1)S(1)}, bf16[64,1024]{1,0:T(8,128)(2,1)S(1)}, u32[]{:S(2)}, u32[]{:S(2)}) collective-permute-start(bf16[64,1024]{1,0:T(8,128)(2,1)S(1)} %pad_maximum_fusion.1.refs_4_), channel_id=1, source_target_pairs={{0,16},{1,17},{2,18},{3,19},{4,20},{5,21},{6,22},{7,23},{8,24},{9,... | collective-permute-start | bytes 393224 | tf_op jit(solution)/shard_map/ppermute | solution.py:351
  15.4 6.2 %collective-permute-start.5 = (bf16[64,1024]{1,0:T(8,128)(2,1)S(1)}, bf16[64,1024]{1,0:T(8,128)(2,1)S(1)}, u32[]{:S(2)}, u32[]{:S(2)}) collective-permute-start(bf16[64,1024]{1,0:T(8,128)(2,1)S(1)} %pad_maximum_fusion.1.refs_4_), channel_id=1, source_target_pairs={{0,24},{1,25},{2,26},{3,27},{4,28},{5,29},{6,30},{7,31},{8,16},{9,... | collective-permute-start | bytes 393224 | tf_op jit(solution)/shard_map/ppermute | solution.py:351
  16.1 5.5 %collective-permute-start.4 = (bf16[64,1024]{1,0:T(8,128)(2,1)S(1)}, bf16[64,1024]{1,0:T(8,128)(2,1)S(1)}, u32[]{:S(2)}, u32[]{:S(2)}) collective-permute-start(bf16[64,1024]{1,0:T(8,128)(2,1)S(1)} %pad_maximum_fusion.1.refs_4_), channel_id=1, source_target_pairs={{0,8},{1,9},{2,10},{3,11},{4,12},{5,13},{6,14},{7,15},{8,0},{9,1},... | collective-permute-start | bytes 393224 | tf_op jit(solution)/shard_map/ppermute | solution.py:351
  22.2 13.1 %collective-permute-start.8 = (bf16[256,1024]{1,0:T(8,128)(2,1)S(1)}, bf16[256,1024]{1,0:T(8,128)(2,1)S(1)}, u32[]{:S(2)}, u32[]{:S(2)}) collective-permute-start(bf16[256,1024]{1,0:T(8,128)(2,1)S(1)} %get-tuple-element.34.refs_1_.refs_3_), channel_id=1, source_target_pairs={{0,24},{1,25},{2,26},{3,27},{4,28},{5,29},{6,30},{7,31},{8,16},{9,... | collective-permute-start | bytes 1572872 | tf_op jit(solution)/shard_map/ppermute | solution.py:354
  24.4 11.2 %collective-permute-start.7 = (bf16[256,1024]{1,0:T(8,128)(2,1)S(1)}, bf16[256,1024]{1,0:T(8,128)(2,1)S(1)}, u32[]{:S(2)}, u32[]{:S(2)}) collective-permute-start(bf16[256,1024]{1,0:T(8,128)(2,1)S(1)} %get-tuple-element.34.refs_1_.refs_3_), channel_id=1, source_target_pairs={{0,8},{1,9},{2,10},{3,11},{4,12},{5,13},{6,14},{7,15},{8,0},{9,1},... | collective-permute-start | bytes 1572872 | tf_op jit(solution)/shard_map/ppermute | solution.py:353
  24.4 13.7 %collective-permute-start.10 = (bf16[256,1024]{1,0:T(8,128)(2,1)S(1)}, bf16[256,1024]{1,0:T(8,128)(2,1)S(1)}, u32[]{:S(2)}, u32[]{:S(2)}) collective-permute-start(bf16[256,1024]{1,0:T(8,128)(2,1)S(1)} %get-tuple-element.35.refs_2_.refs_4_), channel_id=1, source_target_pairs={{0,6},{1,7},{2,4},{3,5},{4,2},{5,3},{6,0},{7,1},{8,14},{9,15},{10,... | collective-permute-start | bytes 1572872 | tf_op jit(solution)/shard_map/ppermute | solution.py:354
  27.6 14.0 %collective-permute-start.9 = (bf16[256,1024]{1,0:T(8,128)(2,1)S(1)}, bf16[256,1024]{1,0:T(8,128)(2,1)S(1)}, u32[]{:S(2)}, u32[]{:S(2)}) collective-permute-start(bf16[256,1024]{1,0:T(8,128)(2,1)S(1)} %get-tuple-element.35.refs_2_.refs_4_), channel_id=1, source_target_pairs={{0,2},{1,3},{2,0},{3,1},{4,6},{5,7},{6,4},{7,5},{8,10},{9,11},{10,... | collective-permute-start | bytes 1572872 | tf_op jit(solution)/shard_map/ppermute | solution.py:353
  27.9 1.9 %copy-start = (bf16[1568,1024]{1,0:T(8,128)(2,1)S(1)}, bf16[1568,1024]{1,0:T(8,128)(2,1)}, u32[]{:S(2)}) copy-start(bf16[1568,1024]{1,0:T(8,128)(2,1)} %refs_5_.1) | copy-start | bytes 9633796
  29.8 14.2 %copy-start.1 = (bf16[1568,1024]{1,0:T(8,128)(2,1)S(1)}, bf16[1568,1024]{1,0:T(8,128)(2,1)}, u32[]{:S(2)}) copy-start(bf16[1568,1024]{1,0:T(8,128)(2,1)} %refs_5_.1) | copy-start | bytes 9633796
  35.4 14.1 %collective-permute-start.11 = (bf16[128,1024]{1,0:T(8,128)(2,1)S(1)}, bf16[128,1024]{1,0:T(8,128)(2,1)S(1)}, u32[]{:S(2)}, u32[]{:S(2)}) collective-permute-start(bf16[128,1024]{1,0:T(8,128)(2,1)S(1)} %slice.40), channel_id=1, source_target_pairs={{0,8},{1,9},{2,10},{3,11},{4,12},{5,13},{6,14},{7,15},{8,0},{9,1},... | collective-permute-start | bytes 786440 | tf_op jit(solution)/shard_map/ppermute | solution.py:357
  35.6 13.8 %collective-permute-start.12 = (bf16[128,1024]{1,0:T(8,128)(2,1)S(1)}, bf16[128,1024]{1,0:T(8,128)(2,1)S(1)}, u32[]{:S(2)}, u32[]{:S(2)}) collective-permute-start(bf16[128,1024]{1,0:T(8,128)(2,1)S(1)} %slice.41), channel_id=1, source_target_pairs={{0,24},{1,25},{2,26},{3,27},{4,28},{5,29},{6,30},{7,31},{8,16},{9,... | collective-permute-start | bytes 786440 | tf_op jit(solution)/shard_map/ppermute | solution.py:358
  38.1 11.3 %collective-permute-start.13 = (bf16[128,1024]{1,0:T(8,128)(2,1)S(1)}, bf16[128,1024]{1,0:T(8,128)(2,1)S(1)}, u32[]{:S(2)}, u32[]{:S(2)}) collective-permute-start(bf16[128,1024]{1,0:T(8,128)(2,1)S(1)} %slice.42), channel_id=1, source_target_pairs={{0,2},{1,3},{2,0},{3,1},{4,6},{5,7},{6,4},{7,5},{8,10},{9,11},{10,... | collective-permute-start | bytes 786440 | tf_op jit(solution)/shard_map/ppermute | solution.py:359
  41.6 7.8 %collective-permute-start.14 = (bf16[128,1024]{1,0:T(8,128)(2,1)S(1)}, bf16[128,1024]{1,0:T(8,128)(2,1)S(1)}, u32[]{:S(2)}, u32[]{:S(2)}) collective-permute-start(bf16[128,1024]{1,0:T(8,128)(2,1)S(1)} %slice.43), channel_id=1, source_target_pairs={{0,6},{1,7},{2,4},{3,5},{4,2},{5,3},{6,0},{7,1},{8,14},{9,15},{10,... | collective-permute-start | bytes 786440 | tf_op jit(solution)/shard_map/ppermute | solution.py:360
  72.4 6.1 %collective-permute-start.15 = (f32[784,384]{1,0:T(8,128)S(1)}, f32[784,384]{1,0:T(8,128)S(1)}, u32[]{:S(2)}, u32[]{:S(2)}) collective-permute-start(f32[784,384]{1,0:T(8,128)S(1)} %get-tuple-element.53.refs_1_), channel_id=1, source_target_pairs={{0,32},{32,0},{64,96},{96,64},{1,33},{33,1},{65,97},{97,65},{2,34}... | collective-permute-start | bytes 3612680 | tf_op jit(solution)/shard_map/ppermute | solution.py:374
  77.5 4.7 %collective-permute-start.16 = (f32[784,384]{1,0:T(8,128)S(1)}, f32[784,384]{1,0:T(8,128)S(1)}, u32[]{:S(2)}, u32[]{:S(2)}) collective-permute-start(f32[784,384]{1,0:T(8,128)S(1)} %get-tuple-element.52.refs_0_.refs_1_), channel_id=1, source_target_pairs={{0,32},{32,0},{64,96},{96,64},{1,33},{33,1},{65,97},{97,65},{2,34}... | collective-permute-start | bytes 3612680 | tf_op jit(solution)/shard_map/ppermute | solution.py:375
  78.0 13.6 %collective-permute-start.18 = (f32[784,256]{1,0:T(8,128)}, f32[784,256]{1,0:T(8,128)}, u32[]{:S(2)}, u32[]{:S(2)}) collective-permute-start(f32[784,256]{1,0:T(8,128)} %get-tuple-element.62), channel_id=1, source_target_pairs={{0,32},{32,0},{64,96},{96,64},{1,33},{33,1},{65,97},{97,65},{2,34}... | collective-permute-start | bytes 2408456 | tf_op jit(solution)/shard_map/ppermute | solution.py:383
  78.0 13.6 %collective-permute-start.17 = (f32[784,256]{1,0:T(8,128)}, f32[784,256]{1,0:T(8,128)}, u32[]{:S(2)}, u32[]{:S(2)}) collective-permute-start(f32[784,256]{1,0:T(8,128)} %get-tuple-element.61), channel_id=1, source_target_pairs={{0,32},{32,0},{64,96},{96,64},{1,33},{33,1},{65,97},{97,65},{2,34}... | collective-permute-start | bytes 2408456 | tf_op jit(solution)/shard_map/ppermute | solution.py:383
  84.5 13.9 %collective-permute-start.21 = (f16[784,256]{1,0:T(8,128)(2,1)}, f16[784,256]{1,0:T(8,128)(2,1)}, u32[]{:S(2)}, u32[]{:S(2)}) collective-permute-start(f16[784,256]{1,0:T(8,128)(2,1)} %convert_element_type.18), channel_id=1, source_target_pairs={{0,64},{32,96},{64,0},{96,32},{1,65},{33,97},{65,1},{97,33},{2,66}... | collective-permute-start | bytes 1204232 | tf_op jit(solution)/shard_map/ppermute | solution.py:380
  87.4 19.6 %collective-permute-start.20 = (f16[784,256]{1,0:T(8,128)(2,1)}, f16[784,256]{1,0:T(8,128)(2,1)}, u32[]{:S(2)}, u32[]{:S(2)}) collective-permute-start(f16[784,256]{1,0:T(8,128)(2,1)} %convert_element_type.15), channel_id=1, source_target_pairs={{0,64},{32,96},{64,0},{96,32},{1,65},{33,97},{65,1},{97,33},{2,66}... | collective-permute-start | bytes 1204232 | tf_op jit(solution)/shard_map/ppermute | solution.py:380
  88.1 20.0 %collective-permute-start.19 = (f32[16,784]{1,0:T(8,128)S(1)}, f32[16,784]{1,0:T(8,128)S(1)}, u32[]{:S(2)}, u32[]{:S(2)}) collective-permute-start(f32[16,784]{1,0:T(8,128)S(1)} %get-tuple-element.64), channel_id=1, source_target_pairs={{0,64},{32,96},{64,0},{96,32},{1,65},{33,97},{65,1},{97,33},{2,66}... | collective-permute-start | bytes 150536 | tf_op jit(solution)/shard_map/ppermute | solution.py:381
  91.6 1.9 %copy-start.2 = (bf16[1568,1024]{1,0:T(8,128)(2,1)S(1)}, bf16[1568,1024]{1,0:T(8,128)(2,1)}, u32[]{:S(2)}) copy-start(bf16[1568,1024]{1,0:T(8,128)(2,1)} %refs_5_.1) | copy-start | bytes 9633796

commit v6 on v4

--- a/solution.py
+++ b/solution.py
@@ -260,26 +260,29 @@
 
 
 def pack_body(pos, first, second, got, *refs):
+    packed, counts, row = refs[-3:]
     cnt = first[:, WIDTH:] + got[:, WIDTH:]
-    packed, counts = refs[1:3] if len(refs) > 2 else refs
     counts[...] = cnt
+    here = lax.dot_general(
+        one_hot((128, 8)),
+        cnt,
+        (((0,), (1,)), ((), ())),
+        precision=lax.Precision.HIGHEST,
+        preferred_element_type=jnp.float32,
+    )
+    if len(refs) > 3:
+        row[:8, :] = refs[0][...]
+        row[8:, :] = here
+    else:
+        row[...] = here
     factor = SPAN / (cnt + 0.25)
     for k in range(2):
         lanes = slice(k * 128, (k + 1) * 128)
         packed[:, lanes] = (second[:, lanes] + got[:, lanes]) * factor
-    if len(refs) > 2:
-        for c, here in enumerate((refs[0][...], cnt)):
-            refs[3][8 * c : 8 * (c + 1), :] = lax.dot_general(
-                one_hot((128, 8)),
-                here,
-                (((0,), (1,)), ((), ())),
-                precision=lax.Precision.HIGHEST,
-                preferred_element_type=jnp.float32,
-            )
 
 
 def pack(pos, first, second, got, after, before=()):
-    outs = (f32(HALF, WIDTH), f32(HALF, 128)) + ((f32(16, HALF),) if before else ())
+    outs = (f32(HALF, WIDTH), f32(HALF, 128), f32(16 if before else 8, HALF))
     return call(pack_body, "pack", pos, (first, second, got, *before), outs, after=after)
 
 
@@ -294,8 +297,7 @@
             near[here, lanes] = total + 0.25 * own.astype(jnp.float32)
 
 
-def fresh_body(pos, near, counts0, counts1, far_row, far0, far1, fresh, out, sem):
-    copies = []
+def fresh_body(pos, near, counts0, counts1, far_row, far0, far1, out):
     for c, (counts, far) in enumerate(((counts0, far0), (counts1, far1))):
         here = slice(c * HALF, (c + 1) * HALF)
         far_counts = lax.dot_general(
@@ -311,10 +313,6 @@
             lanes = slice(k * 128, (k + 1) * 128)
             total = near[here, lanes] + far[:, lanes] * factor
             out[here, lanes] = (total * weight).astype(out.dtype)
-        copies.append(pltpu.make_async_copy(out.at[here], fresh.at[here], sem.at[c]))
-        copies[c].start()
-    for c in copies:
-        c.wait()
 
 
 FROM_PAIR = [(i, i ^ 1) for i in range(N_CENT)]
@@ -373,8 +371,8 @@
     sums1 = chunk_sums(pos, 1, weights[1], pts, (rows,))
     got0 = lax.ppermute(sums0[0], "dp", TO_CORE)
     got1 = lax.ppermute(sums1[0], "dp", TO_CORE)
-    packed0, counts0 = pack(pos, sums0[0], sums0[1], got0, (sums1[0],))
-    packed1, counts1, row = pack(pos, sums1[0], sums1[1], got1, (), (counts0,))
+    packed0, counts0, row = pack(pos, sums0[0], sums0[1], got0, (sums1[0],))
+    packed1, counts1, row = pack(pos, sums1[0], sums1[1], got1, (), (row,))
     far = [lax.ppermute(p.astype(jnp.float16), "dp", TO_Y) for p in (packed0, packed1)]
     far_row = lax.ppermute(row, "dp", TO_Y)
 
@@ -389,9 +387,7 @@
     )
     far = [f.astype(jnp.float32) for f in far]
     args = (near, counts0, counts1, far_row, *far)
-    scratch = [pltpu.VMEM((K_DEV, WIDTH), jnp.bfloat16), pltpu.SemaphoreType.DMA((2,))]
-    out = (bf16(K_DEV, WIDTH),)
-    (fresh,) = call(fresh_body, "fresh", pos, args, out, scratch, far_outs=1)
+    (fresh,) = call(fresh_body, "fresh", pos, args, (bf16(K_DEV, WIDTH),))
 
     mine = 4 * z + x
     own_rows = jnp.concatenate(

time: 111 us -> 107 us (0.964)
  waiting for transfers between devices: 23.7 us -> 18.9 us
    ppermute x1, waiting for transfers between devices: 2.94 us -> 0.01 us  [on_device(): got1 = lax.ppermute(sums1[0], 'dp', TO_CORE)]
    ppermute x2, waiting for transfers between devices: 9.75 us -> 7.92 us  [on_device(): lax.ppermute(p.astype(jnp.float16), 'dp', TO_Y)]
    unnamed x6 -> x14, local copies, waits for them, and re-layouts: 3.82 us -> 4.61 us
  transfers between devices with their start and end apart: 22 -> 22, of which waited for: 9 -> 8; matrix products, arithmetic and copies ran while one was open for 4% -> 4% of each run, Pallas kernels for 16% -> 17%
where the time goes in v6:
time: 107 us; the launch traced here: 106 us
  starting transfers between devices  32.6 us (30%)
  Pallas kernels  29.8 us (28%)
  waiting for transfers between devices  18.9 us (18%)
  blocking collectives  14 us (13%)
  other arithmetic  5.4 us (5%)
  local copies, waits for them, and re-layouts  4.86 us (5%)
    pallas_call x10, Pallas kernels, call(): pl.pallas_call(lambda p, *refs: body(p, *refs[n:]), in_specs=[IN_SMEM] +...  29.8 us
    all_to_all x1, blocking collectives, on_device(): every = lax.all_to_all(stats, 'cent', 0, 0)  14 us
    ppermute x2, waiting for transfers between devices, on_device(): lax.ppermute(p.astype(jnp.float16), 'dp', TO_Y)  7.92 us
    ppermute x3, starting transfers between devices, on_device(): lax.ppermute(b, 'cent', from_z(d))  4.98 us
    ppermute x3, waiting for transfers between devices, on_device(): lax.ppermute(b, 'cent', from_z(d))  4.95 us
    unnamed x14, local copies, waits for them, and re-layouts  4.61 us
    ppermute x2, starting transfers between devices, on_device(): lax.ppermute(p.astype(jnp.float16), 'dp', TO_Y)  4.6 us
    ppermute x3, starting transfers between devices, on_device(): lax.ppermute(a, 'cent', from_x(d))  4.41 us
  transfers between devices with their start and end apart: 22, of which 8 were waited for; matrix products, arithmetic and copies ran while one was open for 4% of the time, Pallas kernels for 17%

profile of v6, /device:TPU:0, one launch (start us, length us, event | category | flops | bytes accessed | tf_op | source)
XLA Modules:
  0.0 106.4 jit_solution(15142440224565564159)
XLA Ops:
  0.6 1.7 %collective-permute-start = (bf16[64,1024]{1,0:T(8,128)(2,1)}, bf16[64,1024]{1,0:T(8,128)(2,1)S(1)}, u32[]{:S(2)}, u32[]{:S(2)}) collective-permute-start(bf16[64,1024]{1,0:T(8,128)(2,1)} %param.2), channel_id=1, source_target_pairs={{0,1},{1,0},{2,3},{3,2},{4,5},{5,4},{6,7},{7,6},{8,9},{9,8},{10,11... | collective-permute-start | bytes 393224 | tf_op jit(solution)/shard_map/ppermute | solution.py:340
  2.4 3.7 %collective-permute-done = bf16[64,1024]{1,0:T(8,128)(2,1)S(1)} collective-permute-done((bf16[64,1024]{1,0:T(8,128)(2,1)}, bf16[64,1024]{1,0:T(8,128)(2,1)S(1)}, u32[]{:S(2)}, u32[]{:S(2)}) %collective-permute-start) | collective-permute-done | bytes 131104 | tf_op jit(solution)/shard_map/ppermute | solution.py:340
  6.1 0.9 broadcast_select_fusion.1
  7.0 3.3 %collective-permute-start.3 = (bf16[64,1024]{1,0:T(8,128)(2,1)S(1)}, bf16[64,1024]{1,0:T(8,128)(2,1)S(1)}, u32[]{:S(2)}, u32[]{:S(2)}) collective-permute-start(bf16[64,1024]{1,0:T(8,128)(2,1)S(1)} %pad_maximum_fusion.refs_0_), channel_id=1, source_target_pairs={{0,4},{1,5},{2,6},{3,7},{4,0},{5,1},{6,2},{7,3},{8,12},{9,13},{10,... | collective-permute-start | bytes 393224 | tf_op jit(solution)/shard_map/ppermute | solution.py:348
  10.3 1.1 %collective-permute-start.2 = (bf16[64,1024]{1,0:T(8,128)(2,1)S(1)}, bf16[64,1024]{1,0:T(8,128)(2,1)S(1)}, u32[]{:S(2)}, u32[]{:S(2)}) collective-permute-start(bf16[64,1024]{1,0:T(8,128)(2,1)S(1)} %pad_maximum_fusion.refs_0_), channel_id=1, source_target_pairs={{0,6},{1,7},{2,4},{3,5},{4,2},{5,3},{6,0},{7,1},{8,14},{9,15},{10,... | collective-permute-start | bytes 393224 | tf_op jit(solution)/shard_map/ppermute | solution.py:348
  11.5 0.0 collective-permute-start.1
  11.5 4.0 %collective-permute-start.6 = (bf16[64,1024]{1,0:T(8,128)(2,1)S(1)}, bf16[64,1024]{1,0:T(8,128)(2,1)S(1)}, u32[]{:S(2)}, u32[]{:S(2)}) collective-permute-start(bf16[64,1024]{1,0:T(8,128)(2,1)S(1)} %pad_maximum_fusion.1.refs_4_), channel_id=1, source_target_pairs={{0,16},{1,17},{2,18},{3,19},{4,20},{5,21},{6,22},{7,23},{8,24},{9,... | collective-permute-start | bytes 393224 | tf_op jit(solution)/shard_map/ppermute | solution.py:349
  15.4 0.7 collective-permute-start.5
  16.1 0.0 collective-permute-done.3.refs_3_
  16.1 0.3 collective-permute-start.4
  16.5 0.1 stack.31.p
  16.5 0.0 collective-permute-done.2.refs_2_
  16.5 0.1 collective-permute-done.1.refs_1_
  16.7 1.8 %collective-permute-done.6.refs_7_ = bf16[64,1024]{1,0:T(8,128)(2,1)S(1)} collective-permute-done((bf16[64,1024]{1,0:T(8,128)(2,1)S(1)}, bf16[64,1024]{1,0:T(8,128)(2,1)S(1)}, u32[]{:S(2)}, u32[]{:S(2)}) %collective-permute-start.6) | collective-permute-done | bytes 131104 | tf_op jit(solution)/shard_map/ppermute | solution.py:349
  18.5 3.1 %collective-permute-done.5.refs_6_ = bf16[64,1024]{1,0:T(8,128)(2,1)S(1)} collective-permute-done((bf16[64,1024]{1,0:T(8,128)(2,1)S(1)}, bf16[64,1024]{1,0:T(8,128)(2,1)S(1)}, u32[]{:S(2)}, u32[]{:S(2)}) %collective-permute-start.5) | collective-permute-done | bytes 131104 | tf_op jit(solution)/shard_map/ppermute | solution.py:349
  21.6 0.0 collective-permute-done.4.refs_5_
  21.6 0.6 join.1
  22.2 2.2 %collective-permute-start.8 = (bf16[256,1024]{1,0:T(8,128)(2,1)S(1)}, bf16[256,1024]{1,0:T(8,128)(2,1)S(1)}, u32[]{:S(2)}, u32[]{:S(2)}) collective-permute-start(bf16[256,1024]{1,0:T(8,128)(2,1)S(1)} %get-tuple-element.35.refs_1_.refs_3_), channel_id=1, source_target_pairs={{0,24},{1,25},{2,26},{3,27},{4,28},{5,29},{6,30},{7,31},{8,16},{9,... | collective-permute-start | bytes 1572872 | tf_op jit(solution)/shard_map/ppermute | solution.py:352
  24.4 0.0 collective-permute-start.7
  24.4 3.2 %collective-permute-start.10 = (bf16[256,1024]{1,0:T(8,128)(2,1)S(1)}, bf16[256,1024]{1,0:T(8,128)(2,1)S(1)}, u32[]{:S(2)}, u32[]{:S(2)}) collective-permute-start(bf16[256,1024]{1,0:T(8,128)(2,1)S(1)} %get-tuple-element.36.refs_2_.refs_4_), channel_id=1, source_target_pairs={{0,6},{1,7},{2,4},{3,5},{4,2},{5,3},{6,0},{7,1},{8,14},{9,15},{10,... | collective-permute-start | bytes 1572872 | tf_op jit(solution)/shard_map/ppermute | solution.py:352
  27.6 0.2 collective-permute-start.9
  27.9 1.9 %copy-done = bf16[1568,1024]{1,0:T(8,128)(2,1)S(1)} copy-done((bf16[1568,1024]{1,0:T(8,128)(2,1)S(1)}, bf16[1568,1024]{1,0:T(8,128)(2,1)}, u32[]{:S(2)}) %copy-start) | copy-done | bytes 3211288
  29.8 3.6 %weights.3 = (f32[4,128]{1,0:T(4,128)S(1)}, f32[1568,1]{1,0:T(8,128)S(1)}, f32[784,512]{1,0:T(8,128)S(1)}, f32[784,512]{1,0:T(8,128)S(1)}, f32[2,512]{1,0:T(2,128)S(1)}) custom-call(s32[7]{0:T(128)S(1)} %stack.31.p, bf16[1568,1024]{1,0:T(8,128)(2,1)S(1)} %copy-done, bf16[256,1024]{1,0:T(8,128)(2,1)S(1)} %get-tuple-element.35.refs_1_.refs_3_, ...), custom_call_target="tpu_custom_call" | custom-call | flops 1644167168 | bytes 7483520 | tf_op jit(solution)/shard_map/weights/pallas_call | solution.py:54
  33.3 2.0 %collective-permute-done.8.refs_2_.refs_6_ = bf16[256,1024]{1,0:T(8,128)(2,1)S(1)} collective-permute-done((bf16[256,1024]{1,0:T(8,128)(2,1)S(1)}, bf16[256,1024]{1,0:T(8,128)(2,1)S(1)}, u32[]{:S(2)}, u32[]{:S(2)}) %collective-permute-start.8) | collective-permute-done | bytes 524320 | tf_op jit(solution)/shard_map/ppermute | solution.py:352
  35.4 0.1 collective-permute-start.11
  35.5 0.2 collective-permute-done.7.refs_1_.refs_5_
  35.6 2.5 %collective-permute-start.12 = (bf16[128,1024]{1,0:T(8,128)(2,1)S(1)}, bf16[128,1024]{1,0:T(8,128)(2,1)S(1)}, u32[]{:S(2)}, u32[]{:S(2)}) collective-permute-start(bf16[128,1024]{1,0:T(8,128)(2,1)S(1)} %slice.37), channel_id=1, source_target_pairs={{0,24},{1,25},{2,26},{3,27},{4,28},{5,29},{6,30},{7,31},{8,16},{9,... | collective-permute-start | bytes 786440 | tf_op jit(solution)/shard_map/ppermute | solution.py:356
  38.1 0.0 collective-permute-done.10.refs_4_.refs_8_
  38.1 3.5 %collective-permute-start.13 = (bf16[128,1024]{1,0:T(8,128)(2,1)S(1)}, bf16[128,1024]{1,0:T(8,128)(2,1)S(1)}, u32[]{:S(2)}, u32[]{:S(2)}) collective-permute-start(bf16[128,1024]{1,0:T(8,128)(2,1)S(1)} %slice.38), channel_id=1, source_target_pairs={{0,2},{1,3},{2,0},{3,1},{4,6},{5,7},{6,4},{7,5},{8,10},{9,11},{10,... | collective-permute-start | bytes 786440 | tf_op jit(solution)/shard_map/ppermute | solution.py:357
  41.6 0.0 collective-permute-done.9.refs_3_.refs_7_
  41.6 2.4 %collective-permute-start.14 = (bf16[128,1024]{1,0:T(8,128)(2,1)S(1)}, bf16[128,1024]{1,0:T(8,128)(2,1)S(1)}, u32[]{:S(2)}, u32[]{:S(2)}) collective-permute-start(bf16[128,1024]{1,0:T(8,128)(2,1)S(1)} %slice.39), channel_id=1, source_target_pairs={{0,6},{1,7},{2,4},{3,5},{4,2},{5,3},{6,0},{7,1},{8,14},{9,15},{10,... | collective-permute-start | bytes 786440 | tf_op jit(solution)/shard_map/ppermute | solution.py:358
  44.0 5.4 %weights.4 = (f32[8,128]{1,0:T(8,128)S(1)}, f32[784,1024]{1,0:T(8,128)S(1)}, f32[784,1024]{1,0:T(8,128)S(1)}, f32[2,1024]{1,0:T(2,128)S(1)}) custom-call(s32[7]{0:T(128)S(1)} %stack.31.p, bf16[1568,1024]{1,0:T(8,128)(2,1)S(1)} %copy-done.1, bf16[256,1024]{1,0:T(8,128)(2,1)S(1)} %collective-permute-done.7.refs_1_.refs_5_, ...), custom_call_target="tpu_custom_call" | custom-call | flops 3288334336 | bytes 11749504 | tf_op jit(solution)/shard_map/weights/pallas_call | solution.py:54
  49.4 0.0 collective-permute-done.11.refs_1_
  49.4 0.0 collective-permute-done.12.refs_2_
  49.5 0.0 collective-permute-done.13.refs_3_
  49.5 0.0 collective-permute-done.14.refs_4_
  49.5 3.2 %weights.5 = (bf16[256,1024]{1,0:T(8,128)(2,1)S(1)}, bf16[256,1024]{1,0:T(8,128)(2,1)S(1)}, f32[32,16,128]{2,1,0:T(8,128)S(1)}, f32[784,512]{1,0:T(8,128)S(1)}, ...) custom-call(s32[7]{0:T(128)S(1)} %stack.31.p, bf16[1568,1024]{1,0:T(8,128)(2,1)S(1)} %copy-done.1, ...), custom_call_target="tpu_custom_call" | custom-call | flops 1644167168 | bytes 8798336 | tf_op jit(solution)/shard_map/weights/pallas_call | solution.py:54
  52.7 14.0 %all_to_all.5.refs_11_ = f32[32,16,128]{2,1,0:T(8,128)S(1)} all-to-all(f32[32,16,128]{2,1,0:T(8,128)S(1)} %get-tuple-element.48), channel_id=1, replica_groups=mesh['dp'=4,'cent'=32] {'cent'}, dimensions={0} | all-to-all | bytes 524288 | tf_op jit(solution)/shard_map/all_to_all | solution.py:367
  66.7 5.7 %sums.2 = (f32[784,384]{1,0:T(8,128)S(1)}, f32[784,256]{1,0:T(8,128)S(1)}, f32[784,256]{1,0:T(8,128)}, f32[784,256]{1,0:T(8,128)S(1)}, f32[16,128]{1,0:T(8,128)S(1)}, /*index=5*/f32[8,2048]{1,0:T(8,128)S(1)}) custom-call(s32[7]{0:T(128)S(1)} %stack.31.p, f32[784,512]{1,0:T(8,128)S(1)} %get-tuple-element.45.refs_0_, ...), custom_call_target="tpu_custom_call" | custom-call | flops 3288334336 | bytes 14581760 | tf_op jit(solution)/shard_map/sums/pallas_call | solution.py:54
  72.4 0.0 collective-permute-start.16
  72.4 5.1 %sums.3 = (f32[784,384]{1,0:T(8,128)S(1)}, f32[784,256]{1,0:T(8,128)S(1)}, f32[784,256]{1,0:T(8,128)}, f32[784,256]{1,0:T(8,128)S(1)}) custom-call(s32[7]{0:T(128)S(1)} %stack.31.p, f32[784,512]{1,0:T(8,128)S(1)} %get-tuple-element.37.refs_0_, f32[784,1024]{1,0:T(8,128)S(1)} %get-tuple-element.39.refs_1_, f32[784,512]{1,0:T(8,128)S(1)} %get-tuple-element.42.refs_2_, ...), custom_call_target="tpu_custom_call" | custom-call | flops 3288334336 | bytes 14295040 | tf_op jit(solution)/shard_map/sums/pallas_call | solution.py:54
  77.5 0.5 collective-permute-start.15
  78.0 0.0 collective-permute-start.18
  78.0 0.5 collective-permute-start.17
  78.5 0.0 collective-permute-done.16.refs_3_
  78.5 1.0 pack.2
  79.6 0.9 convert_element_type.12
  80.5 2.9 %collective-permute-start.20 = (f16[784,256]{1,0:T(8,128)(2,1)}, f16[784,256]{1,0:T(8,128)(2,1)}, u32[]{:S(2)}, u32[]{:S(2)}) collective-permute-start(f16[784,256]{1,0:T(8,128)(2,1)} %convert_element_type.12), channel_id=1, source_target_pairs={{0,64},{32,96},{64,0},{96,32},{1,65},{33,97},{65,1},{97,33},{2,66}... | collective-permute-start | bytes 1204232 | tf_op jit(solution)/shard_map/ppermute | solution.py:376
  83.4 1.1 pack.3
  84.5 0.8 copy-done.5
  85.3 0.8 convert_element_type.14
  86.1 1.7 %collective-permute-start.21 = (f16[784,256]{1,0:T(8,128)(2,1)}, f16[784,256]{1,0:T(8,128)(2,1)}, u32[]{:S(2)}, u32[]{:S(2)}) collective-permute-start(f16[784,256]{1,0:T(8,128)(2,1)} %convert_element_type.14), channel_id=1, source_target_pairs={{0,64},{32,96},{64,0},{96,32},{1,65},{33,97},{65,1},{97,33},{2,66}... | collective-permute-start | bytes 1204232 | tf_op jit(solution)/shard_map/ppermute | solution.py:376
  87.8 0.1 dynamic-slice_bitcast_fusion.1
  87.9 1.8 %collective-permute-start.19 = (f32[16,784]{1,0:T(8,128)S(1)}, f32[16,784]{1,0:T(8,128)S(1)}, u32[]{:S(2)}, u32[]{:S(2)}) collective-permute-start(f32[16,784]{1,0:T(8,128)S(1)} %get-tuple-element.65), channel_id=1, source_target_pairs={{0,64},{32,96},{64,0},{96,32},{1,65},{33,97},{65,1},{97,33},{2,66}... | collective-permute-start | bytes 150536 | tf_op jit(solution)/shard_map/ppermute | solution.py:377
  89.7 0.6 pad_maximum_fusion.2
  90.3 0.0 collective-permute-done.18.refs_4_
  90.3 1.9 %copy-done.2 = bf16[1568,1024]{1,0:T(8,128)(2,1)S(1)} copy-done((bf16[1568,1024]{1,0:T(8,128)(2,1)S(1)}, bf16[1568,1024]{1,0:T(8,128)(2,1)}, u32[]{:S(2)}) %copy-start.2) | copy-done | bytes 3211288
  92.2 1.6 %near.1.refs_0_ = f32[1568,256]{1,0:T(8,128)S(1)} custom-call(s32[7]{0:T(128)S(1)} %stack.31.p, f32[784,256]{1,0:T(8,128)S(1)} %get-tuple-element.58.refs_0_, f32[784,256]{1,0:T(8,128)S(1)} %get-tuple-element.59.refs_1_, f32[784,256]{1,0:T(8,128)S(1)} %get-tuple-element.60.refs_2_, f32[784,256]{1,0:T(8,128)} %collective-permute-done.17.refs_3_, ...), custom_call_target="tpu_custom_call" | custom-call | bytes 8028160 | tf_op jit(solution)/shard_map/near/pallas_call | solution.py:54
  93.8 0.7 collective-permute-done.20
  94.5 1.1 convert_element_type.13.refs_4_
  95.6 7.2 %collective-permute-done.21 = f16[784,256]{1,0:T(8,128)(2,1)} collective-permute-done((f16[784,256]{1,0:T(8,128)(2,1)}, f16[784,256]{1,0:T(8,128)(2,1)}, u32[]{:S(2)}, u32[]{:S(2)}) %collective-permute-start.21) | collective-permute-done | bytes 401440 | tf_op jit(solution)/shard_map/ppermute | solution.py:376
  102.8 1.1 convert_element_type.15.refs_5_
  103.8 0.0 collective-permute-done.19.refs_3_
  103.9 2.6 %fresh.1 = bf16[1568,256]{1,0:T(8,128)(2,1)} custom-call(s32[7]{0:T(128)S(1)} %stack.31.p, f32[1568,256]{1,0:T(8,128)S(1)} %near.1.refs_0_, f32[784,128]{1,0:T(8,128)S(1)} %copy-done.4, f32[784,128]{1,0:T(8,128)S(1)} %copy-done.6, f32[16,784]{1,0:T(8,128)S(1)} %collective-permute-done.19.refs_3_, f32[784,256]{1,0:T(8,128)S(1)} %convert_element_type.13.refs_4_, ...), custom_call_target="tpu_custom_call" | custom-call | bytes 4867072 | tf_op jit(solution)/shard_map/fresh/pallas_call | solution.py:54
  (20 shorter events, 0.1 us)
Async XLA Ops:
  0.6 5.4 %collective-permute-start = (bf16[64,1024]{1,0:T(8,128)(2,1)}, bf16[64,1024]{1,0:T(8,128)(2,1)S(1)}, u32[]{:S(2)}, u32[]{:S(2)}) collective-permute-start(bf16[64,1024]{1,0:T(8,128)(2,1)} %param.2), channel_id=1, source_target_pairs={{0,1},{1,0},{2,3},{3,2},{4,5},{5,4},{6,7},{7,6},{8,9},{9,8},{10,11... | collective-permute-start | bytes 393224 | tf_op jit(solution)/shard_map/ppermute | solution.py:340
  7.0 9.1 %collective-permute-start.3 = (bf16[64,1024]{1,0:T(8,128)(2,1)S(1)}, bf16[64,1024]{1,0:T(8,128)(2,1)S(1)}, u32[]{:S(2)}, u32[]{:S(2)}) collective-permute-start(bf16[64,1024]{1,0:T(8,128)(2,1)S(1)} %pad_maximum_fusion.refs_0_), channel_id=1, source_target_pairs={{0,4},{1,5},{2,6},{3,7},{4,0},{5,1},{6,2},{7,3},{8,12},{9,13},{10,... | collective-permute-start | bytes 393224 | tf_op jit(solution)/shard_map/ppermute | solution.py:348
  10.3 6.2 %collective-permute-start.2 = (bf16[64,1024]{1,0:T(8,128)(2,1)S(1)}, bf16[64,1024]{1,0:T(8,128)(2,1)S(1)}, u32[]{:S(2)}, u32[]{:S(2)}) collective-permute-start(bf16[64,1024]{1,0:T(8,128)(2,1)S(1)} %pad_maximum_fusion.refs_0_), channel_id=1, source_target_pairs={{0,6},{1,7},{2,4},{3,5},{4,2},{5,3},{6,0},{7,1},{8,14},{9,15},{10,... | collective-permute-start | bytes 393224 | tf_op jit(solution)/shard_map/ppermute | solution.py:348
  11.5 5.2 %collective-permute-start.1 = (bf16[64,1024]{1,0:T(8,128)(2,1)S(1)}, bf16[64,1024]{1,0:T(8,128)(2,1)S(1)}, u32[]{:S(2)}, u32[]{:S(2)}) collective-permute-start(bf16[64,1024]{1,0:T(8,128)(2,1)S(1)} %pad_maximum_fusion.refs_0_), channel_id=1, source_target_pairs={{0,2},{1,3},{2,0},{3,1},{4,6},{5,7},{6,4},{7,5},{8,10},{9,11},{10,... | collective-permute-start | bytes 393224 | tf_op jit(solution)/shard_map/ppermute | solution.py:348
  11.5 7.0 %collective-permute-start.6 = (bf16[64,1024]{1,0:T(8,128)(2,1)S(1)}, bf16[64,1024]{1,0:T(8,128)(2,1)S(1)}, u32[]{:S(2)}, u32[]{:S(2)}) collective-permute-start(bf16[64,1024]{1,0:T(8,128)(2,1)S(1)} %pad_maximum_fusion.1.refs_4_), channel_id=1, source_target_pairs={{0,16},{1,17},{2,18},{3,19},{4,20},{5,21},{6,22},{7,23},{8,24},{9,... | collective-permute-start | bytes 393224 | tf_op jit(solution)/shard_map/ppermute | solution.py:349
  15.4 6.2 %collective-permute-start.5 = (bf16[64,1024]{1,0:T(8,128)(2,1)S(1)}, bf16[64,1024]{1,0:T(8,128)(2,1)S(1)}, u32[]{:S(2)}, u32[]{:S(2)}) collective-permute-start(bf16[64,1024]{1,0:T(8,128)(2,1)S(1)} %pad_maximum_fusion.1.refs_4_), channel_id=1, source_target_pairs={{0,24},{1,25},{2,26},{3,27},{4,28},{5,29},{6,30},{7,31},{8,16},{9,... | collective-permute-start | bytes 393224 | tf_op jit(solution)/shard_map/ppermute | solution.py:349
  16.1 5.5 %collective-permute-start.4 = (bf16[64,1024]{1,0:T(8,128)(2,1)S(1)}, bf16[64,1024]{1,0:T(8,128)(2,1)S(1)}, u32[]{:S(2)}, u32[]{:S(2)}) collective-permute-start(bf16[64,1024]{1,0:T(8,128)(2,1)S(1)} %pad_maximum_fusion.1.refs_4_), channel_id=1, source_target_pairs={{0,8},{1,9},{2,10},{3,11},{4,12},{5,13},{6,14},{7,15},{8,0},{9,1},... | collective-permute-start | bytes 393224 | tf_op jit(solution)/shard_map/ppermute | solution.py:349
  22.2 13.1 %collective-permute-start.8 = (bf16[256,1024]{1,0:T(8,128)(2,1)S(1)}, bf16[256,1024]{1,0:T(8,128)(2,1)S(1)}, u32[]{:S(2)}, u32[]{:S(2)}) collective-permute-start(bf16[256,1024]{1,0:T(8,128)(2,1)S(1)} %get-tuple-element.35.refs_1_.refs_3_), channel_id=1, source_target_pairs={{0,24},{1,25},{2,26},{3,27},{4,28},{5,29},{6,30},{7,31},{8,16},{9,... | collective-permute-start | bytes 1572872 | tf_op jit(solution)/shard_map/ppermute | solution.py:352
  24.4 11.2 %collective-permute-start.7 = (bf16[256,1024]{1,0:T(8,128)(2,1)S(1)}, bf16[256,1024]{1,0:T(8,128)(2,1)S(1)}, u32[]{:S(2)}, u32[]{:S(2)}) collective-permute-start(bf16[256,1024]{1,0:T(8,128)(2,1)S(1)} %get-tuple-element.35.refs_1_.refs_3_), channel_id=1, source_target_pairs={{0,8},{1,9},{2,10},{3,11},{4,12},{5,13},{6,14},{7,15},{8,0},{9,1},... | collective-permute-start | bytes 1572872 | tf_op jit(solution)/shard_map/ppermute | solution.py:351
  24.4 13.7 %collective-permute-start.10 = (bf16[256,1024]{1,0:T(8,128)(2,1)S(1)}, bf16[256,1024]{1,0:T(8,128)(2,1)S(1)}, u32[]{:S(2)}, u32[]{:S(2)}) collective-permute-start(bf16[256,1024]{1,0:T(8,128)(2,1)S(1)} %get-tuple-element.36.refs_2_.refs_4_), channel_id=1, source_target_pairs={{0,6},{1,7},{2,4},{3,5},{4,2},{5,3},{6,0},{7,1},{8,14},{9,15},{10,... | collective-permute-start | bytes 1572872 | tf_op jit(solution)/shard_map/ppermute | solution.py:352
  27.6 14.0 %collective-permute-start.9 = (bf16[256,1024]{1,0:T(8,128)(2,1)S(1)}, bf16[256,1024]{1,0:T(8,128)(2,1)S(1)}, u32[]{:S(2)}, u32[]{:S(2)}) collective-permute-start(bf16[256,1024]{1,0:T(8,128)(2,1)S(1)} %get-tuple-element.36.refs_2_.refs_4_), channel_id=1, source_target_pairs={{0,2},{1,3},{2,0},{3,1},{4,6},{5,7},{6,4},{7,5},{8,10},{9,11},{10,... | collective-permute-start | bytes 1572872 | tf_op jit(solution)/shard_map/ppermute | solution.py:351
  27.9 1.9 %copy-start = (bf16[1568,1024]{1,0:T(8,128)(2,1)S(1)}, bf16[1568,1024]{1,0:T(8,128)(2,1)}, u32[]{:S(2)}) copy-start(bf16[1568,1024]{1,0:T(8,128)(2,1)} %refs_5_.1) | copy-start | bytes 9633796
  29.8 14.2 %copy-start.1 = (bf16[1568,1024]{1,0:T(8,128)(2,1)S(1)}, bf16[1568,1024]{1,0:T(8,128)(2,1)}, u32[]{:S(2)}) copy-start(bf16[1568,1024]{1,0:T(8,128)(2,1)} %refs_5_.1) | copy-start | bytes 9633796
  35.4 14.1 %collective-permute-start.11 = (bf16[128,1024]{1,0:T(8,128)(2,1)S(1)}, bf16[128,1024]{1,0:T(8,128)(2,1)S(1)}, u32[]{:S(2)}, u32[]{:S(2)}) collective-permute-start(bf16[128,1024]{1,0:T(8,128)(2,1)S(1)} %slice.36), channel_id=1, source_target_pairs={{0,8},{1,9},{2,10},{3,11},{4,12},{5,13},{6,14},{7,15},{8,0},{9,1},... | collective-permute-start | bytes 786440 | tf_op jit(solution)/shard_map/ppermute | solution.py:355
  35.6 13.8 %collective-permute-start.12 = (bf16[128,1024]{1,0:T(8,128)(2,1)S(1)}, bf16[128,1024]{1,0:T(8,128)(2,1)S(1)}, u32[]{:S(2)}, u32[]{:S(2)}) collective-permute-start(bf16[128,1024]{1,0:T(8,128)(2,1)S(1)} %slice.37), channel_id=1, source_target_pairs={{0,24},{1,25},{2,26},{3,27},{4,28},{5,29},{6,30},{7,31},{8,16},{9,... | collective-permute-start | bytes 786440 | tf_op jit(solution)/shard_map/ppermute | solution.py:356
  38.1 11.3 %collective-permute-start.13 = (bf16[128,1024]{1,0:T(8,128)(2,1)S(1)}, bf16[128,1024]{1,0:T(8,128)(2,1)S(1)}, u32[]{:S(2)}, u32[]{:S(2)}) collective-permute-start(bf16[128,1024]{1,0:T(8,128)(2,1)S(1)} %slice.38), channel_id=1, source_target_pairs={{0,2},{1,3},{2,0},{3,1},{4,6},{5,7},{6,4},{7,5},{8,10},{9,11},{10,... | collective-permute-start | bytes 786440 | tf_op jit(solution)/shard_map/ppermute | solution.py:357
  41.6 7.8 %collective-permute-start.14 = (bf16[128,1024]{1,0:T(8,128)(2,1)S(1)}, bf16[128,1024]{1,0:T(8,128)(2,1)S(1)}, u32[]{:S(2)}, u32[]{:S(2)}) collective-permute-start(bf16[128,1024]{1,0:T(8,128)(2,1)S(1)} %slice.39), channel_id=1, source_target_pairs={{0,6},{1,7},{2,4},{3,5},{4,2},{5,3},{6,0},{7,1},{8,14},{9,15},{10,... | collective-permute-start | bytes 786440 | tf_op jit(solution)/shard_map/ppermute | solution.py:358
  72.4 6.1 %collective-permute-start.16 = (f32[784,384]{1,0:T(8,128)S(1)}, f32[784,384]{1,0:T(8,128)S(1)}, u32[]{:S(2)}, u32[]{:S(2)}) collective-permute-start(f32[784,384]{1,0:T(8,128)S(1)} %get-tuple-element.55.refs_1_), channel_id=1, source_target_pairs={{0,32},{32,0},{64,96},{96,64},{1,33},{33,1},{65,97},{97,65},{2,34}... | collective-permute-start | bytes 3612680 | tf_op jit(solution)/shard_map/ppermute | solution.py:372
  77.5 5.9 %collective-permute-start.15 = (f32[784,384]{1,0:T(8,128)S(1)}, f32[784,384]{1,0:T(8,128)S(1)}, u32[]{:S(2)}, u32[]{:S(2)}) collective-permute-start(f32[784,384]{1,0:T(8,128)S(1)} %get-tuple-element.53.refs_0_), channel_id=1, source_target_pairs={{0,32},{32,0},{64,96},{96,64},{1,33},{33,1},{65,97},{97,65},{2,34}... | collective-permute-start | bytes 3612680 | tf_op jit(solution)/shard_map/ppermute | solution.py:373
  78.0 12.2 %collective-permute-start.18 = (f32[784,256]{1,0:T(8,128)}, f32[784,256]{1,0:T(8,128)S(1)}, u32[]{:S(2)}, u32[]{:S(2)}) collective-permute-start(f32[784,256]{1,0:T(8,128)} %get-tuple-element.62), channel_id=1, source_target_pairs={{0,32},{32,0},{64,96},{96,64},{1,33},{33,1},{65,97},{97,65},{2,34}... | collective-permute-start | bytes 2408456 | tf_op jit(solution)/shard_map/ppermute | solution.py:379
  78.0 12.2 %collective-permute-start.17 = (f32[784,256]{1,0:T(8,128)}, f32[784,256]{1,0:T(8,128)}, u32[]{:S(2)}, u32[]{:S(2)}) collective-permute-start(f32[784,256]{1,0:T(8,128)} %get-tuple-element.61), channel_id=1, source_target_pairs={{0,32},{32,0},{64,96},{96,64},{1,33},{33,1},{65,97},{97,65},{2,34}... | collective-permute-start | bytes 2408456 | tf_op jit(solution)/shard_map/ppermute | solution.py:379
  79.6 4.9 %copy-start.3 = (f32[784,128]{1,0:T(8,128)}, f32[784,128]{1,0:T(8,128)S(1)}, u32[]{:S(2)}) copy-start(f32[784,128]{1,0:T(8,128)S(1)} %get-tuple-element.63.refs_1_) | copy-start | bytes 1204228
  80.5 14.0 %collective-permute-start.20 = (f16[784,256]{1,0:T(8,128)(2,1)}, f16[784,256]{1,0:T(8,128)(2,1)}, u32[]{:S(2)}, u32[]{:S(2)}) collective-permute-start(f16[784,256]{1,0:T(8,128)(2,1)} %convert_element_type.12), channel_id=1, source_target_pairs={{0,64},{32,96},{64,0},{96,32},{1,65},{33,97},{65,1},{97,33},{2,66}... | collective-permute-start | bytes 1204232 | tf_op jit(solution)/shard_map/ppermute | solution.py:376
  84.5 0.8 copy-start.5
  86.1 16.7 %collective-permute-start.21 = (f16[784,256]{1,0:T(8,128)(2,1)}, f16[784,256]{1,0:T(8,128)(2,1)}, u32[]{:S(2)}, u32[]{:S(2)}) collective-permute-start(f16[784,256]{1,0:T(8,128)(2,1)} %convert_element_type.14), channel_id=1, source_target_pairs={{0,64},{32,96},{64,0},{96,32},{1,65},{33,97},{65,1},{97,33},{2,66}... | collective-permute-start | bytes 1204232 | tf_op jit(solution)/shard_map/ppermute | solution.py:376
  87.9 16.0 %collective-permute-start.19 = (f32[16,784]{1,0:T(8,128)S(1)}, f32[16,784]{1,0:T(8,128)S(1)}, u32[]{:S(2)}, u32[]{:S(2)}) collective-permute-start(f32[16,784]{1,0:T(8,128)S(1)} %get-tuple-element.65), channel_id=1, source_target_pairs={{0,64},{32,96},{64,0},{96,32},{1,65},{33,97},{65,1},{97,33},{2,66}... | collective-permute-start | bytes 150536 | tf_op jit(solution)/shard_map/ppermute | solution.py:377
  90.3 1.9 %copy-start.2 = (bf16[1568,1024]{1,0:T(8,128)(2,1)S(1)}, bf16[1568,1024]{1,0:T(8,128)(2,1)}, u32[]{:S(2)}) copy-start(bf16[1568,1024]{1,0:T(8,128)(2,1)} %refs_5_.1) | copy-start | bytes 9633796
  93.8 10.1 %copy-start.4 = (f32[784,128]{1,0:T(8,128)S(1)}, f32[784,128]{1,0:T(8,128)}, u32[]{:S(2)}) copy-start(f32[784,128]{1,0:T(8,128)} %copy-done.3) | copy-start | bytes 1204228
  93.8 10.1 %copy-start.6 = (f32[784,128]{1,0:T(8,128)S(1)}, f32[784,128]{1,0:T(8,128)}, u32[]{:S(2)}) copy-start(f32[784,128]{1,0:T(8,128)} %copy-done.5) | copy-start | bytes 1204228

commit v7 on v6

--- a/solution.py
+++ b/solution.py
@@ -143,7 +143,7 @@
                 value = straight if (h == 0) == a else turned
                 lanes = slice(0, UNIT) if a else slice(UNIT, 128)
                 place[pl.ds(block_of(unit, pos[0], pos[1]), 1), lanes] = value[0:1, lanes]
-        whole = place[...]
+        whole = place[:BLOCKS, :]
         for j in range(N_CENT):
             out[j] = whole
 
@@ -164,7 +164,7 @@
         pos,
         args,
         outs,
-        [pltpu.VMEM((BLOCKS, 128), jnp.float32)] if before else [],
+        [pltpu.VMEM((BLOCKS + 8, 128), jnp.float32)] if before else [],
         flops=2 * K_DEV * n * PIECE * D,
         exps=K_DEV * n * PIECE,
     )
@@ -180,8 +180,8 @@
         total = total + jnp.exp(every[j] - peak)
     both = []
     for value in (peak, 1.0 / total):
-        place[...] = value
-        turned[...] = pltpu.roll(value, UNIT, 1)
+        place[:BLOCKS, :] = value
+        turned[:BLOCKS, :] = pltpu.roll(value, UNIT, 1)
         parts = []
         for units in PIECES:
             for h in range(2):
@@ -243,7 +243,7 @@
     scratch = [pltpu.VMEM((HALF, ROWS), jnp.bfloat16)]
     if chunk == 0:
         outs += [f32(BLOCKS, 128), f32(8, ROWS)]
-        scratch += [pltpu.VMEM((BLOCKS, 128), jnp.float32)] * 2
+        scratch += [pltpu.VMEM((BLOCKS + 8, 128), jnp.float32)] * 2
     return call(
         functools.partial(sums_body, chunk),
         "sums",

time: 107 us -> 107 us (level)
  no operation moved by 1% of the time
where the time goes in v7:
time: 107 us; the launch traced here: 106 us
  starting transfers between devices  32.6 us (30%)
  Pallas kernels  29.8 us (28%)
  waiting for transfers between devices  18.9 us (18%)
  blocking collectives  14 us (13%)
  other arithmetic  5.4 us (5%)
  local copies, waits for them, and re-layouts  4.86 us (5%)
    pallas_call x10, Pallas kernels, call(): pl.pallas_call(lambda p, *refs: body(p, *refs[n:]), in_specs=[IN_SMEM] +...  29.8 us
    all_to_all x1, blocking collectives, on_device(): every = lax.all_to_all(stats, 'cent', 0, 0)  14 us
    ppermute x2, waiting for transfers between devices, on_device(): lax.ppermute(p.astype(jnp.float16), 'dp', TO_Y)  7.91 us
    ppermute x3, starting transfers between devices, on_device(): lax.ppermute(b, 'cent', from_z(d))  4.98 us
    ppermute x3, waiting for transfers between devices, on_device(): lax.ppermute(b, 'cent', from_z(d))  4.95 us
    ppermute x2, starting transfers between devices, on_device(): lax.ppermute(p.astype(jnp.float16), 'dp', TO_Y)  4.62 us
    unnamed x14, local copies, waits for them, and re-layouts  4.61 us
    ppermute x3, starting transfers between devices, on_device(): lax.ppermute(a, 'cent', from_x(d))  4.41 us
  transfers between devices with their start and end apart: 22, of which 8 were waited for; matrix products, arithmetic and copies ran while one was open for 4% of the time, Pallas kernels for 17%

profile of v7, /device:TPU:0, one launch (start us, length us, event | category | flops | bytes accessed | tf_op | source)
XLA Modules:
  0.0 106.4 jit_solution(11831480661802429321)
XLA Ops:
  0.6 1.7 %collective-permute-start = (bf16[64,1024]{1,0:T(8,128)(2,1)}, bf16[64,1024]{1,0:T(8,128)(2,1)S(1)}, u32[]{:S(2)}, u32[]{:S(2)}) collective-permute-start(bf16[64,1024]{1,0:T(8,128)(2,1)} %param.2), channel_id=1, source_target_pairs={{0,1},{1,0},{2,3},{3,2},{4,5},{5,4},{6,7},{7,6},{8,9},{9,8},{10,11... | collective-permute-start | bytes 393224 | tf_op jit(solution)/shard_map/ppermute | solution.py:340
  2.4 3.7 %collective-permute-done = bf16[64,1024]{1,0:T(8,128)(2,1)S(1)} collective-permute-done((bf16[64,1024]{1,0:T(8,128)(2,1)}, bf16[64,1024]{1,0:T(8,128)(2,1)S(1)}, u32[]{:S(2)}, u32[]{:S(2)}) %collective-permute-start) | collective-permute-done | bytes 131104 | tf_op jit(solution)/shard_map/ppermute | solution.py:340
  6.1 0.9 broadcast_select_fusion.1
  7.0 3.3 %collective-permute-start.3 = (bf16[64,1024]{1,0:T(8,128)(2,1)S(1)}, bf16[64,1024]{1,0:T(8,128)(2,1)S(1)}, u32[]{:S(2)}, u32[]{:S(2)}) collective-permute-start(bf16[64,1024]{1,0:T(8,128)(2,1)S(1)} %pad_maximum_fusion.refs_0_), channel_id=1, source_target_pairs={{0,4},{1,5},{2,6},{3,7},{4,0},{5,1},{6,2},{7,3},{8,12},{9,13},{10,... | collective-permute-start | bytes 393224 | tf_op jit(solution)/shard_map/ppermute | solution.py:348
  10.3 1.1 %collective-permute-start.2 = (bf16[64,1024]{1,0:T(8,128)(2,1)S(1)}, bf16[64,1024]{1,0:T(8,128)(2,1)S(1)}, u32[]{:S(2)}, u32[]{:S(2)}) collective-permute-start(bf16[64,1024]{1,0:T(8,128)(2,1)S(1)} %pad_maximum_fusion.refs_0_), channel_id=1, source_target_pairs={{0,6},{1,7},{2,4},{3,5},{4,2},{5,3},{6,0},{7,1},{8,14},{9,15},{10,... | collective-permute-start | bytes 393224 | tf_op jit(solution)/shard_map/ppermute | solution.py:348
  11.5 0.0 collective-permute-start.1
  11.5 4.0 %collective-permute-start.6 = (bf16[64,1024]{1,0:T(8,128)(2,1)S(1)}, bf16[64,1024]{1,0:T(8,128)(2,1)S(1)}, u32[]{:S(2)}, u32[]{:S(2)}) collective-permute-start(bf16[64,1024]{1,0:T(8,128)(2,1)S(1)} %pad_maximum_fusion.1.refs_4_), channel_id=1, source_target_pairs={{0,16},{1,17},{2,18},{3,19},{4,20},{5,21},{6,22},{7,23},{8,24},{9,... | collective-permute-start | bytes 393224 | tf_op jit(solution)/shard_map/ppermute | solution.py:349
  15.4 0.7 collective-permute-start.5
  16.1 0.0 collective-permute-done.3.refs_3_
  16.1 0.3 collective-permute-start.4
  16.5 0.1 stack.31.p
  16.5 0.0 collective-permute-done.2.refs_2_
  16.5 0.1 collective-permute-done.1.refs_1_
  16.7 1.8 %collective-permute-done.6.refs_7_ = bf16[64,1024]{1,0:T(8,128)(2,1)S(1)} collective-permute-done((bf16[64,1024]{1,0:T(8,128)(2,1)S(1)}, bf16[64,1024]{1,0:T(8,128)(2,1)S(1)}, u32[]{:S(2)}, u32[]{:S(2)}) %collective-permute-start.6) | collective-permute-done | bytes 131104 | tf_op jit(solution)/shard_map/ppermute | solution.py:349
  18.5 3.1 %collective-permute-done.5.refs_6_ = bf16[64,1024]{1,0:T(8,128)(2,1)S(1)} collective-permute-done((bf16[64,1024]{1,0:T(8,128)(2,1)S(1)}, bf16[64,1024]{1,0:T(8,128)(2,1)S(1)}, u32[]{:S(2)}, u32[]{:S(2)}) %collective-permute-start.5) | collective-permute-done | bytes 131104 | tf_op jit(solution)/shard_map/ppermute | solution.py:349
  21.6 0.0 collective-permute-done.4.refs_5_
  21.6 0.6 join.1
  22.2 2.2 %collective-permute-start.8 = (bf16[256,1024]{1,0:T(8,128)(2,1)S(1)}, bf16[256,1024]{1,0:T(8,128)(2,1)S(1)}, u32[]{:S(2)}, u32[]{:S(2)}) collective-permute-start(bf16[256,1024]{1,0:T(8,128)(2,1)S(1)} %get-tuple-element.35.refs_1_.refs_3_), channel_id=1, source_target_pairs={{0,24},{1,25},{2,26},{3,27},{4,28},{5,29},{6,30},{7,31},{8,16},{9,... | collective-permute-start | bytes 1572872 | tf_op jit(solution)/shard_map/ppermute | solution.py:352
  24.4 0.0 collective-permute-start.7
  24.4 3.2 %collective-permute-start.10 = (bf16[256,1024]{1,0:T(8,128)(2,1)S(1)}, bf16[256,1024]{1,0:T(8,128)(2,1)S(1)}, u32[]{:S(2)}, u32[]{:S(2)}) collective-permute-start(bf16[256,1024]{1,0:T(8,128)(2,1)S(1)} %get-tuple-element.36.refs_2_.refs_4_), channel_id=1, source_target_pairs={{0,6},{1,7},{2,4},{3,5},{4,2},{5,3},{6,0},{7,1},{8,14},{9,15},{10,... | collective-permute-start | bytes 1572872 | tf_op jit(solution)/shard_map/ppermute | solution.py:352
  27.6 0.2 collective-permute-start.9
  27.9 1.9 %copy-done = bf16[1568,1024]{1,0:T(8,128)(2,1)S(1)} copy-done((bf16[1568,1024]{1,0:T(8,128)(2,1)S(1)}, bf16[1568,1024]{1,0:T(8,128)(2,1)}, u32[]{:S(2)}) %copy-start) | copy-done | bytes 3211288
  29.8 3.6 %weights.3 = (f32[4,128]{1,0:T(4,128)S(1)}, f32[1568,1]{1,0:T(8,128)S(1)}, f32[784,512]{1,0:T(8,128)S(1)}, f32[784,512]{1,0:T(8,128)S(1)}, f32[2,512]{1,0:T(2,128)S(1)}) custom-call(s32[7]{0:T(128)S(1)} %stack.31.p, bf16[1568,1024]{1,0:T(8,128)(2,1)S(1)} %copy-done, bf16[256,1024]{1,0:T(8,128)(2,1)S(1)} %get-tuple-element.35.refs_1_.refs_3_, ...), custom_call_target="tpu_custom_call" | custom-call | flops 1644167168 | bytes 7483520 | tf_op jit(solution)/shard_map/weights/pallas_call | solution.py:54
  33.3 2.0 %collective-permute-done.8.refs_2_.refs_6_ = bf16[256,1024]{1,0:T(8,128)(2,1)S(1)} collective-permute-done((bf16[256,1024]{1,0:T(8,128)(2,1)S(1)}, bf16[256,1024]{1,0:T(8,128)(2,1)S(1)}, u32[]{:S(2)}, u32[]{:S(2)}) %collective-permute-start.8) | collective-permute-done | bytes 524320 | tf_op jit(solution)/shard_map/ppermute | solution.py:352
  35.4 0.1 collective-permute-start.11
  35.5 0.2 collective-permute-done.7.refs_1_.refs_5_
  35.6 2.5 %collective-permute-start.12 = (bf16[128,1024]{1,0:T(8,128)(2,1)S(1)}, bf16[128,1024]{1,0:T(8,128)(2,1)S(1)}, u32[]{:S(2)}, u32[]{:S(2)}) collective-permute-start(bf16[128,1024]{1,0:T(8,128)(2,1)S(1)} %slice.37), channel_id=1, source_target_pairs={{0,24},{1,25},{2,26},{3,27},{4,28},{5,29},{6,30},{7,31},{8,16},{9,... | collective-permute-start | bytes 786440 | tf_op jit(solution)/shard_map/ppermute | solution.py:356
  38.1 0.0 collective-permute-done.10.refs_4_.refs_8_
  38.1 3.5 %collective-permute-start.13 = (bf16[128,1024]{1,0:T(8,128)(2,1)S(1)}, bf16[128,1024]{1,0:T(8,128)(2,1)S(1)}, u32[]{:S(2)}, u32[]{:S(2)}) collective-permute-start(bf16[128,1024]{1,0:T(8,128)(2,1)S(1)} %slice.38), channel_id=1, source_target_pairs={{0,2},{1,3},{2,0},{3,1},{4,6},{5,7},{6,4},{7,5},{8,10},{9,11},{10,... | collective-permute-start | bytes 786440 | tf_op jit(solution)/shard_map/ppermute | solution.py:357
  41.6 2.4 %collective-permute-start.14 = (bf16[128,1024]{1,0:T(8,128)(2,1)S(1)}, bf16[128,1024]{1,0:T(8,128)(2,1)S(1)}, u32[]{:S(2)}, u32[]{:S(2)}) collective-permute-start(bf16[128,1024]{1,0:T(8,128)(2,1)S(1)} %slice.39), channel_id=1, source_target_pairs={{0,6},{1,7},{2,4},{3,5},{4,2},{5,3},{6,0},{7,1},{8,14},{9,15},{10,... | collective-permute-start | bytes 786440 | tf_op jit(solution)/shard_map/ppermute | solution.py:358
  44.0 5.4 %weights.4 = (f32[8,128]{1,0:T(8,128)S(1)}, f32[784,1024]{1,0:T(8,128)S(1)}, f32[784,1024]{1,0:T(8,128)S(1)}, f32[2,1024]{1,0:T(2,128)S(1)}) custom-call(s32[7]{0:T(128)S(1)} %stack.31.p, bf16[1568,1024]{1,0:T(8,128)(2,1)S(1)} %copy-done.1, bf16[256,1024]{1,0:T(8,128)(2,1)S(1)} %collective-permute-done.7.refs_1_.refs_5_, ...), custom_call_target="tpu_custom_call" | custom-call | flops 3288334336 | bytes 11749504 | tf_op jit(solution)/shard_map/weights/pallas_call | solution.py:54
  49.4 0.0 collective-permute-done.11.refs_1_
  49.4 0.0 collective-permute-done.12.refs_2_
  49.5 0.0 collective-permute-done.14.refs_4_
  49.5 3.2 %weights.5 = (bf16[256,1024]{1,0:T(8,128)(2,1)S(1)}, bf16[256,1024]{1,0:T(8,128)(2,1)S(1)}, f32[32,16,128]{2,1,0:T(8,128)S(1)}, f32[784,512]{1,0:T(8,128)S(1)}, ...) custom-call(s32[7]{0:T(128)S(1)} %stack.31.p, bf16[1568,1024]{1,0:T(8,128)(2,1)S(1)} %copy-done.1, ...), custom_call_target="tpu_custom_call" | custom-call | flops 1644167168 | bytes 8798336 | tf_op jit(solution)/shard_map/weights/pallas_call | solution.py:54
  52.7 14.0 %all_to_all.5.refs_11_ = f32[32,16,128]{2,1,0:T(8,128)S(1)} all-to-all(f32[32,16,128]{2,1,0:T(8,128)S(1)} %get-tuple-element.48), channel_id=1, replica_groups=mesh['dp'=4,'cent'=32] {'cent'}, dimensions={0} | all-to-all | bytes 524288 | tf_op jit(solution)/shard_map/all_to_all | solution.py:367
  66.7 5.7 %sums.2 = (f32[784,384]{1,0:T(8,128)S(1)}, f32[784,256]{1,0:T(8,128)S(1)}, f32[784,256]{1,0:T(8,128)}, f32[784,256]{1,0:T(8,128)S(1)}, f32[16,128]{1,0:T(8,128)S(1)}, /*index=5*/f32[8,2048]{1,0:T(8,128)S(1)}) custom-call(s32[7]{0:T(128)S(1)} %stack.31.p, f32[784,512]{1,0:T(8,128)S(1)} %get-tuple-element.45.refs_0_, ...), custom_call_target="tpu_custom_call" | custom-call | flops 3288334336 | bytes 14581760 | tf_op jit(solution)/shard_map/sums/pallas_call | solution.py:54
  72.4 0.0 collective-permute-start.16
  72.4 5.1 %sums.3 = (f32[784,384]{1,0:T(8,128)S(1)}, f32[784,256]{1,0:T(8,128)S(1)}, f32[784,256]{1,0:T(8,128)}, f32[784,256]{1,0:T(8,128)S(1)}) custom-call(s32[7]{0:T(128)S(1)} %stack.31.p, f32[784,512]{1,0:T(8,128)S(1)} %get-tuple-element.37.refs_0_, f32[784,1024]{1,0:T(8,128)S(1)} %get-tuple-element.39.refs_1_, f32[784,512]{1,0:T(8,128)S(1)} %get-tuple-element.42.refs_2_, ...), custom_call_target="tpu_custom_call" | custom-call | flops 3288334336 | bytes 14295040 | tf_op jit(solution)/shard_map/sums/pallas_call | solution.py:54
  77.5 0.5 collective-permute-start.15
  78.0 0.0 collective-permute-start.18
  78.0 0.5 collective-permute-start.17
  78.5 0.0 collective-permute-done.16.refs_3_
  78.5 1.0 pack.2
  79.6 0.9 convert_element_type.12
  80.5 2.9 %collective-permute-start.20 = (f16[784,256]{1,0:T(8,128)(2,1)}, f16[784,256]{1,0:T(8,128)(2,1)}, u32[]{:S(2)}, u32[]{:S(2)}) collective-permute-start(f16[784,256]{1,0:T(8,128)(2,1)} %convert_element_type.12), channel_id=1, source_target_pairs={{0,64},{32,96},{64,0},{96,32},{1,65},{33,97},{65,1},{97,33},{2,66}... | collective-permute-start | bytes 1204232 | tf_op jit(solution)/shard_map/ppermute | solution.py:376
  83.4 0.0 collective-permute-done.15.refs_2_
  83.4 1.1 pack.3
  84.5 0.8 copy-done.5
  85.3 0.8 convert_element_type.14
  86.1 1.7 %collective-permute-start.21 = (f16[784,256]{1,0:T(8,128)(2,1)}, f16[784,256]{1,0:T(8,128)(2,1)}, u32[]{:S(2)}, u32[]{:S(2)}) collective-permute-start(f16[784,256]{1,0:T(8,128)(2,1)} %convert_element_type.14), channel_id=1, source_target_pairs={{0,64},{32,96},{64,0},{96,32},{1,65},{33,97},{65,1},{97,33},{2,66}... | collective-permute-start | bytes 1204232 | tf_op jit(solution)/shard_map/ppermute | solution.py:376
  87.8 0.1 dynamic-slice_bitcast_fusion.1
  87.9 1.8 %collective-permute-start.19 = (f32[16,784]{1,0:T(8,128)S(1)}, f32[16,784]{1,0:T(8,128)S(1)}, u32[]{:S(2)}, u32[]{:S(2)}) collective-permute-start(f32[16,784]{1,0:T(8,128)S(1)} %get-tuple-element.65), channel_id=1, source_target_pairs={{0,64},{32,96},{64,0},{96,32},{1,65},{33,97},{65,1},{97,33},{2,66}... | collective-permute-start | bytes 150536 | tf_op jit(solution)/shard_map/ppermute | solution.py:377
  89.7 0.6 pad_maximum_fusion.2
  90.3 0.0 collective-permute-done.18.refs_4_
  90.3 0.0 collective-permute-done.17.refs_3_
  90.3 1.9 %copy-done.2 = bf16[1568,1024]{1,0:T(8,128)(2,1)S(1)} copy-done((bf16[1568,1024]{1,0:T(8,128)(2,1)S(1)}, bf16[1568,1024]{1,0:T(8,128)(2,1)}, u32[]{:S(2)}) %copy-start.2) | copy-done | bytes 3211288
  92.2 1.6 %near.1.refs_0_ = f32[1568,256]{1,0:T(8,128)S(1)} custom-call(s32[7]{0:T(128)S(1)} %stack.31.p, f32[784,256]{1,0:T(8,128)S(1)} %get-tuple-element.58.refs_0_, f32[784,256]{1,0:T(8,128)S(1)} %get-tuple-element.59.refs_1_, f32[784,256]{1,0:T(8,128)S(1)} %get-tuple-element.60.refs_2_, f32[784,256]{1,0:T(8,128)} %collective-permute-done.17.refs_3_, ...), custom_call_target="tpu_custom_call" | custom-call | bytes 8028160 | tf_op jit(solution)/shard_map/near/pallas_call | solution.py:54
  93.8 0.7 collective-permute-done.20
  94.5 1.1 convert_element_type.13.refs_4_
  95.5 7.2 %collective-permute-done.21 = f16[784,256]{1,0:T(8,128)(2,1)} collective-permute-done((f16[784,256]{1,0:T(8,128)(2,1)}, f16[784,256]{1,0:T(8,128)(2,1)}, u32[]{:S(2)}, u32[]{:S(2)}) %collective-permute-start.21) | collective-permute-done | bytes 401440 | tf_op jit(solution)/shard_map/ppermute | solution.py:376
  102.7 1.1 convert_element_type.15.refs_5_
  103.8 0.0 collective-permute-done.19.refs_3_
  103.8 2.6 %fresh.1 = bf16[1568,256]{1,0:T(8,128)(2,1)} custom-call(s32[7]{0:T(128)S(1)} %stack.31.p, f32[1568,256]{1,0:T(8,128)S(1)} %near.1.refs_0_, f32[784,128]{1,0:T(8,128)S(1)} %copy-done.4, f32[784,128]{1,0:T(8,128)S(1)} %copy-done.6, f32[16,784]{1,0:T(8,128)S(1)} %collective-permute-done.19.refs_3_, f32[784,256]{1,0:T(8,128)S(1)} %convert_element_type.13.refs_4_, ...), custom_call_target="tpu_custom_call" | custom-call | bytes 4867072 | tf_op jit(solution)/shard_map/fresh/pallas_call | solution.py:54
  (20 shorter events, 0.1 us)
Async XLA Ops:
  0.6 5.4 %collective-permute-start = (bf16[64,1024]{1,0:T(8,128)(2,1)}, bf16[64,1024]{1,0:T(8,128)(2,1)S(1)}, u32[]{:S(2)}, u32[]{:S(2)}) collective-permute-start(bf16[64,1024]{1,0:T(8,128)(2,1)} %param.2), channel_id=1, source_target_pairs={{0,1},{1,0},{2,3},{3,2},{4,5},{5,4},{6,7},{7,6},{8,9},{9,8},{10,11... | collective-permute-start | bytes 393224 | tf_op jit(solution)/shard_map/ppermute | solution.py:340
  7.0 9.1 %collective-permute-start.3 = (bf16[64,1024]{1,0:T(8,128)(2,1)S(1)}, bf16[64,1024]{1,0:T(8,128)(2,1)S(1)}, u32[]{:S(2)}, u32[]{:S(2)}) collective-permute-start(bf16[64,1024]{1,0:T(8,128)(2,1)S(1)} %pad_maximum_fusion.refs_0_), channel_id=1, source_target_pairs={{0,4},{1,5},{2,6},{3,7},{4,0},{5,1},{6,2},{7,3},{8,12},{9,13},{10,... | collective-permute-start | bytes 393224 | tf_op jit(solution)/shard_map/ppermute | solution.py:348
  10.3 6.2 %collective-permute-start.2 = (bf16[64,1024]{1,0:T(8,128)(2,1)S(1)}, bf16[64,1024]{1,0:T(8,128)(2,1)S(1)}, u32[]{:S(2)}, u32[]{:S(2)}) collective-permute-start(bf16[64,1024]{1,0:T(8,128)(2,1)S(1)} %pad_maximum_fusion.refs_0_), channel_id=1, source_target_pairs={{0,6},{1,7},{2,4},{3,5},{4,2},{5,3},{6,0},{7,1},{8,14},{9,15},{10,... | collective-permute-start | bytes 393224 | tf_op jit(solution)/shard_map/ppermute | solution.py:348
  11.5 5.2 %collective-permute-start.1 = (bf16[64,1024]{1,0:T(8,128)(2,1)S(1)}, bf16[64,1024]{1,0:T(8,128)(2,1)S(1)}, u32[]{:S(2)}, u32[]{:S(2)}) collective-permute-start(bf16[64,1024]{1,0:T(8,128)(2,1)S(1)} %pad_maximum_fusion.refs_0_), channel_id=1, source_target_pairs={{0,2},{1,3},{2,0},{3,1},{4,6},{5,7},{6,4},{7,5},{8,10},{9,11},{10,... | collective-permute-start | bytes 393224 | tf_op jit(solution)/shard_map/ppermute | solution.py:348
  11.5 7.0 %collective-permute-start.6 = (bf16[64,1024]{1,0:T(8,128)(2,1)S(1)}, bf16[64,1024]{1,0:T(8,128)(2,1)S(1)}, u32[]{:S(2)}, u32[]{:S(2)}) collective-permute-start(bf16[64,1024]{1,0:T(8,128)(2,1)S(1)} %pad_maximum_fusion.1.refs_4_), channel_id=1, source_target_pairs={{0,16},{1,17},{2,18},{3,19},{4,20},{5,21},{6,22},{7,23},{8,24},{9,... | collective-permute-start | bytes 393224 | tf_op jit(solution)/shard_map/ppermute | solution.py:349
  15.4 6.2 %collective-permute-start.5 = (bf16[64,1024]{1,0:T(8,128)(2,1)S(1)}, bf16[64,1024]{1,0:T(8,128)(2,1)S(1)}, u32[]{:S(2)}, u32[]{:S(2)}) collective-permute-start(bf16[64,1024]{1,0:T(8,128)(2,1)S(1)} %pad_maximum_fusion.1.refs_4_), channel_id=1, source_target_pairs={{0,24},{1,25},{2,26},{3,27},{4,28},{5,29},{6,30},{7,31},{8,16},{9,... | collective-permute-start | bytes 393224 | tf_op jit(solution)/shard_map/ppermute | solution.py:349
  16.1 5.5 %collective-permute-start.4 = (bf16[64,1024]{1,0:T(8,128)(2,1)S(1)}, bf16[64,1024]{1,0:T(8,128)(2,1)S(1)}, u32[]{:S(2)}, u32[]{:S(2)}) collective-permute-start(bf16[64,1024]{1,0:T(8,128)(2,1)S(1)} %pad_maximum_fusion.1.refs_4_), channel_id=1, source_target_pairs={{0,8},{1,9},{2,10},{3,11},{4,12},{5,13},{6,14},{7,15},{8,0},{9,1},... | collective-permute-start | bytes 393224 | tf_op jit(solution)/shard_map/ppermute | solution.py:349
  22.2 13.1 %collective-permute-start.8 = (bf16[256,1024]{1,0:T(8,128)(2,1)S(1)}, bf16[256,1024]{1,0:T(8,128)(2,1)S(1)}, u32[]{:S(2)}, u32[]{:S(2)}) collective-permute-start(bf16[256,1024]{1,0:T(8,128)(2,1)S(1)} %get-tuple-element.35.refs_1_.refs_3_), channel_id=1, source_target_pairs={{0,24},{1,25},{2,26},{3,27},{4,28},{5,29},{6,30},{7,31},{8,16},{9,... | collective-permute-start | bytes 1572872 | tf_op jit(solution)/shard_map/ppermute | solution.py:352
  24.4 11.2 %collective-permute-start.7 = (bf16[256,1024]{1,0:T(8,128)(2,1)S(1)}, bf16[256,1024]{1,0:T(8,128)(2,1)S(1)}, u32[]{:S(2)}, u32[]{:S(2)}) collective-permute-start(bf16[256,1024]{1,0:T(8,128)(2,1)S(1)} %get-tuple-element.35.refs_1_.refs_3_), channel_id=1, source_target_pairs={{0,8},{1,9},{2,10},{3,11},{4,12},{5,13},{6,14},{7,15},{8,0},{9,1},... | collective-permute-start | bytes 1572872 | tf_op jit(solution)/shard_map/ppermute | solution.py:351
  24.4 13.7 %collective-permute-start.10 = (bf16[256,1024]{1,0:T(8,128)(2,1)S(1)}, bf16[256,1024]{1,0:T(8,128)(2,1)S(1)}, u32[]{:S(2)}, u32[]{:S(2)}) collective-permute-start(bf16[256,1024]{1,0:T(8,128)(2,1)S(1)} %get-tuple-element.36.refs_2_.refs_4_), channel_id=1, source_target_pairs={{0,6},{1,7},{2,4},{3,5},{4,2},{5,3},{6,0},{7,1},{8,14},{9,15},{10,... | collective-permute-start | bytes 1572872 | tf_op jit(solution)/shard_map/ppermute | solution.py:352
  27.6 14.0 %collective-permute-start.9 = (bf16[256,1024]{1,0:T(8,128)(2,1)S(1)}, bf16[256,1024]{1,0:T(8,128)(2,1)S(1)}, u32[]{:S(2)}, u32[]{:S(2)}) collective-permute-start(bf16[256,1024]{1,0:T(8,128)(2,1)S(1)} %get-tuple-element.36.refs_2_.refs_4_), channel_id=1, source_target_pairs={{0,2},{1,3},{2,0},{3,1},{4,6},{5,7},{6,4},{7,5},{8,10},{9,11},{10,... | collective-permute-start | bytes 1572872 | tf_op jit(solution)/shard_map/ppermute | solution.py:351
  27.9 1.9 %copy-start = (bf16[1568,1024]{1,0:T(8,128)(2,1)S(1)}, bf16[1568,1024]{1,0:T(8,128)(2,1)}, u32[]{:S(2)}) copy-start(bf16[1568,1024]{1,0:T(8,128)(2,1)} %refs_5_.1) | copy-start | bytes 9633796
  29.8 14.2 %copy-start.1 = (bf16[1568,1024]{1,0:T(8,128)(2,1)S(1)}, bf16[1568,1024]{1,0:T(8,128)(2,1)}, u32[]{:S(2)}) copy-start(bf16[1568,1024]{1,0:T(8,128)(2,1)} %refs_5_.1) | copy-start | bytes 9633796
  35.4 14.1 %collective-permute-start.11 = (bf16[128,1024]{1,0:T(8,128)(2,1)S(1)}, bf16[128,1024]{1,0:T(8,128)(2,1)S(1)}, u32[]{:S(2)}, u32[]{:S(2)}) collective-permute-start(bf16[128,1024]{1,0:T(8,128)(2,1)S(1)} %slice.36), channel_id=1, source_target_pairs={{0,8},{1,9},{2,10},{3,11},{4,12},{5,13},{6,14},{7,15},{8,0},{9,1},... | collective-permute-start | bytes 786440 | tf_op jit(solution)/shard_map/ppermute | solution.py:355
  35.6 13.8 %collective-permute-start.12 = (bf16[128,1024]{1,0:T(8,128)(2,1)S(1)}, bf16[128,1024]{1,0:T(8,128)(2,1)S(1)}, u32[]{:S(2)}, u32[]{:S(2)}) collective-permute-start(bf16[128,1024]{1,0:T(8,128)(2,1)S(1)} %slice.37), channel_id=1, source_target_pairs={{0,24},{1,25},{2,26},{3,27},{4,28},{5,29},{6,30},{7,31},{8,16},{9,... | collective-permute-start | bytes 786440 | tf_op jit(solution)/shard_map/ppermute | solution.py:356
  38.1 11.3 %collective-permute-start.13 = (bf16[128,1024]{1,0:T(8,128)(2,1)S(1)}, bf16[128,1024]{1,0:T(8,128)(2,1)S(1)}, u32[]{:S(2)}, u32[]{:S(2)}) collective-permute-start(bf16[128,1024]{1,0:T(8,128)(2,1)S(1)} %slice.38), channel_id=1, source_target_pairs={{0,2},{1,3},{2,0},{3,1},{4,6},{5,7},{6,4},{7,5},{8,10},{9,11},{10,... | collective-permute-start | bytes 786440 | tf_op jit(solution)/shard_map/ppermute | solution.py:357
  41.6 7.8 %collective-permute-start.14 = (bf16[128,1024]{1,0:T(8,128)(2,1)S(1)}, bf16[128,1024]{1,0:T(8,128)(2,1)S(1)}, u32[]{:S(2)}, u32[]{:S(2)}) collective-permute-start(bf16[128,1024]{1,0:T(8,128)(2,1)S(1)} %slice.39), channel_id=1, source_target_pairs={{0,6},{1,7},{2,4},{3,5},{4,2},{5,3},{6,0},{7,1},{8,14},{9,15},{10,... | collective-permute-start | bytes 786440 | tf_op jit(solution)/shard_map/ppermute | solution.py:358
  72.4 6.1 %collective-permute-start.16 = (f32[784,384]{1,0:T(8,128)S(1)}, f32[784,384]{1,0:T(8,128)S(1)}, u32[]{:S(2)}, u32[]{:S(2)}) collective-permute-start(f32[784,384]{1,0:T(8,128)S(1)} %get-tuple-element.55.refs_1_), channel_id=1, source_target_pairs={{0,32},{32,0},{64,96},{96,64},{1,33},{33,1},{65,97},{97,65},{2,34}... | collective-permute-start | bytes 3612680 | tf_op jit(solution)/shard_map/ppermute | solution.py:372
  77.5 5.9 %collective-permute-start.15 = (f32[784,384]{1,0:T(8,128)S(1)}, f32[784,384]{1,0:T(8,128)S(1)}, u32[]{:S(2)}, u32[]{:S(2)}) collective-permute-start(f32[784,384]{1,0:T(8,128)S(1)} %get-tuple-element.53.refs_0_), channel_id=1, source_target_pairs={{0,32},{32,0},{64,96},{96,64},{1,33},{33,1},{65,97},{97,65},{2,34}... | collective-permute-start | bytes 3612680 | tf_op jit(solution)/shard_map/ppermute | solution.py:373
  78.0 12.3 %collective-permute-start.18 = (f32[784,256]{1,0:T(8,128)}, f32[784,256]{1,0:T(8,128)S(1)}, u32[]{:S(2)}, u32[]{:S(2)}) collective-permute-start(f32[784,256]{1,0:T(8,128)} %get-tuple-element.62), channel_id=1, source_target_pairs={{0,32},{32,0},{64,96},{96,64},{1,33},{33,1},{65,97},{97,65},{2,34}... | collective-permute-start | bytes 2408456 | tf_op jit(solution)/shard_map/ppermute | solution.py:379
  78.0 12.3 %collective-permute-start.17 = (f32[784,256]{1,0:T(8,128)}, f32[784,256]{1,0:T(8,128)}, u32[]{:S(2)}, u32[]{:S(2)}) collective-permute-start(f32[784,256]{1,0:T(8,128)} %get-tuple-element.61), channel_id=1, source_target_pairs={{0,32},{32,0},{64,96},{96,64},{1,33},{33,1},{65,97},{97,65},{2,34}... | collective-permute-start | bytes 2408456 | tf_op jit(solution)/shard_map/ppermute | solution.py:379
  79.6 4.9 %copy-start.3 = (f32[784,128]{1,0:T(8,128)}, f32[784,128]{1,0:T(8,128)S(1)}, u32[]{:S(2)}) copy-start(f32[784,128]{1,0:T(8,128)S(1)} %get-tuple-element.63.refs_1_) | copy-start | bytes 1204228
  80.5 14.0 %collective-permute-start.20 = (f16[784,256]{1,0:T(8,128)(2,1)}, f16[784,256]{1,0:T(8,128)(2,1)}, u32[]{:S(2)}, u32[]{:S(2)}) collective-permute-start(f16[784,256]{1,0:T(8,128)(2,1)} %convert_element_type.12), channel_id=1, source_target_pairs={{0,64},{32,96},{64,0},{96,32},{1,65},{33,97},{65,1},{97,33},{2,66}... | collective-permute-start | bytes 1204232 | tf_op jit(solution)/shard_map/ppermute | solution.py:376
  84.5 0.8 copy-start.5
  86.1 16.7 %collective-permute-start.21 = (f16[784,256]{1,0:T(8,128)(2,1)}, f16[784,256]{1,0:T(8,128)(2,1)}, u32[]{:S(2)}, u32[]{:S(2)}) collective-permute-start(f16[784,256]{1,0:T(8,128)(2,1)} %convert_element_type.14), channel_id=1, source_target_pairs={{0,64},{32,96},{64,0},{96,32},{1,65},{33,97},{65,1},{97,33},{2,66}... | collective-permute-start | bytes 1204232 | tf_op jit(solution)/shard_map/ppermute | solution.py:376
  87.9 15.9 %collective-permute-start.19 = (f32[16,784]{1,0:T(8,128)S(1)}, f32[16,784]{1,0:T(8,128)S(1)}, u32[]{:S(2)}, u32[]{:S(2)}) collective-permute-start(f32[16,784]{1,0:T(8,128)S(1)} %get-tuple-element.65), channel_id=1, source_target_pairs={{0,64},{32,96},{64,0},{96,32},{1,65},{33,97},{65,1},{97,33},{2,66}... | collective-permute-start | bytes 150536 | tf_op jit(solution)/shard_map/ppermute | solution.py:377
  90.3 1.9 %copy-start.2 = (bf16[1568,1024]{1,0:T(8,128)(2,1)S(1)}, bf16[1568,1024]{1,0:T(8,128)(2,1)}, u32[]{:S(2)}) copy-start(bf16[1568,1024]{1,0:T(8,128)(2,1)} %refs_5_.1) | copy-start | bytes 9633796
  93.8 10.1 %copy-start.4 = (f32[784,128]{1,0:T(8,128)S(1)}, f32[784,128]{1,0:T(8,128)}, u32[]{:S(2)}) copy-start(f32[784,128]{1,0:T(8,128)} %copy-done.3) | copy-start | bytes 1204228
  93.8 10.1 %copy-start.6 = (f32[784,128]{1,0:T(8,128)S(1)}, f32[784,128]{1,0:T(8,128)}, u32[]{:S(2)}) copy-start(f32[784,128]{1,0:T(8,128)} %copy-done.5) | copy-start | bytes 1204228
